TPU v7x, 128 devices: a whole 4x4x4 slice. The times are simulated.
128 devices in a mesh: lat: 8 (over z, x_lo), lon: 16 (over x_hi, y, core).
Axes of the slice: x: 4 (x_hi: 2, x_lo: 2; x = x_hi * 2 + x_lo), y: 4, z: 4, core: 2. Of those that a mesh axis runs over, the one named last changes fastest.
Arguments:
- tracer_cot: float32 [50, 512, 2048], P(None, 'lat', 'lon'), may hold values from -6 to 6
- east_cot: float32 [50, 512, 2048], P(None, 'lat', 'lon'), may hold values from -3 to 3
- north_cot: float32 [50, 512, 2048], P(None, 'lat', 'lon'), may hold values from -3 to 3
- surface_cot: float32 [512, 2048], P('lat', 'lon'), may hold values from -60 to 60
- depth_levels: int32 [512, 2048], P('lat', 'lon'), may hold values from 0 to 50
- diffusivity: float32 [512, 2048], P('lat', 'lon'), may hold values from 0.03 to 0.2
- coriolis: float32 [512, 2048], P('lat', 'lon'), may hold values from -1 to 1
- storage: float32 [512, 2048], P('lat', 'lon'), may hold values from 0.5 to 5
- thickness: float32 [50], replicated, may hold values from 0.1 to 0.5
Outputs:
- tracer_adj: float32 [50, 512, 2048], P(None, 'lat', 'lon')
- east_adj: float32 [50, 512, 2048], P(None, 'lat', 'lon')
- north_adj: float32 [50, 512, 2048], P(None, 'lat', 'lon')
- surface_adj: float32 [512, 2048], P('lat', 'lon')
All inputs are finite; a program needn't handle non-finite values.
Results may differ from a plain program's by a relative error of at most 0.0003.
Values sent between devices are 32-bit elements; how exact they have to be, the bound alone decides.
No kernel may reach another device: no remote copies, remote signals or barrier semaphores. Data moves between devices by JAX's collectives and lax.ppermute only.
A program may use at most 128 MiB of HBM per device.

v0:
```python
import jax
import jax.numpy as jnp
from jax import lax
from jax.sharding import PartitionSpec as P

ITERS = 4


def extended(block, sides, width, periodic):
    for axis, dim in sides:
        count = lax.axis_size(axis)
        forward = [(i, i + 1) for i in range(count - 1)]
        if periodic:
            forward.append((count - 1, 0))
        backward = [(target, source) for source, target in forward]
        low = lax.ppermute(
            lax.slice_in_dim(block, block.shape[dim] - width, None, axis=dim), axis, forward
        )
        high = lax.ppermute(lax.slice_in_dim(block, 0, width, axis=dim), axis, backward)
        block = jnp.concatenate([low, block, high], axis=dim)
    return block


def from_partner(array, axis, stride):
    return lax.ppermute(array, axis, [(i, i ^ 1 << stride) for i in range(lax.axis_size(axis))])


def neighbours(values):
    lon_wide = extended(values, (("lon", 2),), 1, True)
    lat_wide = extended(values, (("lat", 1),), 1, False)
    partner = values[:, -1:, :]
    for bit_index in range(lax.axis_size("lon").bit_length() - 1):
        partner = from_partner(partner, "lon", bit_index)
    mirror = partner[:, :, ::-1]
    at_top = lax.axis_index("lat") == lax.axis_size("lat") - 1
    north_edge = jnp.where(at_top, mirror, lat_wide[:, -1:, :])
    north_side = jnp.concatenate([lat_wide[:, 2:-1, :], north_edge], axis=1)
    return (lon_wide[:, :, 2:], lon_wide[:, :, :-2], north_side, lat_wide[:, :-2, :])


def diffuse(values, sides, wet_mask, coeffs):
    east_side, west_side, north_side, south_side = sides
    face_east, face_west, face_north, face_south = coeffs
    flows = face_east * (values - east_side) + face_west * (values - west_side)
    flows = flows + face_north * (values - north_side) + face_south * (values - south_side)
    return wet_mask * values - flows


def local(
    tracer_cot,
    east_cot,
    north_cot,
    surface_cot,
    depth_levels,
    diffusivity,
    coriolis,
    storage,
    thickness,
):
    levels_count, rows, columns = tracer_cot.shape
    depth_float = depth_levels.astype(jnp.float32)
    nearby = neighbours(jnp.stack([diffusivity, depth_float]))
    at_top = lax.axis_index("lat") == lax.axis_size("lat") - 1
    row_index = lax.broadcasted_iota(jnp.int32, (rows, columns), 0)
    top_rows = jnp.where(at_top & (row_index == rows - 1), 1.0, 0.0).astype(jnp.float32)
    level_values = lax.broadcasted_iota(jnp.float32, (levels_count, 1, 1), 0)
    wet_mask = (level_values < depth_float).astype(jnp.float32)
    wet_east, wet_west, wet_north, wet_south = [
        (level_values < item[1]).astype(jnp.float32) for item in nearby
    ]
    face_east = diffusivity * wet_mask * wet_east
    face_west = nearby[1][0] * wet_west * wet_mask
    face_north = (diffusivity + top_rows * nearby[2][0]) * wet_mask * wet_north
    face_south = nearby[3][0] * wet_south * wet_mask
    coeffs = (face_east, face_west, face_north, face_south)
    layer_weight = thickness[:, None, None]
    east_depth = jnp.sum(layer_weight * wet_mask * wet_east, axis=0)
    east_depth_w = jnp.sum(layer_weight * wet_west * wet_mask, axis=0)
    north_depth = jnp.sum(layer_weight * wet_mask * wet_north, axis=0) * (1.0 + top_rows)
    north_depth_s = jnp.sum(layer_weight * wet_south * wet_mask, axis=0)
    east_sum = jnp.sum(wet_mask * wet_east * east_cot, axis=0)
    north_sum = jnp.sum(wet_mask * wet_north * north_cot, axis=0)
    flux_sides = neighbours(jnp.stack([east_sum, north_sum]))
    source_plane = (
        surface_cot
        + east_sum
        - flux_sides[1][0]
        + north_sum
        - flux_sides[3][1]
        - top_rows * flux_sides[2][1]
    )
    tracer_adj = diffuse(tracer_cot, neighbours(tracer_cot), wet_mask, coeffs)
    inverse = 1.0 / (storage + east_depth + east_depth_w + north_depth + north_depth_s)

    def operate(values):
        east_side, west_side, north_side, south_side = [
            item[0] for item in neighbours(values[None])
        ]
        total = (
            storage * values
            + east_depth * (values - east_side)
            + east_depth_w * (values - west_side)
        )
        return total + north_depth * (values - north_side) + north_depth_s * (values - south_side)

    solution = jnp.zeros_like(source_plane)
    residual = source_plane
    precond = residual * inverse

    def weighted_norm(current, scaled):
        return lax.psum(jnp.sum(current * scaled), ("lat", "lon"))

    direction = precond
    scaled_norm = weighted_norm(residual, precond)
    for iteration in range(ITERS):
        applied = operate(direction)
        alpha_step = scaled_norm / lax.psum(jnp.sum(direction * applied), ("lat", "lon"))
        solution = solution + alpha_step * direction
        if iteration + 1 < ITERS:
            residual = residual - alpha_step * applied
            precond = residual * inverse
            next_norm = weighted_norm(residual, precond)
            direction = precond + next_norm / scaled_norm * direction
            scaled_norm = next_norm
    surface_adj = storage * solution
    solution_sides = neighbours(solution[None])
    east_flux = solution_sides[0][0] - solution
    north_flux = solution_sides[2][0] - solution
    east_total = east_cot + layer_weight * east_flux
    north_total = north_cot + layer_weight * north_flux
    both_totals = jnp.concatenate([east_total, north_total])
    total_sides = [item.reshape(2, levels_count, rows, columns) for item in neighbours(both_totals)]
    both_smooth = diffuse(
        both_totals.reshape(2, levels_count, rows, columns), total_sides, wet_mask, coeffs
    )
    east_smooth, north_smooth = (both_smooth[0], both_smooth[1])
    east_adj = east_smooth - coriolis * wet_mask * north_total
    north_adj = north_smooth + coriolis * wet_mask * east_total
    return (tracer_adj, east_adj, north_adj, surface_adj)


def solution(mesh):
    placed = (
        P(None, "lat", "lon"),
        P(None, "lat", "lon"),
        P(None, "lat", "lon"),
        P("lat", "lon"),
        P("lat", "lon"),
        P("lat", "lon"),
        P("lat", "lon"),
        P("lat", "lon"),
        P(),
    )
    return jax.shard_map(
        local,
        mesh=mesh,
        in_specs=placed,
        out_specs=(
            P(None, "lat", "lon"),
            P(None, "lat", "lon"),
            P(None, "lat", "lon"),
            P("lat", "lon"),
        ),
        check_vma=False,
    )
```

profile of v0, /device:TPU:1, one launch (start us, length us, event | category | flops | bytes accessed | tf_op | source)
XLA Modules:
  0.0 725.0 jit_solution(5190054298687897584)
XLA Ops:
  3.5 3.2 collective-permute-start.14
  11.0 3.0 collective-permute-start.6
  15.0 2.5 collective-permute-start.7
  17.5 1.5 maximum_bitcast_fusion
  19.2 3.2 fusion.4
  22.4 7.6 %collective-permute-start.18 = (f32[2,1,128]{2,1,0:T(1,128)S(1)}, f32[2,1,128]{2,1,0:T(1,128)S(1)}, u32[]{:S(2)}, u32[]{:S(2)}) collective-permute-start(f32[2,1,128]{2,1,0:T(1,128)S(1)} %get-tuple-element.60), channel_id=1, source_target_pairs={{0,1},{1,0},{2,3},{3,2},{4,5},{5,4},{6,7},{7,6},{8,9},{9,8},{10,11... | collective-permute-start | bytes 3080 | tf_op jit(solution)/shard_map/ppermute | solution.py:25
  30.8 2.4 collective-permute-done.19
  33.2 4.3 collective-permute-start.17
  38.8 2.7 collective-permute-start.21
  41.6 1.7 collective-permute-start.16
  44.7 6.4 collective-permute-start.25
  52.0 2.4 collective-permute-done.26
  54.4 4.6 collective-permute-start.30
  60.3 1.5 collective-permute-start.28
  61.9 1.9 collective-permute-start.24
  65.0 2.2 collective-permute-done.23
  68.0 74.4 %all-reduce = (f32[]{:T(128)}, f32[]{:T(128)}) all-reduce(f32[]{:T(128)} %get-tuple-element.17, f32[]{:T(128)} %get-tuple-element.16), channel_id=1, replica_groups=mesh['lat'=8,'lon'=16] {'lat','lon'}, use_global_device_ids=true, to_apply=%region_7.8 | all-reduce | flops 2 | bytes 16 | tf_op jit(solution)/shard_map/psum | solution.py:111
  144.3 64.2 %psum.58 = f32[]{:T(128)} all-reduce(f32[]{:T(128)} %get-tuple-element.29), channel_id=1, replica_groups=mesh['lat'=8,'lon'=16] {'lat','lon'}, use_global_device_ids=true, to_apply=%region_11.12 | all-reduce | flops 1 | bytes 8 | tf_op jit(solution)/shard_map/psum | solution.py:111
  211.9 2.4 collective-permute-done.34
  215.3 2.1 collective-permute-start.38
  218.7 2.0 collective-permute-start.36
  220.8 3.1 collective-permute-start.32
  224.9 2.8 collective-permute-done.31
  228.4 69.1 %psum.59 = f32[]{:T(128)} all-reduce(f32[]{:T(128)} %get-tuple-element.27), channel_id=1, replica_groups=mesh['lat'=8,'lon'=16] {'lat','lon'}, use_global_device_ids=true, to_apply=%region_13.14 | all-reduce | flops 1 | bytes 8 | tf_op jit(solution)/shard_map/psum | solution.py:117
  299.5 64.1 %psum.60 = f32[]{:T(128)} all-reduce(f32[]{:T(128)} %get-tuple-element.24), channel_id=1, replica_groups=mesh['lat'=8,'lon'=16] {'lat','lon'}, use_global_device_ids=true, to_apply=%region_15.16 | all-reduce | flops 1 | bytes 8 | tf_op jit(solution)/shard_map/psum | solution.py:111
  367.0 2.4 collective-permute-done.42
  370.4 2.1 collective-permute-start.46
  373.8 2.0 collective-permute-start.44
  375.9 3.1 collective-permute-start.40
  380.0 2.6 collective-permute-done.39
  383.3 69.1 %psum.61 = f32[]{:T(128)} all-reduce(f32[]{:T(128)} %get-tuple-element.22), channel_id=1, replica_groups=mesh['lat'=8,'lon'=16] {'lat','lon'}, use_global_device_ids=true, to_apply=%region_17.18 | all-reduce | flops 1 | bytes 8 | tf_op jit(solution)/shard_map/psum | solution.py:117
  454.4 64.1 %psum.62 = f32[]{:T(128)} all-reduce(f32[]{:T(128)} %multiply_reduce_fusion.2), channel_id=1, replica_groups=mesh['lat'=8,'lon'=16] {'lat','lon'}, use_global_device_ids=true, to_apply=%region_19.20 | all-reduce | flops 1 | bytes 8 | tf_op jit(solution)/shard_map/psum | solution.py:111
  522.0 2.4 collective-permute-done.50
  525.3 2.1 collective-permute-start.54
  528.7 2.0 collective-permute-start.52
  530.8 3.1 collective-permute-start.48
  535.0 2.6 collective-permute-done.47
  538.3 69.1 %psum.63 = f32[]{:T(128)} all-reduce(f32[]{:T(128)} %fusion.35), channel_id=1, replica_groups=mesh['lat'=8,'lon'=16] {'lat','lon'}, use_global_device_ids=true, to_apply=%region_21.22 | all-reduce | flops 1 | bytes 8 | tf_op jit(solution)/shard_map/psum | solution.py:117
  612.0 1.8 fusion.117
  613.8 2.6 copy.65
  618.7 2.2 collective-permute-start.58
  626.6 2.5 copy.59
  629.1 1.8 copy.57
  630.9 4.4 collective-permute-start.55
  636.2 2.3 multiply_add_fusion.1
  638.5 3.5 fusion
  642.0 2.6 collective-permute-start.10
  645.4 3.7 collective-permute-start.68
  649.1 3.8 copy.60
  653.4 3.8 copy.62
  658.5 3.1 collective-permute-start.11
  661.5 2.2 fusion.2
  663.7 3.9 collective-permute-start.15
  667.6 4.5 copy.61
  673.3 3.8 copy.63
  679.1 3.6 collective-permute-start.64
  684.1 8.9 %pad_maximum_fusion.5 = (f32[100,64,128]{2,1,0:T(8,128)}, f32[100,64,128]{2,1,0:T(8,128)}, f32[100,64,128]{2,1,0:T(8,128)}, f32[100,64,128]{2,1,0:T(8,128)}) fusion(f32[100,64,1]{2,1,0:T(8,128)} %copy.61, f32[50,64,128]{2,1,0:T(8,128)S(1)} %get-tuple-element.91, f32[50,64,128]{2,1,0:T(8,128)S(1)} %get-tuple-element.90, f32[100,1,128]{2,1,0:T(1,128)} %copy-done.9, ...), kind=kLoop, calls=%fused_computation.18 | loop fusion | flops 5734400 | bytes 16486400 | tf_op jit(solution)/shard_map/concatenate | solution.py:20
  693.0 1.5 rev.28
  695.9 3.3 collective-permute-done.65
  699.2 1.8 collective-permute-start.66
  701.0 8.5 %select_select_fusion.5 = (f32[50,64,128]{2,1,0:T(8,128)}, f32[50,64,128]{2,1,0:T(8,128)}, f32[50,64,128]{2,1,0:T(8,128)}, f32[50,64,128]{2,1,0:T(8,128)}, f32[50,64,128]{2,1,0:T(8,128)}) fusion(f32[64,128]{1,0:T(8,128)S(1)} %copy-done.3, f32[64,128]{1,0:T(8,128)S(1)} %copy-done.6, f32[64,128]{1,0:T(8,128)S(1)} %get-tuple-element.89, ...), kind=kLoop, calls=%fused_computation.59 | loop fusion | flops 12288000 | bytes 11814912 | tf_op jit(solution)/shard_map/mul | solution.py:71
  711.4 2.5 pad_maximum_fusion.7
  715.3 6.8 add_subtract_fusion
  722.1 2.5 fusion.6
  (186 shorter events, 60.5 us)
Async XLA Ops:
  2.1 4.6 collective-permute-start.4
  3.5 14.0 %collective-permute-start.14 = (f32[2,1,128]{2,1,0:T(1,128)S(1)}, f32[2,1,128]{2,1,0:T(1,128)S(1)}, u32[]{:S(2)}, u32[]{:S(2)}) collective-permute-start(f32[2,1,128]{2,1,0:T(1,128)S(1)} %get-tuple-element.65), channel_id=1, source_target_pairs={{0,16},{16,32},{32,48},{48,64},{64,80},{80,96},{96,112},{1,17},{17... | collective-permute-start | bytes 3080 | tf_op jit(solution)/shard_map/ppermute | solution.py:16
  6.7 4.3 collective-permute-start.5
  9.0 8.5 %collective-permute-start.2 = (f32[2,64,1]{2,1,0:T(8,128)S(1)}, f32[2,64,1]{2,1,0:T(8,128)S(1)}, u32[]{:S(2)}, u32[]{:S(2)}) collective-permute-start(f32[2,64,1]{2,1,0:T(8,128)S(1)} %get-tuple-element.66), channel_id=1, source_target_pairs={{0,1},{1,2},{2,3},{3,4},{4,5},{5,6},{6,7},{7,8},{8,9},{9,10},{10,1... | collective-permute-start | bytes 1544 | tf_op jit(solution)/shard_map/ppermute | solution.py:16
  9.7 7.8 %collective-permute-start = (f32[2,64,1]{2,1,0:T(8,128)S(1)}, f32[2,64,1]{2,1,0:T(8,128)S(1)}, u32[]{:S(2)}, u32[]{:S(2)}) collective-permute-start(f32[2,64,1]{2,1,0:T(8,128)S(1)} %get-tuple-element.67), channel_id=1, source_target_pairs={{1,0},{2,1},{3,2},{4,3},{5,4},{6,5},{7,6},{8,7},{9,8},{10,9},{11,1... | collective-permute-start | bytes 1544 | tf_op jit(solution)/shard_map/ppermute | solution.py:19
  9.7 9.4 %collective-permute-start.8 = (f32[2,1,128]{2,1,0:T(1,128)S(1)}, f32[2,1,128]{2,1,0:T(1,128)S(1)}, u32[]{:S(2)}, u32[]{:S(2)}) collective-permute-start(f32[2,1,128]{2,1,0:T(1,128)S(1)} %get-tuple-element.64), channel_id=1, source_target_pairs={{16,0},{32,16},{48,32},{64,48},{80,64},{96,80},{112,96},{17,1},{33... | collective-permute-start | bytes 3080 | tf_op jit(solution)/shard_map/ppermute | solution.py:19
  11.0 4.0 collective-permute-start.6
  15.0 4.0 collective-permute-start.7
  22.4 8.4 %collective-permute-start.18 = (f32[2,1,128]{2,1,0:T(1,128)S(1)}, f32[2,1,128]{2,1,0:T(1,128)S(1)}, u32[]{:S(2)}, u32[]{:S(2)}) collective-permute-start(f32[2,1,128]{2,1,0:T(1,128)S(1)} %get-tuple-element.60), channel_id=1, source_target_pairs={{0,1},{1,0},{2,3},{3,2},{4,5},{5,4},{6,7},{7,6},{8,9},{9,8},{10,11... | collective-permute-start | bytes 3080 | tf_op jit(solution)/shard_map/ppermute | solution.py:25
  30.8 2.4 collective-permute-start.19
  33.2 5.6 collective-permute-start.20
  33.2 11.4 %collective-permute-start.17 = (f32[2,1,128]{2,1,0:T(1,128)S(1)}, f32[2,1,128]{2,1,0:T(1,128)S(1)}, u32[]{:S(2)}, u32[]{:S(2)}) collective-permute-start(f32[2,1,128]{2,1,0:T(1,128)S(1)} %get-tuple-element.60), channel_id=1, source_target_pairs={{0,16},{16,32},{32,48},{48,64},{64,80},{80,96},{96,112},{1,17},{17... | collective-permute-start | bytes 3080 | tf_op jit(solution)/shard_map/ppermute | solution.py:16
  37.5 5.9 collective-permute-start.22
  38.8 4.5 collective-permute-start.21
  41.6 3.0 collective-permute-start.16
  44.7 7.3 %collective-permute-start.25 = (f32[1,1,128]{2,1,0:T(1,128)S(1)}, f32[1,1,128]{2,1,0:T(1,128)S(1)}, u32[]{:S(2)}, u32[]{:S(2)}) collective-permute-start(f32[1,1,128]{2,1,0:T(1,128)S(1)} %get-tuple-element.87), channel_id=1, source_target_pairs={{0,1},{1,0},{2,3},{3,2},{4,5},{5,4},{6,7},{7,6},{8,9},{9,8},{10,11... | collective-permute-start | bytes 1544 | tf_op jit(solution)/shard_map/ppermute | solution.py:25
  52.0 2.4 collective-permute-start.26
  54.4 5.9 collective-permute-start.27
  54.4 12.8 %collective-permute-start.30 = (f32[1,1,128]{2,1,0:T(1,128)S(1)}, f32[1,1,128]{2,1,0:T(1,128)S(1)}, u32[]{:S(2)}, u32[]{:S(2)}) collective-permute-start(f32[1,1,128]{2,1,0:T(1,128)S(1)} %get-tuple-element.87), channel_id=1, source_target_pairs={{0,16},{16,32},{32,48},{48,64},{64,80},{80,96},{96,112},{1,17},{17... | collective-permute-start | bytes 1544 | tf_op jit(solution)/shard_map/ppermute | solution.py:16
  59.0 6.1 collective-permute-start.29
  60.3 4.0 collective-permute-start.28
  61.9 3.2 collective-permute-start.24
  63.8 3.5 collective-permute-start.23
  214.3 4.4 collective-permute-start.35
  215.3 12.3 %collective-permute-start.38 = (f32[1,1,128]{2,1,0:T(1,128)S(1)}, f32[1,1,128]{2,1,0:T(1,128)S(1)}, u32[]{:S(2)}, u32[]{:S(2)}) collective-permute-start(f32[1,1,128]{2,1,0:T(1,128)S(1)} %get-tuple-element.83), channel_id=1, source_target_pairs={{0,16},{16,32},{32,48},{48,64},{64,80},{80,96},{96,112},{1,17},{17... | collective-permute-start | bytes 1544 | tf_op jit(solution)/shard_map/ppermute | solution.py:16
  217.4 6.8 collective-permute-start.37
  218.7 5.3 collective-permute-start.36
  220.8 4.1 collective-permute-start.32
  223.9 3.8 collective-permute-start.31
  367.0 2.4 collective-permute-start.42
  369.4 4.4 collective-permute-start.43
  370.4 12.2 %collective-permute-start.46 = (f32[1,1,128]{2,1,0:T(1,128)S(1)}, f32[1,1,128]{2,1,0:T(1,128)S(1)}, u32[]{:S(2)}, u32[]{:S(2)}) collective-permute-start(f32[1,1,128]{2,1,0:T(1,128)S(1)} %get-tuple-element.79), channel_id=1, source_target_pairs={{0,16},{16,32},{32,48},{48,64},{64,80},{80,96},{96,112},{1,17},{17... | collective-permute-start | bytes 1544 | tf_op jit(solution)/shard_map/ppermute | solution.py:16
  372.5 6.6 collective-permute-start.45
  373.8 5.2 collective-permute-start.44
  375.9 4.1 collective-permute-start.40
  379.0 3.6 collective-permute-start.39
  522.0 2.4 collective-permute-start.50
  524.3 4.4 collective-permute-start.51
  525.3 12.2 %collective-permute-start.54 = (f32[1,1,128]{2,1,0:T(1,128)S(1)}, f32[1,1,128]{2,1,0:T(1,128)S(1)}, u32[]{:S(2)}, u32[]{:S(2)}) collective-permute-start(f32[1,1,128]{2,1,0:T(1,128)S(1)} %get-tuple-element.73), channel_id=1, source_target_pairs={{0,16},{16,32},{32,48},{48,64},{64,80},{80,96},{96,112},{1,17},{17... | collective-permute-start | bytes 1544 | tf_op jit(solution)/shard_map/ppermute | solution.py:16
  527.4 6.6 collective-permute-start.53
  528.7 5.2 collective-permute-start.52
  530.8 4.1 collective-permute-start.48
  533.9 3.6 collective-permute-start.47
  610.7 31.3 %collective-permute-start.9 = (f32[50,1,128]{2,1,0:T(1,128)}, f32[50,1,128]{2,1,0:T(1,128)}, u32[]{:S(2)}, u32[]{:S(2)}) collective-permute-start(f32[50,1,128]{2,1,0:T(1,128)} %get-tuple-element.47), channel_id=1, source_target_pairs={{0,1},{1,0},{2,3},{3,2},{4,5},{5,4},{6,7},{7,6},{8,9},{9,8},{10,11... | collective-permute-start | bytes 76808 | tf_op jit(solution)/shard_map/ppermute | solution.py:25
  610.9 7.8 %collective-permute-start.57 = (f32[1,1,128]{2,1,0:T(1,128)S(1)}, f32[1,1,128]{2,1,0:T(1,128)S(1)}, u32[]{:S(2)}, u32[]{:S(2)}) collective-permute-start(f32[1,1,128]{2,1,0:T(1,128)S(1)} %collective-permute-done.56), channel_id=1, source_target_pairs={{0,2},{1,3},{2,0},{3,1},{4,6},{5,7},{6,4},{7,5},{8,10},{9,11},{10,... | collective-permute-start | bytes 1544 | tf_op jit(solution)/shard_map/ppermute | solution.py:25
  616.4 10.2 %collective-permute-start.3 = (f32[50,64,1]{1,0,2:T(8,128)}, f32[50,64,1]{1,0,2:T(8,128)}, u32[]{:S(2)}, u32[]{:S(2)}) collective-permute-start(f32[50,64,1]{1,0,2:T(8,128)} %copy.65), channel_id=1, source_target_pairs={{0,1},{1,2},{2,3},{3,4},{4,5},{5,6},{6,7},{7,8},{8,9},{9,10},{10,1... | collective-permute-start | bytes 38408 | tf_op jit(solution)/shard_map/ppermute | solution.py:16
  618.7 10.4 %collective-permute-start.1 = (f32[50,64,1]{1,0,2:T(8,128)}, f32[50,64,1]{1,0,2:T(8,128)S(1)}, u32[]{:S(2)}, u32[]{:S(2)}) collective-permute-start(f32[50,64,1]{1,0,2:T(8,128)} %copy.64), channel_id=1, source_target_pairs={{1,0},{2,1},{3,2},{4,3},{5,4},{6,5},{7,6},{8,7},{9,8},{10,9},{11,1... | collective-permute-start | bytes 38408 | tf_op jit(solution)/shard_map/ppermute | solution.py:19
  618.7 6.2 collective-permute-start.58
  623.6 11.8 %collective-permute-start.60 = (f32[1,1,128]{2,1,0:T(1,128)S(1)}, f32[1,1,128]{2,1,0:T(1,128)S(1)}, u32[]{:S(2)}, u32[]{:S(2)}) collective-permute-start(f32[1,1,128]{2,1,0:T(1,128)S(1)} %get-tuple-element.70), channel_id=1, source_target_pairs={{16,0},{32,16},{48,32},{64,48},{80,64},{96,80},{112,96},{17,1},{33... | collective-permute-start | bytes 1544 | tf_op jit(solution)/shard_map/ppermute | solution.py:19
  624.9 10.4 %collective-permute-start.59 = (f32[1,1,128]{2,1,0:T(1,128)S(1)}, f32[1,1,128]{2,1,0:T(1,128)S(1)}, u32[]{:S(2)}, u32[]{:S(2)}) collective-permute-start(f32[1,1,128]{2,1,0:T(1,128)S(1)} %collective-permute-done.58), channel_id=1, source_target_pairs={{0,8},{1,9},{2,10},{3,11},{4,12},{5,13},{6,14},{7,15},{8,0},{9,1},... | collective-permute-start | bytes 1544 | tf_op jit(solution)/shard_map/ppermute | solution.py:25
  630.9 5.3 collective-permute-start.55
  642.0 16.5 %collective-permute-start.10 = (f32[50,1,128]{2,1,0:T(1,128)}, f32[50,1,128]{2,1,0:T(1,128)}, u32[]{:S(2)}, u32[]{:S(2)}) collective-permute-start(f32[50,1,128]{2,1,0:T(1,128)} %collective-permute-done.9), channel_id=1, source_target_pairs={{0,2},{1,3},{2,0},{3,1},{4,6},{5,7},{6,4},{7,5},{8,10},{9,11},{10,... | collective-permute-start | bytes 76808 | tf_op jit(solution)/shard_map/ppermute | solution.py:25
  645.4 31.7 %collective-permute-start.68 = (f32[100,1,128]{2,1,0:T(1,128)}, f32[100,1,128]{2,1,0:T(1,128)S(1)}, u32[]{:S(2)}, u32[]{:S(2)}) collective-permute-start(f32[100,1,128]{2,1,0:T(1,128)} %get-tuple-element.45), channel_id=1, source_target_pairs={{0,16},{16,32},{32,48},{48,64},{64,80},{80,96},{96,112},{1,17},{17... | collective-permute-start | bytes 153608 | tf_op jit(solution)/shard_map/ppermute | solution.py:16
  649.0 30.1 %collective-permute-start.63 = (f32[100,1,128]{2,1,0:T(1,128)}, f32[100,1,128]{2,1,0:T(1,128)}, u32[]{:S(2)}, u32[]{:S(2)}) collective-permute-start(f32[100,1,128]{2,1,0:T(1,128)} %get-tuple-element.45), channel_id=1, source_target_pairs={{0,1},{1,0},{2,3},{3,2},{4,5},{5,4},{6,7},{7,6},{8,9},{9,8},{10,11... | collective-permute-start | bytes 153608 | tf_op jit(solution)/shard_map/ppermute | solution.py:25
  652.9 10.8 %collective-permute-start.61 = (f32[100,64,1]{0,1,2:T(8,128)}, f32[100,64,1]{0,1,2:T(8,128)}, u32[]{:S(2)}, u32[]{:S(2)}) collective-permute-start(f32[100,64,1]{0,1,2:T(8,128)} %copy.60), channel_id=1, source_target_pairs={{1,0},{2,1},{3,2},{4,3},{5,4},{6,5},{7,6},{8,7},{9,8},{10,9},{11,1... | collective-permute-start | bytes 76808 | tf_op jit(solution)/shard_map/ppermute | solution.py:19
  657.2 14.8 %collective-permute-start.62 = (f32[100,64,1]{0,1,2:T(8,128)}, f32[100,64,1]{0,1,2:T(8,128)S(1)}, u32[]{:S(2)}, u32[]{:S(2)}) collective-permute-start(f32[100,64,1]{0,1,2:T(8,128)} %copy.62), channel_id=1, source_target_pairs={{0,1},{1,2},{2,3},{3,4},{4,5},{5,6},{6,7},{7,8},{8,9},{9,10},{10,1... | collective-permute-start | bytes 76808 | tf_op jit(solution)/shard_map/ppermute | solution.py:16
  658.5 24.2 %collective-permute-start.11 = (f32[50,1,128]{2,1,0:T(1,128)}, f32[50,1,128]{2,1,0:T(1,128)}, u32[]{:S(2)}, u32[]{:S(2)}) collective-permute-start(f32[50,1,128]{2,1,0:T(1,128)} %collective-permute-done.10), channel_id=1, source_target_pairs={{0,4},{1,5},{2,6},{3,7},{4,0},{5,1},{6,2},{7,3},{8,12},{9,13},{10,... | collective-permute-start | bytes 76808 | tf_op jit(solution)/shard_map/ppermute | solution.py:25
  663.7 37.3 %collective-permute-start.15 = (f32[50,1,128]{2,1,0:T(1,128)}, f32[50,1,128]{2,1,0:T(1,128)}, u32[]{:S(2)}, u32[]{:S(2)}) collective-permute-start(f32[50,1,128]{2,1,0:T(1,128)} %get-tuple-element.47), channel_id=1, source_target_pairs={{0,16},{16,32},{32,48},{48,64},{64,80},{80,96},{96,112},{1,17},{17... | collective-permute-start | bytes 76808 | tf_op jit(solution)/shard_map/ppermute | solution.py:16
  672.0 23.1 %collective-permute-start.13 = (f32[50,1,128]{2,1,0:T(1,128)}, f32[50,1,128]{2,1,0:T(1,128)}, u32[]{:S(2)}, u32[]{:S(2)}) collective-permute-start(f32[50,1,128]{2,1,0:T(1,128)} %get-tuple-element.46), channel_id=1, source_target_pairs={{16,0},{32,16},{48,32},{64,48},{80,64},{96,80},{112,96},{17,1},{33... | collective-permute-start | bytes 76808 | tf_op jit(solution)/shard_map/ppermute | solution.py:19
  677.7 32.8 %collective-permute-start.67 = (f32[100,1,128]{2,1,0:T(1,128)}, f32[100,1,128]{2,1,0:T(1,128)}, u32[]{:S(2)}, u32[]{:S(2)}) collective-permute-start(f32[100,1,128]{2,1,0:T(1,128)} %get-tuple-element.44), channel_id=1, source_target_pairs={{16,0},{32,16},{48,32},{64,48},{80,64},{96,80},{112,96},{17,1},{33... | collective-permute-start | bytes 153608 | tf_op jit(solution)/shard_map/ppermute | solution.py:19
  679.1 15.4 %collective-permute-start.64 = (f32[100,1,128]{2,1,0:T(1,128)}, f32[100,1,128]{2,1,0:T(1,128)}, u32[]{:S(2)}, u32[]{:S(2)}) collective-permute-start(f32[100,1,128]{2,1,0:T(1,128)} %collective-permute-done.63), channel_id=1, source_target_pairs={{0,2},{1,3},{2,0},{3,1},{4,6},{5,7},{6,4},{7,5},{8,10},{9,11},{10,... | collective-permute-start | bytes 153608 | tf_op jit(solution)/shard_map/ppermute | solution.py:25
  682.7 10.3 %collective-permute-start.12 = (f32[50,1,128]{2,1,0:T(1,128)}, f32[50,1,128]{2,1,0:T(1,128)}, u32[]{:S(2)}, u32[]{:S(2)}) collective-permute-start(f32[50,1,128]{2,1,0:T(1,128)} %collective-permute-done.11), channel_id=1, source_target_pairs={{0,8},{1,9},{2,10},{3,11},{4,12},{5,13},{6,14},{7,15},{8,0},{9,1},... | collective-permute-start | bytes 76808 | tf_op jit(solution)/shard_map/ppermute | solution.py:25
  694.5 4.7 collective-permute-start.65
  699.2 10.3 %collective-permute-start.66 = (f32[100,1,128]{2,1,0:T(1,128)S(1)}, f32[100,1,128]{2,1,0:T(1,128)}, u32[]{:S(2)}, u32[]{:S(2)}) collective-permute-start(f32[100,1,128]{2,1,0:T(1,128)S(1)} %collective-permute-done.65), channel_id=1, source_target_pairs={{0,8},{1,9},{2,10},{3,11},{4,12},{5,13},{6,14},{7,15},{8,0},{9,1},... | collective-permute-start | bytes 153608 | tf_op jit(solution)/shard_map/ppermute | solution.py:25
  (18 other events, 709.8 us)
where the time goes:
time: 737 us; the launch traced here: 725 us
  blocking collectives  474 us (64%)
  starting transfers between devices  116 us (16%)
  other arithmetic  55 us (7%)
  waiting for transfers between devices  35.3 us (5%)
  local copies, waits for them, and re-layouts  33.4 us (5%)
  between operations  11 us (1%)
    psum x4, blocking collectives, weighted_norm(): return lax.psum(jnp.sum(current * scaled), ('lat', 'lon'))  267 us
    psum x3, blocking collectives, local(): lax.psum(jnp.sum(direction * applied), ('lat', 'lon'))  207 us
    ppermute x36, starting transfers between devices, from_partner(): lax.ppermute(array, axis, [(i, i ^ 1 << stride) for i in range(lax.axis_s...  57.1 us
    ppermute x16, starting transfers between devices, extended(): lax.ppermute(lax.slice_in_dim(block, block.shape[dim] - width, None, axis...  41.7 us
    ppermute x36, waiting for transfers between devices, from_partner(): lax.ppermute(array, axis, [(i, i ^ 1 << stride) for i in range(lax.axis_s...  19.8 us
    ppermute x17, starting transfers between devices, extended(): lax.ppermute(lax.slice_in_dim(block, 0, width, axis=dim), axis, backward)  17.3 us
  transfers between devices with their start and end apart: 69, of which 23 were waited for; matrix products, arithmetic and copies ran while one was open for 9% of the time, Pallas kernels for 0%

commit v1 on v0

v1 whole, which is shorter than its diff:
```python
import jax
import jax.numpy as jnp
from jax import lax
from jax.experimental import pallas as pl
from jax.experimental.pallas import tpu as pltpu
from jax.sharding import PartitionSpec as P

WIDE = 6
PAD = 8
SHIFTS = (1.0, 0.3, 1.7)
PARTS = 5
LANES = 128
BOTH = ("lat", "lon")
VMEM_BYTES = 24 * 1024 * 1024

DEPTH_AT, STORE_AT, SOURCE_AT, STRIP_AT, DIFF_AT = 64, 70, 76, 82, 88
LEVEL_ROWS = 56
RAW_AT = 3 * PAD
PAIR_AT = RAW_AT + LEVEL_ROWS
MESSAGE_ROWS = PAIR_AT + LEVEL_ROWS


def iota(shape, dim):
    return lax.broadcasted_iota(jnp.int32, shape, dim)


def turn(values, shift, dim):
    return pltpu.roll(values, shift % values.shape[dim], dim)


def pack_kernel(
    east, north, tracer, depth, storage, surf, diff,
    to_east, to_west, source, rows_out,
    px, py, m_east, m_north, first_east, first_west, second_east, second_west,
):
    step = pl.program_id(0)
    size, rows, lanes = east.shape
    lane = iota((rows, lanes), 1)
    row = iota((rows, lanes), 0)

    @pl.when(step == 0)
    def _():
        deep = depth[...].astype(jnp.float32)
        m_east[...] = jnp.where(lane == lanes - 1, 0.0, jnp.minimum(deep, turn(deep, -1, 1)))
        m_north[...] = jnp.where(row == rows - 1, 0.0, jnp.minimum(deep, turn(deep, -1, 0)))
        for ref in (px, py, first_east, first_west, second_east, second_west):
            ref[...] = jnp.zeros((rows, lanes), jnp.float32)
        rows_out[...] = jnp.zeros(rows_out.shape, jnp.float32)

    levels = [step * size + t for t in range(size)]
    for number, ref in enumerate((east, north, tracer)):
        for t, level in enumerate(levels):
            rows_out[number, pl.ds(level, 1), :] = ref[t, rows - 1 : rows, :]
            rows_out[3 + number, pl.ds(level, 1), :] = ref[t, 0:1, :]
    for ref, limit, total in ((east, m_east, px), (north, m_north, py)):
        bound = limit[...]
        acc = total[...]
        for t, level in enumerate(levels):
            acc = acc + jnp.where(level.astype(jnp.float32) < bound, ref[t], 0.0)
        total[...] = acc
    for ref, start, low, high in (
        (east, 0, first_west, first_east),
        (north, 50, first_west, first_east),
        (tracer, 0, second_west, second_east),
    ):
        left, right = low[...], high[...]
        for t, level in enumerate(levels):
            here = lane == level + start
            values = ref[t]
            left = jnp.where(here, values[:, 0:1], left)
            right = jnp.where(here, values[:, lanes - 1 :], right)
        low[...] = left
        high[...] = right

    @pl.when(step == pl.num_programs(0) - 1)
    def _():
        plane = surf[...] + px[...] - turn(px[...], 1, 1) + py[...] - turn(py[...], 1, 0)
        source[...] = plane
        deep = depth[...].astype(jnp.float32)
        planes = (
            (deep, DEPTH_AT), (storage[...], STORE_AT), (plane, SOURCE_AT), (rows_out[1], STRIP_AT)
        )

        def put(target, values, start, place, count):
            moved = turn(values, place - start, 1)
            return jnp.where((lane >= place) & (lane < place + count), moved, target)

        for ref, first, second, start in (
            (to_east, first_east, second_east, lanes - WIDE), (to_west, first_west, second_west, 0)
        ):
            tile = second[...]
            for values, place in planes:
                tile = put(tile, values, start, place, WIDE)
            tile = put(tile, diff[...], lanes - 1, DIFF_AT, 1)
            ref[:, :lanes] = first[...]
            ref[:, lanes:] = tile


def stitch_kernel(
    from_west, from_east, to_east, depth, storage, source, diff, rows_in,
    wide, face_west, message_a, message_b,
):
    rows, lanes = depth.shape
    lane = iota((rows, lanes), 1)
    left_tile, right_tile = from_west[:, lanes:], from_east[:, lanes:]

    def side(place):
        right = turn(right_tile, -place, 1)
        left = turn(left_tile, lanes - WIDE - place, 1)
        return jnp.where(lane < WIDE, right, jnp.where(lane >= lanes - WIDE, left, 0.0))

    deep, deep_side = depth[...].astype(jnp.float32), side(DEPTH_AT)
    store, store_side = storage[...], side(STORE_AT)
    plane, plane_side = source[...], side(SOURCE_AT)
    strip = side(STRIP_AT)
    level = lane.astype(jnp.float32)
    bound = jnp.minimum(deep[:, lanes - 1 :], deep_side[:, 0:1])
    flux_east = jnp.sum(
        jnp.where(level < bound, to_east[:, :lanes], 0.0), axis=1, keepdims=True
    )
    bound = jnp.minimum(deep_side[:, lanes - 1 :], deep[:, 0:1])
    flux_west = jnp.sum(
        jnp.where(level < bound, from_west[:, :lanes], 0.0), axis=1, keepdims=True
    )
    first, last = lane == 0, lane == lanes - 1
    plane = plane + jnp.where(last, flux_east, 0.0) - jnp.where(first, flux_west, 0.0)
    plane_side = plane_side - jnp.where(first, flux_east, 0.0) + jnp.where(last, flux_west, 0.0)
    top_rows = rows_in[1]
    both = ((deep, deep_side), (store, store_side), (plane, plane_side), (top_rows, strip))
    for number, (one, two) in enumerate(both):
        wide[number, :, :lanes] = one
        wide[number, :, lanes:] = two
    faces = diff[...]
    face_west[...] = jnp.where(first, turn(left_tile, -DIFF_AT, 1), turn(faces, 1, 1))

    def fill(ref, up):
        start = rows - PAD if up else 0
        for number, (one, two) in enumerate(both[:3]):
            ref[number * PAD : (number + 1) * PAD, :lanes] = one[start : start + PAD]
            ref[number * PAD : (number + 1) * PAD, lanes:] = two[start : start + PAD]
        base = 0 if up else 3
        ref[RAW_AT:PAIR_AT, :lanes] = rows_in[base + 1, :LEVEL_ROWS]
        ref[RAW_AT:PAIR_AT, lanes:] = strip[:LEVEL_ROWS]
        ref[PAIR_AT:, :lanes] = rows_in[base, :LEVEL_ROWS]
        ref[PAIR_AT:, lanes:] = rows_in[base + 2, :LEVEL_ROWS]
        if up:
            ref[PAIR_AT - 1 : PAIR_AT, :lanes] = faces[rows - 1 :]

    even = lax.rem(lax.axis_index("lat"), 2) == 0

    @pl.when(even)
    def _():
        fill(message_a, True)
        fill(message_b, False)

    @pl.when(jnp.logical_not(even))
    def _():
        fill(message_a, False)
        fill(message_b, True)


def level_kernel(
    from_west, from_east, wide, diff, face_west, coriolis, east, north, tracer,
    east_out, north_out, tracer_out,
    m_east, m_west, m_north, m_south,
):
    step = pl.program_id(0)
    size, rows, lanes = east.shape
    lane = iota((rows, lanes), 1)
    row = iota((rows, lanes), 0)
    first, last = lane == 0, lane == lanes - 1

    @pl.when(step == 0)
    def _():
        deep, beside = wide[0, :, :lanes], wide[0, :, lanes:]
        m_east[...] = jnp.minimum(deep, jnp.where(last, beside[:, 0:1], turn(deep, -1, 1)))
        m_west[...] = jnp.minimum(deep, jnp.where(first, beside[:, lanes - 1 :], turn(deep, 1, 1)))
        m_north[...] = jnp.where(row == rows - 1, 0.0, jnp.minimum(deep, turn(deep, -1, 0)))
        m_south[...] = jnp.where(row == 0, 0.0, jnp.minimum(deep, turn(deep, 1, 0)))

    for t in range(size):
        level = step * size + t
        height = level.astype(jnp.float32)
        deep = wide[0, :, :lanes]
        wet = height < deep
        has_east, has_west = height < m_east[...], height < m_west[...]
        has_north, has_south = height < m_north[...], height < m_south[...]
        face = diff[...]
        left_face = face_west[...]
        south_face = turn(face, 1, 0)

        def smooth(values, tile, start):
            cols_east = from_east[:, tile * lanes : (tile + 1) * lanes]
            cols_west = from_west[:, tile * lanes : (tile + 1) * lanes]
            east_halo = pltpu.roll(cols_east, lanes - 1 - start - level, 1)
            west_halo = pltpu.roll(cols_west, lanes - start - level, 1)
            east_side = jnp.where(last, east_halo, turn(values, -1, 1))
            west_side = jnp.where(first, west_halo, turn(values, 1, 1))
            ahead = jnp.where(has_east, values - east_side, 0.0)
            ahead = ahead + jnp.where(has_north, values - turn(values, -1, 0), 0.0)
            flows = face * ahead + jnp.where(has_west, left_face * (values - west_side), 0.0)
            flows = flows + jnp.where(has_south, south_face * (values - turn(values, 1, 0)), 0.0)
            return jnp.where(wet, values, 0.0) - flows

        spin = jnp.where(wet, coriolis[...], 0.0)
        east_out[t] = smooth(east[t], 0, 0) - spin * north[t]
        north_out[t] = smooth(north[t], 0, 50) + spin * east[t]
        tracer_out[t] = smooth(tracer[t], 1, 0)


def shifted(values):
    return turn(values, -1, 1), turn(values, 1, 1), turn(values, -1, 0), turn(values, 1, 0)


def basis_kernel(thickness, got_a, got_b, wide, gram, basis, depth_wide, halo):
    rows, lanes = wide.shape[1], wide.shape[2] // 2
    lat = lax.axis_index("lat")
    even = lax.rem(lat, 2) == 0
    at_top = lat == lax.axis_size("lat") - 1
    at_bottom = lat == 0

    @pl.when(at_top)
    def _():
        back = lanes - 1 - iota((PAD, lanes), 1)
        for number in range(MESSAGE_ROWS // PAD):
            for tile in range(2):
                values = got_b[number * PAD : (number + 1) * PAD, tile * lanes : (tile + 1) * lanes]
                values = jnp.take_along_axis(values, back, axis=1)
                if number < 3:
                    values = jnp.concatenate(
                        [values[i : i + 1] for i in range(PAD - 1, -1, -1)], axis=0
                    )
                halo[0, number * PAD : (number + 1) * PAD, tile * lanes : (tile + 1) * lanes] = values

    @pl.when(jnp.logical_not(at_top))
    def _():
        halo[0] = jnp.where(even, got_a[...], got_b[...])

    halo[1] = jnp.where(at_bottom, 0.0, jnp.where(even, got_b[...], got_a[...]))

    def whole(number):
        place = slice(number * PAD, (number + 1) * PAD)
        return jnp.concatenate([halo[1, place], wide[number], halo[0, place]], axis=0)

    deep, store, plane = whole(0), whole(1), whole(2)
    depth_wide[...] = deep
    full = deep.shape
    row = iota(full, 0)
    core_end = PAD + rows
    level = iota((LEVEL_ROWS, full[1]), 0).astype(jnp.float32)
    bound = jnp.minimum(deep[core_end - 1 : core_end], deep[core_end : core_end + 1])
    edge = wide[3, :LEVEL_ROWS] - jnp.where(at_top, halo[0, RAW_AT:PAIR_AT], 0.0)
    flux = jnp.sum(jnp.where(level < bound, edge, 0.0), axis=0, keepdims=True)
    plane = plane + jnp.where(row == core_end - 1, flux, 0.0) - jnp.where(row == core_end, flux, 0.0)
    bound = jnp.minimum(deep[PAD - 1 : PAD], deep[PAD : PAD + 1])
    flux = jnp.sum(jnp.where(level < bound, halo[1, RAW_AT:PAIR_AT], 0.0), axis=0, keepdims=True)
    plane = plane + jnp.where(row == PAD - 1, flux, 0.0) - jnp.where(row == PAD, flux, 0.0)

    place = iota((PAD, lanes), 1)
    table = jnp.zeros((PAD, lanes), jnp.float32)
    for number in range(thickness.shape[0]):
        table = table + jnp.where(place > number, thickness[number], 0.0)

    def column(bound):
        index = bound.astype(jnp.int32)
        return jnp.concatenate(
            [
                jnp.concatenate(
                    [
                        jnp.take_along_axis(
                            table, index[i : i + PAD, j : j + lanes], axis=1
                        )
                        for j in range(0, full[1], lanes)
                    ],
                    axis=1,
                )
                for i in range(0, full[0], PAD)
            ],
            axis=0,
        )

    beside, _, above, _ = shifted(deep)
    to_east = column(jnp.minimum(deep, beside))
    to_north = column(jnp.minimum(deep, above))
    to_north = jnp.where(at_top & (row == core_end - 1), 2.0, 1.0) * to_north
    to_west, to_south = turn(to_east, 1, 1), turn(to_north, 1, 0)
    diag = store + to_east + to_west + to_north + to_south
    there = diag > 0.0
    inverse = jnp.where(there, 1.0 / jnp.where(there, diag, 1.0), 0.0)

    def operate(values):
        east_side, west_side, north_side, south_side = shifted(values)
        total = (
            store * values + to_east * (values - east_side) + to_west * (values - west_side)
        )
        return total + to_north * (values - north_side) + to_south * (values - south_side)

    vectors, images = [plane * inverse], []
    for number in range(4):
        images.append(operate(vectors[-1]))
        if number < 3:
            vectors.append(images[-1] * inverse - SHIFTS[number] * vectors[-1])
    for number in range(4):
        basis[number] = vectors[number]

    def core(values):
        return values[PAD:core_end, :lanes]

    sums = []
    for i in range(4):
        for j in range(i, 4):
            sums.append(core(vectors[i]) * core(images[j]))
    for i in range(4):
        sums.append(core(vectors[i]) * core(plane))
    sums = [jnp.sum(item, axis=0, keepdims=True) for item in sums]
    sums = sums + [jnp.zeros((1, lanes), jnp.float32)] * (16 - len(sums))
    sums = jnp.sum(jnp.concatenate(sums, axis=0), axis=1, keepdims=True)
    same = iota((16, lanes), 0) == iota((16, lanes), 1)
    line = jnp.sum(jnp.where(same, sums, 0.0), axis=0, keepdims=True)
    gram[...] = jnp.broadcast_to(line, gram.shape)


def solve(line):
    entry = [line[:, i : i + 1] for i in range(14)]
    system = [[None] * 5 for _ in range(4)]
    for i in range(4):
        for j in range(i, 4):
            system[i][j] = entry.pop(0)
    for i in range(4):
        system[i][4] = entry.pop(0)
    factor, part = {}, []
    for k in range(4):
        pivot = system[k][k]
        usable = pivot > 0.0
        scale = jnp.where(usable, 1.0 / jnp.where(usable, pivot, 1.0), 0.0)
        part.append(system[k][4] * scale)
        for i in range(k + 1, 4):
            factor[i, k] = system[k][i] * scale
            for j in range(i, 5):
                system[i][j] = system[i][j] - factor[i, k] * system[k][j]
    for k in range(2, -1, -1):
        for i in range(k + 1, 4):
            part[k] = part[k] - factor[i, k] * part[i]
    return part


def final_kernel(
    thickness, totals, basis, depth_wide, storage, diff, face_west, coriolis, halo, rows_in,
    east, north, tracer_in,
    tracer, east_out, north_out, surface,
    planes, fixes, edges, load_sems, store_sems,
):
    step = pl.program_id(0)
    size, rows, lanes = east.shape
    levels_count = edges.shape[1]
    core_end = PAD + rows

    def edge_copy(number, back):
        inside = tracer.at[:, pl.ds(number * (rows - PAD), PAD), :]
        if back:
            return pltpu.make_async_copy(edges.at[number], inside, store_sems.at[number])
        return pltpu.make_async_copy(inside, edges.at[number], load_sems.at[number])

    @pl.when(step == 0)
    def _():
        edge_copy(0, False).start()
        edge_copy(1, False).start()
        at_top = lax.axis_index("lat") == lax.axis_size("lat") - 1
        row = iota((rows, lanes), 0)
        deep = depth_wide[...]
        bounds = [jnp.minimum(deep, item)[PAD:core_end, :lanes] for item in shifted(deep)]
        face = diff[...]
        north_face = face + jnp.where(
            at_top & (row == rows - 1), halo[0, PAIR_AT - 1 : PAIR_AT, :lanes], 0.0
        )
        south_face = jnp.where(row == 0, halo[1, PAIR_AT - 1 : PAIR_AT, :lanes], turn(face, 1, 0))
        faces = (face, face_west[...], north_face, south_face)
        planes[0] = deep[PAD:core_end, :lanes]
        for number in range(4):
            planes[1 + number] = bounds[number]
        level = iota((LEVEL_ROWS, lanes), 0).astype(jnp.float32)
        for side, line in ((0, rows - 1), (1, 0)):
            bound = bounds[2 + side][line : line + 1]
            weight = faces[2 + side][line : line + 1]
            outer = (
                halo[side, PAIR_AT:, :lanes],
                halo[side, RAW_AT:PAIR_AT, :lanes],
                halo[side, PAIR_AT:, lanes:],
            )
            for number in range(3):
                inner = rows_in[3 * side + number, :LEVEL_ROWS]
                fixes[3 * side + number] = jnp.where(
                    level < bound, weight * (outer[number] - inner), 0.0
                )
        parts = solve(jnp.sum(totals[...], axis=0, keepdims=True))
        height = parts[0] * basis[0]
        for number in range(1, 4):
            height = height + parts[number] * basis[number]
        surface[...] = storage[...] * height[PAD:core_end, :lanes]
        full_row = iota(height.shape, 0)
        folded = at_top & (full_row == core_end)
        to_east, to_west, to_north, to_south = shifted(height)
        slope_x = jnp.where(folded, to_west, to_east) - height
        slope_y = jnp.where(folded, to_south, to_north) - height
        inner_x, inner_y = slope_x[PAD:core_end, :lanes], slope_y[PAD:core_end, :lanes]
        spin = coriolis[...]
        planes[5] = inner_x - spin * inner_y
        planes[6] = inner_y + spin * inner_x
        for start, slope, inner in ((7, slope_x, inner_x), (11, slope_y, inner_y)):
            for number, item in enumerate(shifted(slope)):
                planes[start + number] = faces[number] * (inner - item[PAD:core_end, :lanes])
        for number, line in ((0, 0), (1, PAD - 1)):
            edge_copy(number, False).wait()
            fix = fixes[3 * (1 - number) + 2]
            edges[number, :, line, :] = edges[number, :, line, :] + fix[:levels_count]
            edge_copy(number, True).start()

    line = iota((PAD, lanes), 0)
    for tile in range(rows // PAD):
        place = slice(tile * PAD, (tile + 1) * PAD)
        own = [planes[number, place] for number in range(15)]
        for t in range(size):
            level = step * size + t
            height = level.astype(jnp.float32)
            open_sides = [height < own[number] for number in range(5)]
            for out, values, base, start, number in (
                (east_out, east, 5, 7, 0), (north_out, north, 6, 11, 1)
            ):
                change = jnp.where(open_sides[0], own[base], 0.0)
                for side in range(4):
                    change = change - jnp.where(open_sides[1 + side], own[start + side], 0.0)
                result = values[t, place] + thickness[level] * change
                if tile == 0:
                    fix = fixes[3 + number, pl.ds(level, 1), :]
                    result = result + jnp.where(line == 0, fix, 0.0)
                if tile == rows // PAD - 1:
                    fix = fixes[number, pl.ds(level, 1), :]
                    result = result + jnp.where(line == PAD - 1, fix, 0.0)
                out[t, place] = result

    @pl.when(step == pl.num_programs(0) - 1)
    def _():
        edge_copy(0, True).wait()
        edge_copy(1, True).wait()


def swaps(lats, lons, odd):
    pairs = []
    for lat in range(lats):
        for lon in range(lons):
            other = lat + 1 if lat % 2 == odd else lat - 1
            if other < 0:
                continue
            if other == lats:
                pairs.append((lat * lons + lon, lat * lons + lons - 1 - lon))
            else:
                pairs.append((lat * lons + lon, other * lons + lon))
    return pairs


def local(
    tracer_cot, east_cot, north_cot, surface_cot, depth_levels, diffusivity, coriolis, storage,
    thickness,
):
    levels, rows, lanes = tracer_cot.shape
    size = levels // PARTS
    lats, lons = lax.axis_size("lat"), lax.axis_size("lon")
    floats = lambda *shape: jax.ShapeDtypeStruct(shape, jnp.float32)
    scratch = lambda *shape: pltpu.VMEM(shape, jnp.float32)
    whole = lambda *shape: pl.BlockSpec(shape, lambda *_: (0,) * len(shape))
    block = pl.BlockSpec((size, rows, lanes), lambda i: (i, 0, 0))
    plane = whole(rows, lanes)
    pair = whole(rows, 2 * lanes)
    scalars = pl.BlockSpec(memory_space=pltpu.SMEM)
    anywhere = pl.BlockSpec(memory_space=pl.ANY)
    params = pltpu.CompilerParams(vmem_limit_bytes=VMEM_BYTES)
    full = (rows + 2 * PAD, 2 * lanes)
    message = (MESSAGE_ROWS, 2 * lanes)

    to_east, to_west, source, edge_rows = pl.pallas_call(
        pack_kernel,
        grid=(PARTS,),
        in_specs=[block] * 3 + [plane] * 4,
        out_specs=[pair, pair, plane, whole(6, rows, lanes)],
        out_shape=[floats(rows, 2 * lanes)] * 2 + [floats(rows, lanes), floats(6, rows, lanes)],
        scratch_shapes=[scratch(rows, lanes)] * 8,
        compiler_params=params,
        name="pack",
    )(east_cot, north_cot, tracer_cot, depth_levels, storage, surface_cot, diffusivity)

    from_west = lax.ppermute(to_east, "lon", [(i, (i + 1) % lons) for i in range(lons)])
    from_east = lax.ppermute(to_west, "lon", [(i, (i - 1) % lons) for i in range(lons)])

    wide, face_west, message_a, message_b = pl.pallas_call(
        stitch_kernel,
        grid=(1,),
        in_specs=[pair] * 3 + [plane] * 4 + [whole(6, rows, lanes)],
        out_specs=[whole(4, rows, 2 * lanes), plane, whole(*message), whole(*message)],
        out_shape=[
            floats(4, rows, 2 * lanes), floats(rows, lanes), floats(*message), floats(*message)
        ],
        compiler_params=params,
        name="stitch",
    )(from_west, from_east, to_east, depth_levels, storage, source, diffusivity, edge_rows)

    got_a = lax.ppermute(message_a, BOTH, swaps(lats, lons, 0))
    got_b = lax.ppermute(message_b, BOTH, swaps(lats, lons, 1))

    east_part, north_part, tracer_part = pl.pallas_call(
        level_kernel,
        grid=(PARTS,),
        in_specs=[pair, pair, whole(4, rows, 2 * lanes)] + [plane] * 3 + [block] * 3,
        out_specs=[block] * 3,
        out_shape=[floats(levels, rows, lanes)] * 3,
        scratch_shapes=[scratch(rows, lanes)] * 4,
        compiler_params=params,
        cost_estimate=pl.CostEstimate(
            flops=60 * levels * rows * lanes, bytes_accessed=24 * levels * rows * lanes,
            transcendentals=0,
        ),
        name="level",
    )(from_west, from_east, wide, diffusivity, face_west, coriolis, east_cot, north_cot, tracer_cot)

    gram, basis, depth_wide, halo = pl.pallas_call(
        basis_kernel,
        grid=(1,),
        in_specs=[scalars, whole(*message), whole(*message), whole(4, rows, 2 * lanes)],
        out_specs=[
            whole(lats * lons, lanes), whole(4, *full), whole(*full), whole(2, *message)
        ],
        out_shape=[
            floats(lats * lons, lanes), floats(4, *full), floats(*full), floats(2, *message)
        ],
        compiler_params=params,
        name="basis",
    )(thickness, got_a, got_b, wide)

    totals = lax.all_to_all(gram, BOTH, 0, 0, tiled=True)

    tracer_adj, east_adj, north_adj, surface_adj = pl.pallas_call(
        final_kernel,
        grid=(PARTS,),
        in_specs=[scalars, whole(lats * lons, lanes), whole(4, *full), whole(*full)]
        + [plane] * 4
        + [whole(2, *message), whole(6, rows, lanes), block, block, anywhere],
        out_specs=[anywhere, block, block, plane],
        out_shape=[floats(levels, rows, lanes)] * 3 + [floats(rows, lanes)],
        scratch_shapes=[
            scratch(15, rows, lanes),
            scratch(6, LEVEL_ROWS, lanes),
            scratch(2, levels, PAD, lanes),
            pltpu.SemaphoreType.DMA((2,)),
            pltpu.SemaphoreType.DMA((2,)),
        ],
        input_output_aliases={12: 0},
        compiler_params=params,
        name="final",
    )(
        thickness, totals, basis, depth_wide, storage, diffusivity, face_west, coriolis, halo,
        edge_rows, east_part, north_part, tracer_part,
    )
    return tracer_adj, east_adj, north_adj, surface_adj


def solution(mesh):
    field, plane = P(None, "lat", "lon"), P("lat", "lon")
    return jax.shard_map(
        local,
        mesh=mesh,
        in_specs=(field, field, field, plane, plane, plane, plane, plane, P()),
        out_specs=(field, field, field, plane),
        check_vma=False,
    )
```

time: 737 us -> 79.8 us (0.11); the launches traced: 725 us -> 78.4 us
  blocking collectives: 474 us -> 0 us
  starting transfers between devices: 116 us -> 23.1 us
  other arithmetic: 55 us -> 0 us
  waiting for transfers between devices: 35.3 us -> 7.62 us
  Pallas kernels: 0 us -> 19 us
  between operations: 11 us -> 0.76 us
    psum x7 -> x0, blocking collectives: 474 us -> none  [the longest x4 267 us: weighted_norm(): return lax.psum(jnp.sum(current * scaled), ('lat', 'lon'))]
    ppermute x69 -> x4, starting transfers between devices: 116 us -> 3.81 us  [the longest x1 1.49 us: local(): lax.ppermute(to_west, 'lon', [(i, (i - 1) % lons) for i in range(lons)])]
    ppermute x69 -> x4, waiting for transfers between devices: 35.3 us -> 7.61 us  [the longest x1 3.22 us: local(): got_a = lax.ppermute(message_a, BOTH, swaps(lats, lons, 0))]
    unnamed x28 -> x72, local copies, waits for them, and re-layouts: 5.89 us -> 28 us
    all_to_all x0 -> x1, starting transfers between devices: none -> 19.2 us  [local(): totals = lax.all_to_all(gram, BOTH, 0, 0, tiled=True)]
    pallas_call x0 -> x5, Pallas kernels: none -> 19 us  [the longest x1 7.11 us: local(): pl.pallas_call(level_kernel, grid=(PARTS,), in_specs=[pair, pair, whole(4...]
    concatenate x5 -> x0, other arithmetic: 17.8 us -> none  [the longest x1 8.88 us: extended(): block = jnp.concatenate([low, block, high], axis=dim)]
    ppermute x4 -> x0, local copies, waits for them, and re-layouts: 12.5 us -> none  [the longest x2 6.27 us: extended(): lax.ppermute(lax.slice_in_dim(block, 0, width, axis=dim), axis, backward)]
  transfers between devices with their start and end apart: 69 -> 5, of which waited for: 23 -> 3; matrix products, arithmetic and copies ran while one was open for 9% -> 0% of each run, Pallas kernels for 0% -> 9%
where the time goes in v1:
time: 79.8 us; the launch traced here: 78.4 us
  local copies, waits for them, and re-layouts  28 us (35%)
  starting transfers between devices  23.1 us (29%)
  Pallas kernels  19 us (24%)
  waiting for transfers between devices  7.62 us (10%)
    unnamed x72, local copies, waits for them, and re-layouts  28 us
    all_to_all x1, starting transfers between devices, local(): totals = lax.all_to_all(gram, BOTH, 0, 0, tiled=True)  19.2 us
    pallas_call x1, Pallas kernels, local(): pl.pallas_call(level_kernel, grid=(PARTS,), in_specs=[pair, pair, whole(4...  7.11 us
    pallas_call x1, Pallas kernels, local(): pl.pallas_call(final_kernel, grid=(PARTS,), in_specs=[scalars, whole(lats...  6.61 us
    pallas_call x1, Pallas kernels, local(): pl.pallas_call(pack_kernel, grid=(PARTS,), in_specs=[block] * 3 + [plane]...  3.62 us
    ppermute x1, waiting for transfers between devices, local(): got_a = lax.ppermute(message_a, BOTH, swaps(lats, lons, 0))  3.22 us
    ppermute x1, waiting for transfers between devices, local(): lax.ppermute(to_east, 'lon', [(i, (i + 1) % lons) for i in range(lons)])  2.53 us
    ppermute x1, waiting for transfers between devices, local(): lax.ppermute(to_west, 'lon', [(i, (i - 1) % lons) for i in range(lons)])  1.87 us
  transfers between devices with their start and end apart: 5, of which 3 were waited for; matrix products, arithmetic and copies ran while one was open for 0% of the time, Pallas kernels for 9%

profile of v1, /device:TPU:1, one launch (start us, length us, event | category | flops | bytes accessed | tf_op | source)
XLA Modules:
  0.0 78.4 jit_solution(16784596014614724207)
XLA Ops:
  0.6 0.0 copy-start
  0.6 1.4 %copy-done = f32[50,64,128]{2,1,0:T(8,128)S(1)} copy-done((f32[50,64,128]{2,1,0:T(8,128)S(1)}, f32[50,64,128]{2,1,0:T(8,128)}, u32[]{:S(2)}) %copy-start) | copy-done | bytes 1638424
  2.1 0.0 copy-start.2
  2.1 1.4 %copy-done.2 = f32[50,64,128]{2,1,0:T(8,128)S(1)} copy-done((f32[50,64,128]{2,1,0:T(8,128)S(1)}, f32[50,64,128]{2,1,0:T(8,128)}, u32[]{:S(2)}) %copy-start.2) | copy-done | bytes 1638424
  3.5 0.0 copy-start.4
  3.5 1.4 %copy-done.4 = f32[50,64,128]{2,1,0:T(8,128)S(1)} copy-done((f32[50,64,128]{2,1,0:T(8,128)S(1)}, f32[50,64,128]{2,1,0:T(8,128)}, u32[]{:S(2)}) %copy-start.4) | copy-done | bytes 1638424
  4.9 0.0 copy-start.12
  4.9 0.8 copy-done.12
  5.7 0.0 copy-start.17
  5.7 0.8 copy-done.17
  6.4 0.0 copy-start.30
  6.4 0.8 copy-done.30
  7.2 0.0 copy-start.34
  7.2 0.8 copy-done.34
  8.0 0.0 copy-start.35
  8.0 0.0 copy-start.1
  8.0 0.0 copy-start.3
  8.0 3.6 %pack.1 = (f32[64,256]{1,0:T(8,128)S(1)}, f32[64,256]{1,0:T(8,128)S(1)}, f32[64,128]{1,0:T(8,128)S(1)}, f32[6,64,128]{2,1,0:T(8,128)S(1)}) custom-call(f32[50,64,128]{2,1,0:T(8,128)S(1)} %copy-done, f32[50,64,128]{2,1,0:T(8,128)S(1)} %copy-done.2, f32[50,64,128]{2,1,0:T(8,128)S(1)} %copy-done.4, s32[64,128]{1,0:T(8,128)S(1)} %copy-done.30, ...), custom_call_target="tpu_custom_call" | custom-call | tf_op jit(solution)/shard_map/pack/pallas_call | solution.py:480
  11.6 1.5 %collective-permute-start.1 = (f32[64,256]{1,0:T(8,128)S(1)}, f32[64,256]{1,0:T(8,128)S(1)}, u32[]{:S(2)}, u32[]{:S(2)}) collective-permute-start(f32[64,256]{1,0:T(8,128)S(1)} %get-tuple-element.20), channel_id=1, source_target_pairs={{0,15},{1,0},{2,1},{3,2},{4,3},{5,4},{6,5},{7,6},{8,7},{9,8},{10,9... | collective-permute-start | bytes 196616 | tf_op jit(solution)/shard_map/ppermute | solution.py:492
  13.1 1.3 %collective-permute-start = (f32[64,256]{1,0:T(8,128)S(1)}, f32[64,256]{1,0:T(8,128)S(1)}, u32[]{:S(2)}, u32[]{:S(2)}) collective-permute-start(f32[64,256]{1,0:T(8,128)S(1)} %get-tuple-element.19.to_east), channel_id=1, source_target_pairs={{0,1},{1,2},{2,3},{3,4},{4,5},{5,6},{6,7},{7,8},{8,9},{9,10},{10,1... | collective-permute-start | bytes 196616 | tf_op jit(solution)/shard_map/ppermute | solution.py:491
  14.4 1.9 %collective-permute-done.1.from_east = f32[64,256]{1,0:T(8,128)S(1)} collective-permute-done((f32[64,256]{1,0:T(8,128)S(1)}, f32[64,256]{1,0:T(8,128)S(1)}, u32[]{:S(2)}, u32[]{:S(2)}) %collective-permute-start.1) | collective-permute-done | bytes 65568 | tf_op jit(solution)/shard_map/ppermute | solution.py:492
  16.3 2.5 %collective-permute-done.from_west = f32[64,256]{1,0:T(8,128)S(1)} collective-permute-done((f32[64,256]{1,0:T(8,128)S(1)}, f32[64,256]{1,0:T(8,128)S(1)}, u32[]{:S(2)}, u32[]{:S(2)}) %collective-permute-start) | collective-permute-done | bytes 65568 | tf_op jit(solution)/shard_map/ppermute | solution.py:491
  18.8 0.3 stitch.1
  19.2 0.0 copy-start.10
  19.2 0.7 copy-done.10
  19.9 0.3 collective-permute-start.2
  20.2 0.7 collective-permute-start.3
  20.8 3.2 %collective-permute-done.2.got_a = f32[136,256]{1,0:T(8,128)S(1)} collective-permute-done((f32[136,256]{1,0:T(8,128)S(1)}, f32[136,256]{1,0:T(8,128)S(1)}, u32[]{:S(2)}, u32[]{:S(2)}) %collective-permute-start.2) | collective-permute-done | bytes 139296 | tf_op jit(solution)/shard_map/ppermute | solution.py:506
  24.1 0.0 collective-permute-done.3.got_b
  24.1 0.0 copy-done.35
  24.1 1.3 %basis.1 = (f32[128,128]{1,0:T(8,128)S(1)}, f32[4,80,256]{2,1,0:T(8,128)S(1)}, f32[80,256]{1,0:T(8,128)S(1)}, f32[2,136,256]{2,1,0:T(8,128)S(1)}) custom-call(f32[50]{0:T(128)S(1)} %copy-done.35, f32[136,256]{1,0:T(8,128)S(1)} %collective-permute-done.2.got_a, f32[136,256]{1,0:T(8,128)S(1)} %collective-permute-done.3.got_b, ...), custom_call_target="tpu_custom_call" | custom-call | tf_op jit(solution)/shard_map/basis/pallas_call | solution.py:524
  25.4 0.0 copy-done.21
  25.4 0.0 copy-start.15
  25.4 0.7 copy-done.15
  26.1 0.7 copy-done.19
  26.8 0.6 copy-done.31
  27.4 0.6 copy-done.33
  28.1 0.0 copy-done.23
  28.1 0.0 copy-done.27
  28.1 19.2 %all-to-all-start = ((f32[128,1,128]{2,1,0:T(1,128)}), f32[128,1,128]{2,1,0:T(1,128)}, u32[]{:S(2)}, u32[]{:S(2)}) async-start(f32[128,1,128]{2,1,0:T(1,128)} %bitcast.4), calls=%async_computation | async-start | bytes 131072 | tf_op jit(solution)/shard_map/all_to_all | solution.py:538
  47.3 0.0 copy-done.1
  47.3 0.0 copy-done.3
  47.3 0.0 copy-start.5
  47.3 1.4 %copy-done.5 = f32[50,64,128]{2,1,0:T(8,128)S(1)} copy-done((f32[50,64,128]{2,1,0:T(8,128)S(1)}, f32[50,64,128]{2,1,0:T(8,128)}, u32[]{:S(2)}) %copy-start.5) | copy-done | bytes 1638424
  48.8 0.8 copy-done.13
  49.5 0.8 %copy-done.22 = f32[64,256]{1,0:T(8,128)S(1)} copy-done((f32[64,256]{1,0:T(8,128)S(1)}, f32[64,256]{1,0:T(8,128)}, u32[]{:S(2)}) %copy-start.22) | copy-done | bytes 65560
  50.4 0.8 %copy-done.24 = f32[64,256]{1,0:T(8,128)S(1)} copy-done((f32[64,256]{1,0:T(8,128)S(1)}, f32[64,256]{1,0:T(8,128)}, u32[]{:S(2)}) %copy-start.24) | copy-done | bytes 65560
  51.2 0.8 copy-done.25
  52.0 0.8 copy-done.28
  52.7 7.1 %level.1 = (f32[50,64,128]{2,1,0:T(8,128)S(1)}, f32[50,64,128]{2,1,0:T(8,128)S(1)}, f32[50,64,128]{2,1,0:T(8,128)}) custom-call(f32[64,256]{1,0:T(8,128)S(1)} %copy-done.24, f32[64,256]{1,0:T(8,128)S(1)} %copy-done.22, f32[4,64,256]{2,1,0:T(8,128)S(1)} %get-tuple-element.25.wide, f32[64,128]{1,0:T(8,128)S(1)} %copy-done.13, f32[64,128]{1,0:T(8,128)S(1)} %copy-done.28, ...), custom_call_target="tpu_custom_call" | custom-call | flops 24576000 | bytes 9830400 | tf_op jit(solution)/shard_map/level/pallas_call | solution.py:509
  59.8 1.2 %copy-done.6 = f32[50,64,128]{2,1,0:T(8,128)} copy-done((f32[50,64,128]{2,1,0:T(8,128)}, f32[50,64,128]{2,1,0:T(8,128)S(1)}, u32[]{:S(2)}) %copy-start.6) | copy-done | bytes 1638424
  61.0 1.2 %copy-done.8 = f32[50,64,128]{2,1,0:T(8,128)} copy-done((f32[50,64,128]{2,1,0:T(8,128)}, f32[50,64,128]{2,1,0:T(8,128)S(1)}, u32[]{:S(2)}) %copy-start.8) | copy-done | bytes 1638424
  62.2 0.0 all-to-all-done
  62.2 1.4 %copy-done.7 = f32[50,64,128]{2,1,0:T(8,128)S(1)} copy-done((f32[50,64,128]{2,1,0:T(8,128)S(1)}, f32[50,64,128]{2,1,0:T(8,128)}, u32[]{:S(2)}) %copy-start.7) | copy-done | bytes 1638424
  63.6 1.4 %copy-done.9 = f32[50,64,128]{2,1,0:T(8,128)S(1)} copy-done((f32[50,64,128]{2,1,0:T(8,128)S(1)}, f32[50,64,128]{2,1,0:T(8,128)}, u32[]{:S(2)}) %copy-start.9) | copy-done | bytes 1638424
  65.0 0.9 %copy-done.11 = f32[6,64,128]{2,1,0:T(8,128)S(1)} copy-done((f32[6,64,128]{2,1,0:T(8,128)S(1)}, f32[6,64,128]{2,1,0:T(8,128)}, u32[]{:S(2)}) %copy-start.11) | copy-done | bytes 196632
  66.0 0.8 copy-done.14
  66.7 1.0 %copy-done.16 = f32[4,80,256]{2,1,0:T(8,128)S(1)} copy-done((f32[4,80,256]{2,1,0:T(8,128)S(1)}, f32[4,80,256]{2,1,0:T(8,128)}, u32[]{:S(2)}) %copy-start.16) | copy-done | bytes 327704
  67.7 0.8 copy-done.18
  68.4 1.0 %copy-done.20 = f32[2,136,256]{2,1,0:T(8,128)S(1)} copy-done((f32[2,136,256]{2,1,0:T(8,128)S(1)}, f32[2,136,256]{2,1,0:T(8,128)}, u32[]{:S(2)}) %copy-start.20) | copy-done | bytes 278552
  69.4 0.8 copy-done.26
  70.2 0.8 copy-done.29
  70.9 0.9 %copy-done.32 = f32[80,256]{1,0:T(8,128)S(1)} copy-done((f32[80,256]{1,0:T(8,128)S(1)}, f32[80,256]{1,0:T(8,128)}, u32[]{:S(2)}) %copy-start.32) | copy-done | bytes 81944
  71.8 6.6 %final.1 = (f32[50,64,128]{2,1,0:T(8,128)}, f32[50,64,128]{2,1,0:T(8,128)}, f32[50,64,128]{2,1,0:T(8,128)}, f32[64,128]{1,0:T(8,128)}) custom-call(f32[50]{0:T(128)S(1)} %copy-done.35, f32[128,128]{1,0:T(8,128)} %bitcast.2.totals, f32[4,80,256]{2,1,0:T(8,128)S(1)} %copy-done.16, f32[80,256]{1,0:T(8,128)S(1)} %copy-done.32, ...), custom_call_target="tpu_custom_call", output_to_operand_aliasing={{0}: (12, {})} | custom-call | tf_op jit(solution)/shard_map/final/pallas_call | solution.py:540
  (23 shorter events, 0.0 us)
Async XLA Ops:
  0.6 1.4 %copy-start = (f32[50,64,128]{2,1,0:T(8,128)S(1)}, f32[50,64,128]{2,1,0:T(8,128)}, u32[]{:S(2)}) copy-start(f32[50,64,128]{2,1,0:T(8,128)} %east.3) | copy-start | bytes 4915204
  2.1 1.4 %copy-start.2 = (f32[50,64,128]{2,1,0:T(8,128)S(1)}, f32[50,64,128]{2,1,0:T(8,128)}, u32[]{:S(2)}) copy-start(f32[50,64,128]{2,1,0:T(8,128)} %north.3) | copy-start | bytes 4915204
  3.5 1.4 %copy-start.4 = (f32[50,64,128]{2,1,0:T(8,128)S(1)}, f32[50,64,128]{2,1,0:T(8,128)}, u32[]{:S(2)}) copy-start(f32[50,64,128]{2,1,0:T(8,128)} %tracer.3) | copy-start | bytes 4915204
  4.9 0.8 copy-start.12
  5.7 0.8 copy-start.17
  6.4 0.8 copy-start.30
  7.2 0.8 copy-start.34
  8.0 16.1 %copy-start.35 = (f32[50]{0:T(128)S(1)}, f32[50]{0:T(128)}, u32[]{:S(2)}) copy-start(f32[50]{0:T(128)} %thickness.3) | copy-start | bytes 604
  8.0 39.4 %copy-start.1 = (f32[50,64,128]{2,1,0:T(8,128)S(1)}, f32[50,64,128]{2,1,0:T(8,128)}, u32[]{:S(2)}) copy-start(f32[50,64,128]{2,1,0:T(8,128)} %east.3) | copy-start | bytes 4915204
  8.0 39.4 %copy-start.3 = (f32[50,64,128]{2,1,0:T(8,128)S(1)}, f32[50,64,128]{2,1,0:T(8,128)}, u32[]{:S(2)}) copy-start(f32[50,64,128]{2,1,0:T(8,128)} %north.3) | copy-start | bytes 4915204
  11.6 4.7 %collective-permute-start.1 = (f32[64,256]{1,0:T(8,128)S(1)}, f32[64,256]{1,0:T(8,128)S(1)}, u32[]{:S(2)}, u32[]{:S(2)}) collective-permute-start(f32[64,256]{1,0:T(8,128)S(1)} %get-tuple-element.20), channel_id=1, source_target_pairs={{0,15},{1,0},{2,1},{3,2},{4,3},{5,4},{6,5},{7,6},{8,7},{9,8},{10,9... | collective-permute-start | bytes 196616 | tf_op jit(solution)/shard_map/ppermute | solution.py:492
  13.1 5.7 %collective-permute-start = (f32[64,256]{1,0:T(8,128)S(1)}, f32[64,256]{1,0:T(8,128)S(1)}, u32[]{:S(2)}, u32[]{:S(2)}) collective-permute-start(f32[64,256]{1,0:T(8,128)S(1)} %get-tuple-element.19.to_east), channel_id=1, source_target_pairs={{0,1},{1,2},{2,3},{3,4},{4,5},{5,6},{6,7},{7,8},{8,9},{9,10},{10,1... | collective-permute-start | bytes 196616 | tf_op jit(solution)/shard_map/ppermute | solution.py:491
  16.3 9.1 %copy-start.21 = (f32[64,256]{1,0:T(8,128)}, f32[64,256]{1,0:T(8,128)S(1)}, u32[]{:S(2)}) copy-start(f32[64,256]{1,0:T(8,128)S(1)} %collective-permute-done.1.from_east) | copy-start | bytes 196612
  18.8 9.2 %copy-start.23 = (f32[64,256]{1,0:T(8,128)}, f32[64,256]{1,0:T(8,128)S(1)}, u32[]{:S(2)}) copy-start(f32[64,256]{1,0:T(8,128)S(1)} %collective-permute-done.from_west) | copy-start | bytes 196612
  19.2 0.7 copy-start.10
  19.9 8.2 %copy-start.27 = (f32[64,128]{1,0:T(8,128)}, f32[64,128]{1,0:T(8,128)S(1)}, u32[]{:S(2)}) copy-start(f32[64,128]{1,0:T(8,128)S(1)} %get-tuple-element.29.face_west) | copy-start | bytes 98308
  19.9 4.2 %collective-permute-start.2 = (f32[136,256]{1,0:T(8,128)S(1)}, f32[136,256]{1,0:T(8,128)S(1)}, u32[]{:S(2)}, u32[]{:S(2)}) collective-permute-start(f32[136,256]{1,0:T(8,128)S(1)} %get-tuple-element.23), channel_id=1, source_target_pairs={{0,16},{1,17},{2,18},{3,19},{4,20},{5,21},{6,22},{7,23},{8,24},{9,... | collective-permute-start | bytes 417800 | tf_op jit(solution)/shard_map/ppermute | solution.py:506
  20.2 3.9 %collective-permute-start.3 = (f32[136,256]{1,0:T(8,128)S(1)}, f32[136,256]{1,0:T(8,128)S(1)}, u32[]{:S(2)}, u32[]{:S(2)}) collective-permute-start(f32[136,256]{1,0:T(8,128)S(1)} %get-tuple-element.24), channel_id=1, source_target_pairs={{16,32},{17,33},{18,34},{19,35},{20,36},{21,37},{22,38},{23,39},{2... | collective-permute-start | bytes 417800 | tf_op jit(solution)/shard_map/ppermute | solution.py:507
  25.4 0.7 copy-start.15
  26.1 0.7 copy-start.19
  26.8 0.6 copy-start.31
  27.4 0.6 copy-start.33
  28.1 34.1 %all-to-all-start = ((f32[128,1,128]{2,1,0:T(1,128)}), f32[128,1,128]{2,1,0:T(1,128)}, u32[]{:S(2)}, u32[]{:S(2)}) async-start(f32[128,1,128]{2,1,0:T(1,128)} %bitcast.4), calls=%async_computation | async-start | bytes 131072 | tf_op jit(solution)/shard_map/all_to_all | solution.py:538
  47.3 1.4 %copy-start.5 = (f32[50,64,128]{2,1,0:T(8,128)S(1)}, f32[50,64,128]{2,1,0:T(8,128)}, u32[]{:S(2)}) copy-start(f32[50,64,128]{2,1,0:T(8,128)} %tracer.3) | copy-start | bytes 4915204
  48.8 0.8 copy-start.13
  49.5 0.8 %copy-start.22 = (f32[64,256]{1,0:T(8,128)S(1)}, f32[64,256]{1,0:T(8,128)}, u32[]{:S(2)}) copy-start(f32[64,256]{1,0:T(8,128)} %copy-done.21) | copy-start | bytes 196612
  50.4 0.8 %copy-start.24 = (f32[64,256]{1,0:T(8,128)S(1)}, f32[64,256]{1,0:T(8,128)}, u32[]{:S(2)}) copy-start(f32[64,256]{1,0:T(8,128)} %copy-done.23) | copy-start | bytes 196612
  51.2 0.8 copy-start.25
  52.0 0.8 copy-start.28
  59.8 1.2 %copy-start.6 = (f32[50,64,128]{2,1,0:T(8,128)}, f32[50,64,128]{2,1,0:T(8,128)S(1)}, u32[]{:S(2)}) copy-start(f32[50,64,128]{2,1,0:T(8,128)S(1)} %get-tuple-element.31.east) | copy-start | bytes 4915204
  61.0 1.2 %copy-start.8 = (f32[50,64,128]{2,1,0:T(8,128)}, f32[50,64,128]{2,1,0:T(8,128)S(1)}, u32[]{:S(2)}) copy-start(f32[50,64,128]{2,1,0:T(8,128)S(1)} %get-tuple-element.32.north) | copy-start | bytes 4915204
  62.2 1.4 %copy-start.7 = (f32[50,64,128]{2,1,0:T(8,128)S(1)}, f32[50,64,128]{2,1,0:T(8,128)}, u32[]{:S(2)}) copy-start(f32[50,64,128]{2,1,0:T(8,128)} %copy-done.6) | copy-start | bytes 4915204
  63.6 1.4 %copy-start.9 = (f32[50,64,128]{2,1,0:T(8,128)S(1)}, f32[50,64,128]{2,1,0:T(8,128)}, u32[]{:S(2)}) copy-start(f32[50,64,128]{2,1,0:T(8,128)} %copy-done.8) | copy-start | bytes 4915204
  65.0 0.9 %copy-start.11 = (f32[6,64,128]{2,1,0:T(8,128)S(1)}, f32[6,64,128]{2,1,0:T(8,128)}, u32[]{:S(2)}) copy-start(f32[6,64,128]{2,1,0:T(8,128)} %copy-done.10) | copy-start | bytes 589828
  66.0 0.8 copy-start.14
  66.7 1.0 %copy-start.16 = (f32[4,80,256]{2,1,0:T(8,128)S(1)}, f32[4,80,256]{2,1,0:T(8,128)}, u32[]{:S(2)}) copy-start(f32[4,80,256]{2,1,0:T(8,128)} %copy-done.15) | copy-start | bytes 983044
  67.7 0.8 copy-start.18
  68.4 1.0 %copy-start.20 = (f32[2,136,256]{2,1,0:T(8,128)S(1)}, f32[2,136,256]{2,1,0:T(8,128)}, u32[]{:S(2)}) copy-start(f32[2,136,256]{2,1,0:T(8,128)} %copy-done.19) | copy-start | bytes 835588
  69.4 0.8 copy-start.26
  70.2 0.8 copy-start.29
  70.9 0.9 %copy-start.32 = (f32[80,256]{1,0:T(8,128)S(1)}, f32[80,256]{1,0:T(8,128)}, u32[]{:S(2)}) copy-start(f32[80,256]{1,0:T(8,128)} %copy-done.31) | copy-start | bytes 245764

commit v2 on v1

v2 whole, which is shorter than its diff:
```python
import jax
import jax.numpy as jnp
from jax import lax
from jax.experimental import pallas as pl
from jax.experimental.pallas import tpu as pltpu
from jax.sharding import PartitionSpec as P

WIDE = 6
PAD = 8
SHIFTS = (1.0, 0.3, 1.7)
PARTS = 5
LANES = 128
BOTH = ("lat", "lon")
VMEM_BYTES = 32 * 1024 * 1024

DEPTH_AT, STORE_AT, SOURCE_AT, STRIP_AT, DIFF_AT = 100, 106, 112, 118, 124
LEVEL_ROWS = 56
RAW_AT = 3 * PAD
PAIR_AT = RAW_AT + LEVEL_ROWS
MESSAGE_ROWS = PAIR_AT + LEVEL_ROWS


def iota(shape, dim):
    return lax.broadcasted_iota(jnp.int32, shape, dim)


def turn(values, shift, dim):
    return pltpu.roll(values, shift % values.shape[dim], dim)


def pack_kernel(
    east_in, north_in, tracer_in, depth_in, storage_in, surf_in, diff_in, spin_in,
    message_0, message_1, planes, rows_out, edges, east, north, tracer,
    depth, surf, px, py, bounds, field_sems, plane_sems,
):
    levels, rows, lanes = east.shape
    size = levels // PARTS
    sources, fields = (east_in, north_in, tracer_in), (east, north, tracer)

    def part_copy(number, part):
        place = pl.ds(part * size, size)
        return pltpu.make_async_copy(
            sources[number].at[place], fields[number].at[place], field_sems.at[number, part]
        )

    moves = [
        pltpu.make_async_copy(source, target, plane_sems.at[number])
        for number, (source, target) in enumerate(
            (
                (depth_in, depth), (storage_in, planes.at[1]), (surf_in, surf),
                (diff_in, planes.at[2]), (spin_in, planes.at[4]),
            )
        )
    ]
    for move in moves:
        move.start()
    for part in range(PARTS):
        for number in range(3):
            part_copy(number, part).start()
    rows_out[:, levels - levels % PAD :] = jnp.zeros((6, rows - levels + levels % PAD, lanes), jnp.float32)
    px[...] = jnp.zeros((rows, lanes), jnp.float32)
    py[...] = jnp.zeros((rows, lanes), jnp.float32)
    edges[...] = jnp.zeros((3, rows, lanes), jnp.float32)
    for move in moves:
        move.wait()
    lane = iota((rows, lanes), 1)
    row = iota((rows, lanes), 0)
    deep = depth[...].astype(jnp.float32)
    planes[0] = deep
    bounds[0] = jnp.where(lane == lanes - 1, 0.0, jnp.minimum(deep, turn(deep, -1, 1)))
    bounds[1] = jnp.where(row == rows - 1, 0.0, jnp.minimum(deep, turn(deep, -1, 0)))
    pair_lane = lax.shift_right_logical(iota((PAD, lanes), 1), 1)

    def part_step(part, carry):
        for number in range(3):
            part_copy(number, part).wait()
        for t in range(size):
            level = part * size + t
            for number, ref in enumerate(fields):
                rows_out[number, pl.ds(level, 1), :] = ref[level, rows - 1 : rows, :]
                rows_out[3 + number, pl.ds(level, 1), :] = ref[level, 0:1, :]
        for tile in range(rows // PAD):
            place = slice(tile * PAD, (tile + 1) * PAD)
            sum_x, sum_y = px[place], py[place]
            limit_x, limit_y = bounds[0, place], bounds[1, place]
            ends = [edges[number, place] for number in range(3)]
            for t in range(size):
                level = part * size + t
                height = level.astype(jnp.float32)
                here = pair_lane == level
                values = [ref[level, place] for ref in fields]
                for number in range(3):
                    moved = pltpu.roll(values[number], 2 * level + 1, 1)
                    ends[number] = jnp.where(here, moved, ends[number])
                sum_x = sum_x + jnp.where(height < limit_x, values[0], 0.0)
                sum_y = sum_y + jnp.where(height < limit_y, values[1], 0.0)
            px[place], py[place] = sum_x, sum_y
            for number in range(3):
                edges[number, place] = ends[number]
        return carry

    lax.fori_loop(0, PARTS, part_step, 0)
    plane = surf[...] + px[...] - turn(px[...], 1, 1) + py[...] - turn(py[...], 1, 0)
    planes[3] = plane
    odd_lane = lax.rem(lane, 2) == 1

    def put(target, values, start, place, count):
        moved = turn(values, place - start, 1)
        return jnp.where((lane >= place) & (lane < place + count), moved, target)

    def fill(ref, eastward):
        if eastward:
            ref[:, :lanes] = jnp.where(odd_lane, turn(edges[1], 1, 1), edges[0])
        else:
            ref[:, :lanes] = jnp.where(odd_lane, edges[0], turn(edges[1], -1, 1))
        start = lanes - WIDE if eastward else 0
        tile = edges[2]
        for values, place in (
            (deep, DEPTH_AT), (planes[1], STORE_AT), (plane, SOURCE_AT), (rows_out[1], STRIP_AT)
        ):
            tile = put(tile, values, start, place, WIDE)
        ref[:, lanes:] = put(tile, planes[2], lanes - 1, DIFF_AT, 1)

    even = lax.rem(lax.axis_index("lon"), 2) == 0

    @pl.when(even)
    def _():
        fill(message_0, True)
        fill(message_1, False)

    @pl.when(jnp.logical_not(even))
    def _():
        fill(message_0, False)
        fill(message_1, True)


def received(got_0, got_1):
    even = lax.rem(lax.axis_index("lon"), 2) == 0
    one, two = got_0[...], got_1[...]
    return jnp.where(even, two, one), jnp.where(even, one, two)


def stitch_kernel(
    got_0, got_1, planes, rows_in, edges,
    wide, face_west, message_a, message_b,
):
    rows, lanes = planes.shape[1:]
    from_west, from_east = received(got_0, got_1)
    lane = iota((rows, lanes), 1)
    left_tile, right_tile = from_west[:, lanes:], from_east[:, lanes:]

    def side(place):
        right = turn(right_tile, -place, 1)
        left = turn(left_tile, lanes - WIDE - place, 1)
        return jnp.where(lane < WIDE, right, jnp.where(lane >= lanes - WIDE, left, 0.0))

    deep, deep_side = planes[0], side(DEPTH_AT)
    store, store_side = planes[1], side(STORE_AT)
    plane, plane_side = planes[3], side(SOURCE_AT)
    strip = side(STRIP_AT)
    level = lax.shift_right_logical(lane, 1).astype(jnp.float32)
    even_lane = lax.rem(lane, 2) == 0

    def flux(values, bound):
        used = even_lane & (level < bound)
        return jnp.sum(jnp.where(used, values, 0.0), axis=1, keepdims=True)

    flux_east = flux(edges[0], jnp.minimum(deep[:, lanes - 1 :], deep_side[:, 0:1]))
    flux_west = flux(from_west[:, :lanes], jnp.minimum(deep_side[:, lanes - 1 :], deep[:, 0:1]))
    first, last = lane == 0, lane == lanes - 1
    plane = plane + jnp.where(last, flux_east, 0.0) - jnp.where(first, flux_west, 0.0)
    plane_side = plane_side - jnp.where(first, flux_east, 0.0) + jnp.where(last, flux_west, 0.0)
    both = ((deep, deep_side), (store, store_side), (plane, plane_side), (rows_in[1], strip))
    for number, (one, two) in enumerate(both):
        wide[number, :, :lanes] = one
        wide[number, :, lanes:] = two
    faces = planes[2]
    face_west[...] = jnp.where(first, turn(left_tile, -DIFF_AT, 1), turn(faces, 1, 1))

    def fill(ref, up):
        start = rows - PAD if up else 0
        for number, (one, two) in enumerate(both[:3]):
            ref[number * PAD : (number + 1) * PAD, :lanes] = one[start : start + PAD]
            ref[number * PAD : (number + 1) * PAD, lanes:] = two[start : start + PAD]
        base = 0 if up else 3
        ref[RAW_AT:PAIR_AT, :lanes] = rows_in[base + 1, :LEVEL_ROWS]
        ref[RAW_AT:PAIR_AT, lanes:] = strip[:LEVEL_ROWS]
        ref[PAIR_AT:, :lanes] = rows_in[base, :LEVEL_ROWS]
        ref[PAIR_AT:, lanes:] = rows_in[base + 2, :LEVEL_ROWS]
        if up:
            ref[PAIR_AT - 1 : PAIR_AT, :lanes] = faces[rows - 1 :]

    even = lax.rem(lax.axis_index("lat"), 2) == 0

    @pl.when(even)
    def _():
        fill(message_a, True)
        fill(message_b, False)

    @pl.when(jnp.logical_not(even))
    def _():
        fill(message_a, False)
        fill(message_b, True)


def level_kernel(
    got_0, got_1, wide, planes, face_west, edges, east, north, tracer,
    east_out, north_out, tracer_out,
    bounds, sides,
):
    levels, rows, lanes = east.shape
    from_west, from_east = received(got_0, got_1)
    lane = iota((rows, lanes), 1)
    row = iota((rows, lanes), 0)
    deep, beside = wide[0, :, :lanes], wide[0, :, lanes:]
    bounds[0] = jnp.where(lane == lanes - 1, 0.0, jnp.minimum(deep, turn(deep, -1, 1)))
    bounds[1] = jnp.where(row == rows - 1, 0.0, jnp.minimum(deep, turn(deep, -1, 0)))
    level = lax.shift_right_logical(lane, 1).astype(jnp.float32)
    odd_lane = lax.rem(lane, 2) == 1
    bound_east = jnp.minimum(deep[:, lanes - 1 :], beside[:, 0:1])
    bound_west = jnp.minimum(deep[:, 0:1], beside[:, lanes - 1 :])
    weight_east, weight_west = planes[2, :, lanes - 1 :], face_west[:, 0:1]
    weight = jnp.where(odd_lane, weight_west, weight_east)
    weight = jnp.where(level < jnp.where(odd_lane, bound_west, bound_east), weight, 0.0)
    halos = (
        jnp.where(odd_lane, turn(from_west[:, :lanes], 1, 1), turn(from_east[:, :lanes], -1, 1)),
        jnp.where(odd_lane, from_west[:, :lanes], from_east[:, :lanes]),
        jnp.where(odd_lane, turn(from_west[:, lanes:], 1, 1), turn(from_east[:, lanes:], -1, 1)),
    )
    for number in range(3):
        sides[number] = weight * (halos[number] - edges[number])
    small_lane, line = iota((PAD, lanes), 1), iota((PAD, lanes), 0)
    rim = (small_lane == 0) | (small_lane == lanes - 1)
    first_line, last_line = line == 0, line == PAD - 1
    fields, outs = (east, north, tracer), (east_out, north_out, tracer_out)
    tiles = rows // PAD

    def level_step(level, carry):
        height = level.astype(jnp.float32)
        values = [ref[level, :PAD] for ref in fields]
        lifted = [turn(item, -1, 0) for item in values]
        below = [jnp.zeros((PAD, lanes), jnp.float32)] * 3
        for tile in range(tiles):
            place = slice(tile * PAD, (tile + 1) * PAD)
            wet = height < planes[0, place]
            face = planes[2, place]
            face_east = jnp.where(height < bounds[0, place], face, 0.0)
            face_north = jnp.where(height < bounds[1, place], face, 0.0)
            results = []
            for number in range(3):
                item = values[number]
                flux = face_east * (item - turn(item, -1, 1))
                if tile + 1 < tiles:
                    upper = fields[number][level, (tile + 1) * PAD : (tile + 2) * PAD]
                    upper_lifted = turn(upper, -1, 0)
                    above = jnp.where(last_line, upper_lifted, lifted[number])
                else:
                    upper, upper_lifted, above = item, lifted[number], lifted[number]
                rise = face_north * (item - above)
                moved = turn(rise, 1, 0)
                fall = jnp.where(first_line, below[number], moved)
                rim_part = pltpu.roll(sides[number, place], lanes - 1 - 2 * level + lanes, 1)
                result = jnp.where(wet, item, 0.0) + jnp.where(rim, rim_part, 0.0)
                results.append(result + (turn(flux, 1, 1) - flux) + (fall - rise))
                below[number] = moved
                values[number], lifted[number] = upper, upper_lifted
                if number < 2:
                    results.append(item)
            spin = jnp.where(wet, planes[4, place], 0.0)
            east_out[level, place] = results[0] - spin * results[3]
            north_out[level, place] = results[2] + spin * results[1]
            tracer_out[level, place] = results[4]
        return carry

    lax.fori_loop(0, levels, level_step, 0, unroll=2)


def shifted(values):
    return turn(values, -1, 1), turn(values, 1, 1), turn(values, -1, 0), turn(values, 1, 0)


def basis_kernel(thickness, got_a, got_b, wide, gram, basis, depth_wide, halo):
    rows, lanes = wide.shape[1], wide.shape[2] // 2
    lat = lax.axis_index("lat")
    even = lax.rem(lat, 2) == 0
    at_top = lat == lax.axis_size("lat") - 1
    at_bottom = lat == 0

    @pl.when(at_top)
    def _():
        back = lanes - 1 - iota((PAD, lanes), 1)
        for number in range(MESSAGE_ROWS // PAD):
            for tile in range(2):
                values = got_b[number * PAD : (number + 1) * PAD, tile * lanes : (tile + 1) * lanes]
                values = jnp.take_along_axis(values, back, axis=1)
                if number < 3:
                    values = jnp.concatenate(
                        [values[i : i + 1] for i in range(PAD - 1, -1, -1)], axis=0
                    )
                halo[0, number * PAD : (number + 1) * PAD, tile * lanes : (tile + 1) * lanes] = values

    @pl.when(jnp.logical_not(at_top))
    def _():
        halo[0] = jnp.where(even, got_a[...], got_b[...])

    halo[1] = jnp.where(at_bottom, 0.0, jnp.where(even, got_b[...], got_a[...]))

    def whole(number):
        place = slice(number * PAD, (number + 1) * PAD)
        return jnp.concatenate([halo[1, place], wide[number], halo[0, place]], axis=0)

    deep, store, plane = whole(0), whole(1), whole(2)
    depth_wide[...] = deep
    full = deep.shape
    row = iota(full, 0)
    core_end = PAD + rows
    level = iota((LEVEL_ROWS, full[1]), 0).astype(jnp.float32)
    bound = jnp.minimum(deep[core_end - 1 : core_end], deep[core_end : core_end + 1])
    edge = wide[3, :LEVEL_ROWS] - jnp.where(at_top, halo[0, RAW_AT:PAIR_AT], 0.0)
    flux = jnp.sum(jnp.where(level < bound, edge, 0.0), axis=0, keepdims=True)
    plane = plane + jnp.where(row == core_end - 1, flux, 0.0) - jnp.where(row == core_end, flux, 0.0)
    bound = jnp.minimum(deep[PAD - 1 : PAD], deep[PAD : PAD + 1])
    flux = jnp.sum(jnp.where(level < bound, halo[1, RAW_AT:PAIR_AT], 0.0), axis=0, keepdims=True)
    plane = plane + jnp.where(row == PAD - 1, flux, 0.0) - jnp.where(row == PAD, flux, 0.0)

    place = iota((PAD, lanes), 1)
    table = jnp.zeros((PAD, lanes), jnp.float32)
    for number in range(thickness.shape[0]):
        table = table + jnp.where(place > number, thickness[number], 0.0)

    def column(bound):
        index = bound.astype(jnp.int32)
        return jnp.concatenate(
            [
                jnp.concatenate(
                    [
                        jnp.take_along_axis(
                            table, index[i : i + PAD, j : j + lanes], axis=1
                        )
                        for j in range(0, full[1], lanes)
                    ],
                    axis=1,
                )
                for i in range(0, full[0], PAD)
            ],
            axis=0,
        )

    beside, _, above, _ = shifted(deep)
    to_east = column(jnp.minimum(deep, beside))
    to_north = column(jnp.minimum(deep, above))
    to_north = jnp.where(at_top & (row == core_end - 1), 2.0, 1.0) * to_north
    to_west, to_south = turn(to_east, 1, 1), turn(to_north, 1, 0)
    diag = store + to_east + to_west + to_north + to_south
    there = diag > 0.0
    inverse = jnp.where(there, 1.0 / jnp.where(there, diag, 1.0), 0.0)

    def operate(values):
        east_side, west_side, north_side, south_side = shifted(values)
        total = (
            store * values + to_east * (values - east_side) + to_west * (values - west_side)
        )
        return total + to_north * (values - north_side) + to_south * (values - south_side)

    vectors, images = [plane * inverse], []
    for number in range(4):
        images.append(operate(vectors[-1]))
        if number < 3:
            vectors.append(images[-1] * inverse - SHIFTS[number] * vectors[-1])
    for number in range(4):
        basis[number] = vectors[number]

    def core(values):
        return values[PAD:core_end, :lanes]

    sums = []
    for i in range(4):
        for j in range(i, 4):
            sums.append(core(vectors[i]) * core(images[j]))
    for i in range(4):
        sums.append(core(vectors[i]) * core(plane))
    sums = [jnp.sum(item, axis=0, keepdims=True) for item in sums]
    sums = sums + [jnp.zeros((1, lanes), jnp.float32)] * (16 - len(sums))
    sums = jnp.sum(jnp.concatenate(sums, axis=0), axis=1, keepdims=True)
    same = iota((16, lanes), 0) == iota((16, lanes), 1)
    line = jnp.sum(jnp.where(same, sums, 0.0), axis=0, keepdims=True)
    gram[...] = jnp.broadcast_to(line, gram.shape)


def solve(line):
    entry = [line[:, i : i + 1] for i in range(14)]
    system = [[None] * 5 for _ in range(4)]
    for i in range(4):
        for j in range(i, 4):
            system[i][j] = entry.pop(0)
    for i in range(4):
        system[i][4] = entry.pop(0)
    factor, part = {}, []
    for k in range(4):
        pivot = system[k][k]
        usable = pivot > 0.0
        scale = jnp.where(usable, 1.0 / jnp.where(usable, pivot, 1.0), 0.0)
        part.append(system[k][4] * scale)
        for i in range(k + 1, 4):
            factor[i, k] = system[k][i] * scale
            for j in range(i, 5):
                system[i][j] = system[i][j] - factor[i, k] * system[k][j]
    for k in range(2, -1, -1):
        for i in range(k + 1, 4):
            part[k] = part[k] - factor[i, k] * part[i]
    return part


def final_kernel(
    thickness, totals, basis, depth_wide, planes_in, face_west, halo, rows_in,
    east, north, tracer_in,
    tracer_hbm, east_hbm, north_hbm, surface,
    planes, fixes, tracer, east_out, north_out, sems, tracer_sem,
):
    levels, rows, lanes = east.shape
    size = levels // PARTS
    core_end = PAD + rows
    outs = ((east_out, east_hbm), (north_out, north_hbm))

    def part_copy(number, part):
        place = pl.ds(part * size, size)
        source, target = outs[number]
        return pltpu.make_async_copy(source.at[place], target.at[place], sems.at[number, part])

    tracer_copy = pltpu.make_async_copy(tracer, tracer_hbm, tracer_sem)
    at_top = lax.axis_index("lat") == lax.axis_size("lat") - 1
    row = iota((rows, lanes), 0)
    deep = depth_wide[...]
    bounds = [jnp.minimum(deep, item)[PAD:core_end, :lanes] for item in shifted(deep)]
    face = planes_in[2]
    north_face = face + jnp.where(
        at_top & (row == rows - 1), halo[0, PAIR_AT - 1 : PAIR_AT, :lanes], 0.0
    )
    south_face = jnp.where(row == 0, halo[1, PAIR_AT - 1 : PAIR_AT, :lanes], turn(face, 1, 0))
    faces = (face, face_west[...], north_face, south_face)
    planes[0] = deep[PAD:core_end, :lanes]
    for number in range(4):
        planes[1 + number] = bounds[number]
    level = iota((LEVEL_ROWS, lanes), 0).astype(jnp.float32)
    for side, line in ((0, rows - 1), (1, 0)):
        bound = bounds[2 + side][line : line + 1]
        weight = faces[2 + side][line : line + 1]
        outer = (
            halo[side, PAIR_AT:, :lanes],
            halo[side, RAW_AT:PAIR_AT, :lanes],
            halo[side, PAIR_AT:, lanes:],
        )
        for number in range(3):
            inner = rows_in[3 * side + number, :LEVEL_ROWS]
            fixes[3 * side + number] = jnp.where(
                level < bound, weight * (outer[number] - inner), 0.0
            )
    parts = solve(jnp.sum(totals[...], axis=0, keepdims=True))
    height = parts[0] * basis[0]
    for number in range(1, 4):
        height = height + parts[number] * basis[number]
    surface[...] = planes_in[1] * height[PAD:core_end, :lanes]
    full_row = iota(height.shape, 0)
    folded = at_top & (full_row == core_end)
    to_east, to_west, to_north, to_south = shifted(height)
    slope_x = jnp.where(folded, to_west, to_east) - height
    slope_y = jnp.where(folded, to_south, to_north) - height
    inner_x, inner_y = slope_x[PAD:core_end, :lanes], slope_y[PAD:core_end, :lanes]
    spin = planes_in[4]
    planes[5] = inner_x - spin * inner_y
    planes[6] = inner_y + spin * inner_x
    for start, slope, inner in ((7, slope_x, inner_x), (11, slope_y, inner_y)):
        for number, item in enumerate(shifted(slope)):
            planes[start + number] = faces[number] * (inner - item[PAD:core_end, :lanes])

    line = iota((PAD, lanes), 0)
    first_line, last_line = line == 0, line == PAD - 1

    def part_step(part, carry):
        for tile in range(rows // PAD):
            place = slice(tile * PAD, (tile + 1) * PAD)
            own = [planes[number, place] for number in range(15)]
            for t in range(size):
                level = part * size + t
                height = level.astype(jnp.float32)
                open_sides = [height < own[number] for number in range(5)]
                for out, values, base, start, number in (
                    (east_out, east, 5, 7, 0), (north_out, north, 6, 11, 1)
                ):
                    change = jnp.where(open_sides[0], own[base], 0.0)
                    for side in range(4):
                        change = change - jnp.where(open_sides[1 + side], own[start + side], 0.0)
                    result = values[level, place] + thickness[level] * change
                    if tile == 0:
                        fix = fixes[3 + number, pl.ds(level, 1), :]
                        result = result + jnp.where(first_line, fix, 0.0)
                    if tile == rows // PAD - 1:
                        fix = fixes[number, pl.ds(level, 1), :]
                        result = result + jnp.where(last_line, fix, 0.0)
                    out[level, place] = result
        part_copy(0, part).start()
        part_copy(1, part).start()
        return carry

    def tracer_step(level, carry):
        for tile in range(rows // PAD):
            place = slice(tile * PAD, (tile + 1) * PAD)
            result = tracer_in[level, place]
            if tile == 0:
                result = result + jnp.where(first_line, fixes[5, pl.ds(level, 1), :], 0.0)
            if tile == rows // PAD - 1:
                result = result + jnp.where(last_line, fixes[2, pl.ds(level, 1), :], 0.0)
            tracer[level, place] = result
        return carry

    lax.fori_loop(0, levels, tracer_step, 0, unroll=5)
    tracer_copy.start()
    lax.fori_loop(0, PARTS, part_step, 0)
    tracer_copy.wait()
    for part in range(PARTS):
        part_copy(0, part).wait()
        part_copy(1, part).wait()


def swaps(lats, lons, odd):
    pairs = []
    for lat in range(lats):
        for lon in range(lons):
            other = lat + 1 if lat % 2 == odd else lat - 1
            if other < 0:
                continue
            if other == lats:
                pairs.append((lat * lons + lon, lat * lons + lons - 1 - lon))
            else:
                pairs.append((lat * lons + lon, other * lons + lon))
    return pairs


def lon_swaps(lons, odd):
    return [(lon, (lon + (1 if lon % 2 == odd else -1)) % lons) for lon in range(lons)]


def local(
    tracer_cot, east_cot, north_cot, surface_cot, depth_levels, diffusivity, coriolis, storage,
    thickness,
):
    levels, rows, lanes = tracer_cot.shape
    lats, lons = lax.axis_size("lat"), lax.axis_size("lon")
    far = lambda value: pltpu.with_memory_space_constraint(value, pltpu.HBM)
    near = lambda value: pltpu.with_memory_space_constraint(value, pltpu.VMEM)
    floats = lambda *shape: pltpu.HBM(shape, jnp.float32)
    scratch = lambda *shape: pltpu.VMEM(shape, jnp.float32)
    scalars = pl.BlockSpec(memory_space=pltpu.SMEM)
    in_hbm = pl.BlockSpec(memory_space=pltpu.HBM)
    in_vmem = pl.BlockSpec(memory_space=pltpu.VMEM)
    params = pltpu.CompilerParams(vmem_limit_bytes=VMEM_BYTES)
    plane, pair, field = (rows, lanes), (rows, 2 * lanes), (levels, rows, lanes)
    full = (rows + 2 * PAD, 2 * lanes)
    message = (MESSAGE_ROWS, 2 * lanes)

    message_0, message_1, planes, edge_rows, edges, east, north, tracer = pl.pallas_call(
        pack_kernel,
        in_specs=[in_hbm] * 8,
        out_specs=[in_vmem] * 8,
        out_shape=[
            scratch(*pair), scratch(*pair), scratch(5, *plane), scratch(6, *plane),
            scratch(3, *plane), scratch(*field), scratch(*field), scratch(*field),
        ],
        scratch_shapes=[
            pltpu.VMEM(plane, jnp.int32), scratch(*plane), scratch(*plane), scratch(*plane),
            scratch(2, *plane), pltpu.SemaphoreType.DMA((3, PARTS)), pltpu.SemaphoreType.DMA((5,)),
        ],
        compiler_params=params,
        name="pack",
    )(
        *[
            far(item)
            for item in (
                east_cot, north_cot, tracer_cot, depth_levels, storage, surface_cot, diffusivity,
                coriolis,
            )
        ]
    )

    got_1 = near(lax.ppermute(message_1, "lon", lon_swaps(lons, 1)))
    got_0 = near(lax.ppermute(message_0, "lon", lon_swaps(lons, 0)))

    wide, face_west, message_a, message_b = pl.pallas_call(
        stitch_kernel,
        in_specs=[in_vmem] * 5,
        out_specs=[in_vmem] * 4,
        out_shape=[scratch(4, *pair), scratch(*plane), scratch(*message), scratch(*message)],
        compiler_params=params,
        name="stitch",
    )(got_0, got_1, near(planes), near(edge_rows), near(edges))

    got_b = lax.ppermute(message_b, BOTH, swaps(lats, lons, 1))
    got_a = lax.ppermute(message_a, BOTH, swaps(lats, lons, 0))

    east_part, north_part, tracer_part = pl.pallas_call(
        level_kernel,
        in_specs=[in_vmem] * 9,
        out_specs=[in_vmem] * 3,
        out_shape=[scratch(*field)] * 3,
        scratch_shapes=[scratch(2, *plane), scratch(3, *plane)],
        compiler_params=params,
        cost_estimate=pl.CostEstimate(
            flops=60 * levels * rows * lanes, bytes_accessed=24 * levels * rows * lanes,
            transcendentals=0,
        ),
        name="level",
    )(
        got_0, got_1, near(wide), near(planes), near(face_west), near(edges), near(east),
        near(north), near(tracer),
    )

    wide, east_part = lax.optimization_barrier((wide, east_part))
    gram, basis, depth_wide, halo = pl.pallas_call(
        basis_kernel,
        in_specs=[scalars] + [in_vmem] * 3,
        out_specs=[in_vmem] * 4,
        out_shape=[
            scratch(lats * lons, lanes), scratch(4, *full), scratch(*full), scratch(2, *message)
        ],
        compiler_params=params,
        name="basis",
    )(thickness, near(got_a), near(got_b), near(wide))

    totals = lax.all_to_all(gram, BOTH, 0, 0, tiled=True)

    tracer_adj, east_adj, north_adj, surface_adj = pl.pallas_call(
        final_kernel,
        in_specs=[scalars] + [in_vmem] * 10,
        out_specs=[in_hbm] * 3 + [in_vmem],
        out_shape=[floats(*field)] * 3 + [jax.ShapeDtypeStruct(plane, jnp.float32)],
        scratch_shapes=[
            scratch(15, *plane), scratch(6, LEVEL_ROWS, lanes), scratch(*field), scratch(*field),
            scratch(*field), pltpu.SemaphoreType.DMA((2, PARTS)), pltpu.SemaphoreType.DMA,
        ],
        compiler_params=params,
        name="final",
    )(
        thickness, near(totals), near(basis), near(depth_wide), near(planes), near(face_west),
        near(halo), near(edge_rows), near(east_part), near(north_part), near(tracer_part),
    )
    return tracer_adj, east_adj, north_adj, surface_adj


def solution(mesh):
    field, plane = P(None, "lat", "lon"), P("lat", "lon")
    return jax.shard_map(
        local,
        mesh=mesh,
        in_specs=(field, field, field, plane, plane, plane, plane, plane, P()),
        out_specs=(field, field, field, plane),
        check_vma=False,
    )
```

time: 79.8 us -> 54.9 us (0.69); the launches traced: 78.4 us -> 54.8 us
  local copies, waits for them, and re-layouts: 28 us -> 0.01 us
  blocking collectives: 0 us -> 25.9 us
  starting transfers between devices: 23.1 us -> 4.9 us
  waiting for transfers between devices: 7.62 us -> 2.34 us
  Pallas kernels: 19 us -> 20.9 us
    unnamed x72 -> x2, local copies, waits for them, and re-layouts: 28 us -> 0.01 us
    all_to_all x0 -> x1, blocking collectives: none -> 25.9 us  [local(): totals = lax.all_to_all(gram, BOTH, 0, 0, tiled=True)]
    all_to_all x1 -> x0, starting transfers between devices: 19.2 us -> none  [local(): totals = lax.all_to_all(gram, BOTH, 0, 0, tiled=True)]
    ppermute x1, waiting for transfers between devices: 3.22 us -> 0.01 us  [local(): got_a = lax.ppermute(message_a, BOTH, swaps(lats, lons, 0))]
    ppermute x2, waiting for transfers between devices: 4.39 us -> 2.33 us  [the longest x1 2.33 us: local(): got_1 = near(lax.ppermute(message_1, 'lon', lon_swaps(lons, 1)))]
    pallas_call x5, Pallas kernels: 19 us -> 20.9 us  [the longest x1 8.36 us: local(): pl.pallas_call(level_kernel, in_specs=[in_vmem] * 9, out_specs=[in_vmem]...]
    ppermute x1, starting transfers between devices: 0.32 us -> 1.39 us  [local(): got_a = lax.ppermute(message_a, BOTH, swaps(lats, lons, 0))]
  transfers between devices with their start and end apart: 5 -> 4, of which waited for: 3 -> 1; matrix products, arithmetic and copies ran while one was open for 0% -> 0% of each run, Pallas kernels for 9% -> 15%
where the time goes in v2:
time: 54.9 us; the launch traced here: 54.8 us
  blocking collectives  25.9 us (47%)
  Pallas kernels  20.9 us (38%)
  starting transfers between devices  4.9 us (9%)
  waiting for transfers between devices  2.34 us (4%)
  between operations  0.7 us (1%)
    all_to_all x1, blocking collectives, local(): totals = lax.all_to_all(gram, BOTH, 0, 0, tiled=True)  25.9 us
    pallas_call x1, Pallas kernels, local(): pl.pallas_call(level_kernel, in_specs=[in_vmem] * 9, out_specs=[in_vmem]...  8.36 us
    pallas_call x1, Pallas kernels, local(): pl.pallas_call(final_kernel, in_specs=[scalars] + [in_vmem] * 10, out_spe...  6.55 us
    pallas_call x1, Pallas kernels, local(): pl.pallas_call(pack_kernel, in_specs=[in_hbm] * 8, out_specs=[in_vmem] *...  4.4 us
    ppermute x1, waiting for transfers between devices, local(): got_1 = near(lax.ppermute(message_1, 'lon', lon_swaps(lons, 1)))  2.33 us
    ppermute x1, starting transfers between devices, local(): got_0 = near(lax.ppermute(message_0, 'lon', lon_swaps(lons, 0)))  1.5 us
    ppermute x1, starting transfers between devices, local(): got_a = lax.ppermute(message_a, BOTH, swaps(lats, lons, 0))  1.39 us
    ppermute x1, starting transfers between devices, local(): got_1 = near(lax.ppermute(message_1, 'lon', lon_swaps(lons, 1)))  1.36 us
  transfers between devices with their start and end apart: 4, of which 1 were waited for; matrix products, arithmetic and copies ran while one was open for 0% of the time, Pallas kernels for 15%

profile of v2, /device:TPU:1, one launch (start us, length us, event | category | flops | bytes accessed | tf_op | source)
XLA Modules:
  0.0 54.8 jit_solution(3965104035844379638)
XLA Ops:
  0.6 4.4 %pack.1 = (f32[64,256]{1,0:T(8,128)S(1)}, f32[64,256]{1,0:T(8,128)S(1)}, f32[5,64,128]{2,1,0:T(8,128)S(1)}, f32[6,64,128]{2,1,0:T(8,128)S(1)}, f32[3,64,128]{2,1...) custom-call(f32[50,64,128]{2,1,0:T(8,128)} %east_in.1, ...), custom_call_target="tpu_custom_call" | custom-call | tf_op jit(solution)/shard_map/pack/pallas_call | solution.py:561
  5.0 1.5 %collective-permute-start = (f32[64,256]{1,0:T(8,128)S(1)}, f32[64,256]{1,0:T(8,128)S(1)}, u32[]{:S(2)}, u32[]{:S(2)}) collective-permute-start(f32[64,256]{1,0:T(8,128)S(1)} %get-tuple-element.25), channel_id=1, source_target_pairs={{0,1},{1,0},{2,3},{3,2},{4,5},{5,4},{6,7},{7,6},{8,9},{9,8},{10,11... | collective-permute-start | bytes 196616 | tf_op jit(solution)/shard_map/ppermute | solution.py:586
  6.5 1.4 %collective-permute-start.1 = (f32[64,256]{1,0:T(8,128)S(1)}, f32[64,256]{1,0:T(8,128)S(1)}, u32[]{:S(2)}, u32[]{:S(2)}) collective-permute-start(f32[64,256]{1,0:T(8,128)S(1)} %get-tuple-element.26), channel_id=1, source_target_pairs={{0,15},{1,2},{2,1},{3,4},{4,3},{5,6},{6,5},{7,8},{8,7},{9,10},{10,... | collective-permute-start | bytes 196616 | tf_op jit(solution)/shard_map/ppermute | solution.py:585
  7.9 0.0 collective-permute-done.got_0
  7.9 2.3 %collective-permute-done.1.got_1 = f32[64,256]{1,0:T(8,128)S(1)} collective-permute-done((f32[64,256]{1,0:T(8,128)S(1)}, f32[64,256]{1,0:T(8,128)S(1)}, u32[]{:S(2)}, u32[]{:S(2)}) %collective-permute-start.1) | collective-permute-done | bytes 65568 | tf_op jit(solution)/shard_map/ppermute | solution.py:585
  10.2 0.3 stitch.1
  10.6 1.4 %collective-permute-start.2 = (f32[136,256]{1,0:T(8,128)S(1)}, f32[136,256]{1,0:T(8,128)S(1)}, u32[]{:S(2)}, u32[]{:S(2)}) collective-permute-start(f32[136,256]{1,0:T(8,128)S(1)} %get-tuple-element.30), channel_id=1, source_target_pairs={{0,16},{1,17},{2,18},{3,19},{4,20},{5,21},{6,22},{7,23},{8,24},{9,... | collective-permute-start | bytes 417800 | tf_op jit(solution)/shard_map/ppermute | solution.py:598
  12.0 0.7 %collective-permute-start.3 = (f32[136,256]{1,0:T(8,128)S(1)}, f32[136,256]{1,0:T(8,128)S(1)}, u32[]{:S(2)}, u32[]{:S(2)}) collective-permute-start(f32[136,256]{1,0:T(8,128)S(1)} %get-tuple-element.31), channel_id=1, source_target_pairs={{16,32},{17,33},{18,34},{19,35},{20,36},{21,37},{22,38},{23,39},{2... | collective-permute-start | bytes 417800 | tf_op jit(solution)/shard_map/ppermute | solution.py:597
  12.6 0.0 copy-start
  12.6 8.4 %level.1 = (f32[50,64,128]{2,1,0:T(8,128)S(1)}, f32[50,64,128]{2,1,0:T(8,128)S(1)}, f32[50,64,128]{2,1,0:T(8,128)S(1)}) custom-call(f32[64,256]{1,0:T(8,128)S(1)} %collective-permute-done.got_0, f32[64,256]{1,0:T(8,128)S(1)} %collective-permute-done.1.got_1, f32[4,64,256]{2,1,0:T(8,128)S(1)} %get-tuple-element.38.wide, ...), custom_call_target="tpu_custom_call" | custom-call | flops 24576000 | bytes 9830400 | tf_op jit(solution)/shard_map/level/pallas_call | solution.py:600
  21.0 0.0 collective-permute-done.2.got_a
  21.0 0.0 collective-permute-done.3.got_b
  21.0 0.0 copy-done
  21.0 1.3 %basis.1 = (f32[128,128]{1,0:T(8,128)S(1)}, f32[4,80,256]{2,1,0:T(8,128)S(1)}, f32[80,256]{1,0:T(8,128)S(1)}, f32[2,136,256]{2,1,0:T(8,128)S(1)}) custom-call(f32[50]{0:T(128)S(1)} %copy-done, f32[136,256]{1,0:T(8,128)S(1)} %collective-permute-done.2.got_a, f32[136,256]{1,0:T(8,128)S(1)} %collective-permute-done.3.got_b, ...), custom_call_target="tpu_custom_call" | custom-call | tf_op jit(solution)/shard_map/basis/pallas_call | solution.py:618
  22.3 25.9 %all_to_all.11 = f32[128,1,128]{2,1,0:T(1,128)S(1)} all-to-all(f32[128,1,128]{2,1,0:T(1,128)S(1)} %bitcast.5), channel_id=1, replica_groups=mesh['lat'=8,'lon'=16] {'lat','lon'}, dimensions={0} | all-to-all | bytes 131072 | tf_op jit(solution)/shard_map/all_to_all | solution.py:629
  48.2 6.6 %final.1 = (f32[50,64,128]{2,1,0:T(8,128)}, f32[50,64,128]{2,1,0:T(8,128)}, f32[50,64,128]{2,1,0:T(8,128)}, f32[64,128]{1,0:T(8,128)}) custom-call(f32[50]{0:T(128)S(1)} %copy-done, f32[128,128]{1,0:T(8,128)S(1)} %bitcast.4, f32[4,80,256]{2,1,0:T(8,128)S(1)} %get-tuple-element.40.basis, f32[80,256]{1,0:T(8,128)S(1)} %get-tuple-element.41.depth_wide, ...), custom_call_target="tpu_custom_call" | custom-call | tf_op jit(solution)/shard_map/final/pallas_call | solution.py:631
Async XLA Ops:
  5.0 2.9 %collective-permute-start = (f32[64,256]{1,0:T(8,128)S(1)}, f32[64,256]{1,0:T(8,128)S(1)}, u32[]{:S(2)}, u32[]{:S(2)}) collective-permute-start(f32[64,256]{1,0:T(8,128)S(1)} %get-tuple-element.25), channel_id=1, source_target_pairs={{0,1},{1,0},{2,3},{3,2},{4,5},{5,4},{6,7},{7,6},{8,9},{9,8},{10,11... | collective-permute-start | bytes 196616 | tf_op jit(solution)/shard_map/ppermute | solution.py:586
  6.5 3.7 %collective-permute-start.1 = (f32[64,256]{1,0:T(8,128)S(1)}, f32[64,256]{1,0:T(8,128)S(1)}, u32[]{:S(2)}, u32[]{:S(2)}) collective-permute-start(f32[64,256]{1,0:T(8,128)S(1)} %get-tuple-element.26), channel_id=1, source_target_pairs={{0,15},{1,2},{2,1},{3,4},{4,3},{5,6},{6,5},{7,8},{8,7},{9,10},{10,... | collective-permute-start | bytes 196616 | tf_op jit(solution)/shard_map/ppermute | solution.py:585
  10.6 10.4 %collective-permute-start.2 = (f32[136,256]{1,0:T(8,128)S(1)}, f32[136,256]{1,0:T(8,128)S(1)}, u32[]{:S(2)}, u32[]{:S(2)}) collective-permute-start(f32[136,256]{1,0:T(8,128)S(1)} %get-tuple-element.30), channel_id=1, source_target_pairs={{0,16},{1,17},{2,18},{3,19},{4,20},{5,21},{6,22},{7,23},{8,24},{9,... | collective-permute-start | bytes 417800 | tf_op jit(solution)/shard_map/ppermute | solution.py:598
  12.0 9.1 %collective-permute-start.3 = (f32[136,256]{1,0:T(8,128)S(1)}, f32[136,256]{1,0:T(8,128)S(1)}, u32[]{:S(2)}, u32[]{:S(2)}) collective-permute-start(f32[136,256]{1,0:T(8,128)S(1)} %get-tuple-element.31), channel_id=1, source_target_pairs={{16,32},{17,33},{18,34},{19,35},{20,36},{21,37},{22,38},{23,39},{2... | collective-permute-start | bytes 417800 | tf_op jit(solution)/shard_map/ppermute | solution.py:597
  12.6 8.4 %copy-start = (f32[50]{0:T(128)S(1)}, f32[50]{0:T(128)}, u32[]{:S(2)}) copy-start(f32[50]{0:T(128)} %thickness.3) | copy-start | bytes 604

commit v3 on v2

--- a/solution.py
+++ b/solution.py
@@ -9,7 +9,10 @@
 PAD = 8
 SHIFTS = (1.0, 0.3, 1.7)
 PARTS = 5
+OUT_PARTS = 10
 LANES = 128
+GROUP = 5
+TILES = 4
 BOTH = ("lat", "lon")
 VMEM_BYTES = 32 * 1024 * 1024
 
@@ -17,7 +20,10 @@
 LEVEL_ROWS = 56
 RAW_AT = 3 * PAD
 PAIR_AT = RAW_AT + LEVEL_ROWS
-MESSAGE_ROWS = PAIR_AT + LEVEL_ROWS
+HALO_ROWS = PAIR_AT + LEVEL_ROWS
+SIDES_AT = HALO_ROWS + LEVEL_ROWS
+MESSAGE_ROWS = SIDES_AT + PAD
+SIDE_GROUPS = PAIR_AT // PAD
 
 
 def iota(shape, dim):
@@ -71,14 +77,14 @@
     bounds[1] = jnp.where(row == rows - 1, 0.0, jnp.minimum(deep, turn(deep, -1, 0)))
     pair_lane = lax.shift_right_logical(iota((PAD, lanes), 1), 1)
 
-    def part_step(part, carry):
+    for part in range(PARTS):
         for number in range(3):
             part_copy(number, part).wait()
         for t in range(size):
             level = part * size + t
             for number, ref in enumerate(fields):
-                rows_out[number, pl.ds(level, 1), :] = ref[level, rows - 1 : rows, :]
-                rows_out[3 + number, pl.ds(level, 1), :] = ref[level, 0:1, :]
+                rows_out[number, level : level + 1, :] = ref[level, rows - 1 : rows, :]
+                rows_out[3 + number, level : level + 1, :] = ref[level, 0:1, :]
         for tile in range(rows // PAD):
             place = slice(tile * PAD, (tile + 1) * PAD)
             sum_x, sum_y = px[place], py[place]
@@ -86,20 +92,17 @@
             ends = [edges[number, place] for number in range(3)]
             for t in range(size):
                 level = part * size + t
-                height = level.astype(jnp.float32)
                 here = pair_lane == level
                 values = [ref[level, place] for ref in fields]
                 for number in range(3):
-                    moved = pltpu.roll(values[number], 2 * level + 1, 1)
+                    moved = turn(values[number], 2 * level + 1, 1)
                     ends[number] = jnp.where(here, moved, ends[number])
-                sum_x = sum_x + jnp.where(height < limit_x, values[0], 0.0)
-                sum_y = sum_y + jnp.where(height < limit_y, values[1], 0.0)
+                sum_x = sum_x + jnp.where(limit_x > level, values[0], 0.0)
+                sum_y = sum_y + jnp.where(limit_y > level, values[1], 0.0)
             px[place], py[place] = sum_x, sum_y
             for number in range(3):
                 edges[number, place] = ends[number]
-        return carry
-
-    lax.fori_loop(0, PARTS, part_step, 0)
+
     plane = surf[...] + px[...] - turn(px[...], 1, 1) + py[...] - turn(py[...], 1, 0)
     planes[3] = plane
     odd_lane = lax.rem(lane, 2) == 1
@@ -177,18 +180,26 @@
     faces = planes[2]
     face_west[...] = jnp.where(first, turn(left_tile, -DIFF_AT, 1), turn(faces, 1, 1))
 
+    small_lane = iota((PAD, lanes), 1)
+
     def fill(ref, up):
         start = rows - PAD if up else 0
-        for number, (one, two) in enumerate(both[:3]):
-            ref[number * PAD : (number + 1) * PAD, :lanes] = one[start : start + PAD]
-            ref[number * PAD : (number + 1) * PAD, lanes:] = two[start : start + PAD]
         base = 0 if up else 3
-        ref[RAW_AT:PAIR_AT, :lanes] = rows_in[base + 1, :LEVEL_ROWS]
-        ref[RAW_AT:PAIR_AT, lanes:] = strip[:LEVEL_ROWS]
-        ref[PAIR_AT:, :lanes] = rows_in[base, :LEVEL_ROWS]
-        ref[PAIR_AT:, lanes:] = rows_in[base + 2, :LEVEL_ROWS]
+        groups = [two[start : start + PAD] for _, two in both[:3]]
+        groups = groups + [strip[i : i + PAD] for i in range(0, LEVEL_ROWS, PAD)]
+        packed = jnp.zeros((PAD, lanes), jnp.float32)
+        for number, item in enumerate(groups):
+            place = 2 * WIDE * number
+            here = (small_lane >= place) & (small_lane < place + 2 * WIDE)
+            packed = jnp.where(here, turn(item, place + WIDE, 1), packed)
+        for number, (one, _) in enumerate(both[:3]):
+            ref[number * PAD : (number + 1) * PAD] = one[start : start + PAD]
+        ref[RAW_AT:PAIR_AT] = rows_in[base + 1, :LEVEL_ROWS]
+        ref[PAIR_AT:HALO_ROWS] = rows_in[base, :LEVEL_ROWS]
+        ref[HALO_ROWS:SIDES_AT] = rows_in[base + 2, :LEVEL_ROWS]
+        ref[SIDES_AT:] = packed
         if up:
-            ref[PAIR_AT - 1 : PAIR_AT, :lanes] = faces[rows - 1 :]
+            ref[PAIR_AT - 1 : PAIR_AT] = faces[rows - 1 :]
 
     even = lax.rem(lax.axis_index("lat"), 2) == 0
 
@@ -203,95 +214,153 @@
         fill(message_b, True)
 
 
-def level_kernel(
+def shifted(values):
+    return turn(values, -1, 1), turn(values, 1, 1), turn(values, -1, 0), turn(values, 1, 0)
+
+
+def face_planes(planes, limits, weights):
+    deep, face = planes[0], planes[2]
+    lane, row = iota(deep.shape, 1), iota(deep.shape, 0)
+    rows, lanes = deep.shape
+    edges = (lane == lanes - 1, lane == 0, row == rows - 1, row == 0)
+    for number, (edge, values) in enumerate(zip(edges, shifted(deep))):
+        limits[number] = jnp.where(edge, 0.0, jnp.minimum(deep, values))
+    weights[0] = turn(face, 1, 1)
+    weights[1] = turn(face, 1, 0)
+
+
+def level_faces(level, place, planes, limits, weights):
+    height = level.astype(jnp.float32)
+    face = planes[2, place]
+    return (
+        height < planes[0, place],
+        jnp.where(height < limits[0, place], face, 0.0),
+        jnp.where(height < limits[1, place], weights[0, place], 0.0),
+        jnp.where(height < limits[2, place], face, 0.0),
+        jnp.where(height < limits[3, place], weights[1, place], 0.0),
+    )
+
+
+def smooth(ref, level, tile, tiles, faces):
+    wet, face_east, face_west, face_north, face_south = faces
+    start = tile * PAD
+    item = ref[level, start : start + PAD]
+    if tile + 1 < tiles:
+        above = ref[level, start + 1 : start + 1 + PAD]
+    else:
+        above = turn(item, -1, 0)
+    below = ref[level, start - 1 : start - 1 + PAD] if tile else turn(item, 1, 0)
+    change = face_north * (above - item) + face_south * (below - item)
+    change = change + face_east * (turn(item, -1, 1) - item)
+    change = change + face_west * (turn(item, 1, 1) - item)
+    return item, jnp.where(wet, item, 0.0) + change
+
+
+def inner_kernel(
+    planes, east, north, tracer, east_out, north_out, tracer_out, limits, weights
+):
+    levels, rows, lanes = tracer.shape
+    tiles = rows // PAD
+    face_planes(planes, limits, weights)
+    for first in range(0, tiles, TILES):
+
+        def step(group, carry):
+            for t in range(GROUP):
+                level = group * GROUP + t
+                for tile in range(first, first + TILES):
+                    place = slice(tile * PAD, (tile + 1) * PAD)
+                    faces = level_faces(level, place, planes, limits, weights)
+                    one, new_one = smooth(east, level, tile, tiles, faces)
+                    two, new_two = smooth(north, level, tile, tiles, faces)
+                    spin = jnp.where(faces[0], planes[4, place], 0.0)
+                    east_out[level, place] = new_one - spin * two
+                    north_out[level, place] = new_two + spin * one
+                    tracer_out[level, place] = smooth(tracer, level, tile, tiles, faces)[1]
+            return carry
+
+        lax.fori_loop(0, levels // GROUP, step, 0)
+
+
+def rim_kernel(
     got_0, got_1, wide, planes, face_west, edges, east, north, tracer,
     east_out, north_out, tracer_out,
-    bounds, sides,
+    sides,
 ):
     levels, rows, lanes = east.shape
     from_west, from_east = received(got_0, got_1)
     lane = iota((rows, lanes), 1)
-    row = iota((rows, lanes), 0)
     deep, beside = wide[0, :, :lanes], wide[0, :, lanes:]
-    bounds[0] = jnp.where(lane == lanes - 1, 0.0, jnp.minimum(deep, turn(deep, -1, 1)))
-    bounds[1] = jnp.where(row == rows - 1, 0.0, jnp.minimum(deep, turn(deep, -1, 0)))
-    level = lax.shift_right_logical(lane, 1).astype(jnp.float32)
+    level_of = lax.shift_right_logical(lane, 1).astype(jnp.float32)
     odd_lane = lax.rem(lane, 2) == 1
     bound_east = jnp.minimum(deep[:, lanes - 1 :], beside[:, 0:1])
     bound_west = jnp.minimum(deep[:, 0:1], beside[:, lanes - 1 :])
-    weight_east, weight_west = planes[2, :, lanes - 1 :], face_west[:, 0:1]
-    weight = jnp.where(odd_lane, weight_west, weight_east)
-    weight = jnp.where(level < jnp.where(odd_lane, bound_west, bound_east), weight, 0.0)
+    weight = jnp.where(odd_lane, face_west[:, 0:1], planes[2, :, lanes - 1 :])
+    weight = jnp.where(level_of < jnp.where(odd_lane, bound_west, bound_east), weight, 0.0)
     halos = (
         jnp.where(odd_lane, turn(from_west[:, :lanes], 1, 1), turn(from_east[:, :lanes], -1, 1)),
         jnp.where(odd_lane, from_west[:, :lanes], from_east[:, :lanes]),
         jnp.where(odd_lane, turn(from_west[:, lanes:], 1, 1), turn(from_east[:, lanes:], -1, 1)),
     )
     for number in range(3):
-        sides[number] = weight * (halos[number] - edges[number])
-    small_lane, line = iota((PAD, lanes), 1), iota((PAD, lanes), 0)
+        sides[number] = turn(weight * (halos[number] - edges[number]), -1, 1)
+    small_lane = iota((PAD, lanes), 1)
     rim = (small_lane == 0) | (small_lane == lanes - 1)
-    first_line, last_line = line == 0, line == PAD - 1
-    fields, outs = (east, north, tracer), (east_out, north_out, tracer_out)
     tiles = rows // PAD
-
-    def level_step(level, carry):
-        height = level.astype(jnp.float32)
-        values = [ref[level, :PAD] for ref in fields]
-        lifted = [turn(item, -1, 0) for item in values]
-        below = [jnp.zeros((PAD, lanes), jnp.float32)] * 3
-        for tile in range(tiles):
-            place = slice(tile * PAD, (tile + 1) * PAD)
-            wet = height < planes[0, place]
-            face = planes[2, place]
-            face_east = jnp.where(height < bounds[0, place], face, 0.0)
-            face_north = jnp.where(height < bounds[1, place], face, 0.0)
-            results = []
-            for number in range(3):
-                item = values[number]
-                flux = face_east * (item - turn(item, -1, 1))
-                if tile + 1 < tiles:
-                    upper = fields[number][level, (tile + 1) * PAD : (tile + 2) * PAD]
-                    upper_lifted = turn(upper, -1, 0)
-                    above = jnp.where(last_line, upper_lifted, lifted[number])
-                else:
-                    upper, upper_lifted, above = item, lifted[number], lifted[number]
-                rise = face_north * (item - above)
-                moved = turn(rise, 1, 0)
-                fall = jnp.where(first_line, below[number], moved)
-                rim_part = pltpu.roll(sides[number, place], lanes - 1 - 2 * level + lanes, 1)
-                result = jnp.where(wet, item, 0.0) + jnp.where(rim, rim_part, 0.0)
-                results.append(result + (turn(flux, 1, 1) - flux) + (fall - rise))
-                below[number] = moved
-                values[number], lifted[number] = upper, upper_lifted
-                if number < 2:
-                    results.append(item)
-            spin = jnp.where(wet, planes[4, place], 0.0)
-            east_out[level, place] = results[0] - spin * results[3]
-            north_out[level, place] = results[2] + spin * results[1]
-            tracer_out[level, place] = results[4]
-        return carry
-
-    lax.fori_loop(0, levels, level_step, 0, unroll=2)
-
-
-def shifted(values):
-    return turn(values, -1, 1), turn(values, 1, 1), turn(values, -1, 0), turn(values, 1, 0)
-
-
-def basis_kernel(thickness, got_a, got_b, wide, gram, basis, depth_wide, halo):
+    pairs = ((east, east_out), (north, north_out), (tracer, tracer_out))
+    for first in range(0, tiles, TILES):
+        chunk = range(first, first + TILES)
+
+        def step(group, rims):
+            for t in range(GROUP):
+                level = group * GROUP + t
+                for number, tile in enumerate(chunk):
+                    place = slice(tile * PAD, (tile + 1) * PAD)
+                    for index, (source, target) in enumerate(pairs):
+                        part = turn(rims[3 * number + index], -2 * t, 1)
+                        target[level, place] = source[level, place] + jnp.where(rim, part, 0.0)
+            return tuple(turn(item, -2 * GROUP, 1) for item in rims)
+
+        lax.fori_loop(
+            0, levels // GROUP, step,
+            tuple(
+                sides[number, tile * PAD : (tile + 1) * PAD] for tile in chunk for number in range(3)
+            ),
+        )
+
+
+def basis_kernel(
+    thickness, got_a, got_b, wide, planes, rows_in, tracer_in,
+    gram, basis, depth_wide, halo, fixes, tracer,
+):
     rows, lanes = wide.shape[1], wide.shape[2] // 2
     lat = lax.axis_index("lat")
     even = lax.rem(lat, 2) == 0
     at_top = lat == lax.axis_size("lat") - 1
     at_bottom = lat == 0
 
+    one, two = got_a[...], got_b[...]
+    small_lane = iota((PAD, lanes), 1)
+    near_side = (small_lane < WIDE) | (small_lane >= lanes - WIDE)
+
+    def tiles_of(values, number):
+        start = number * PAD
+        first = values[start : start + PAD]
+        if number < SIDE_GROUPS:
+            second = turn(values[SIDES_AT:], -2 * WIDE * number - WIDE, 1)
+            second = jnp.where(near_side, second, 0.0)
+        else:
+            start = start + LEVEL_ROWS
+            second = values[start : start + PAD]
+        return first, second
+
+    groups = range(HALO_ROWS // PAD)
+    above = jnp.where(even, one, two)
+
     @pl.when(at_top)
     def _():
-        back = lanes - 1 - iota((PAD, lanes), 1)
-        for number in range(MESSAGE_ROWS // PAD):
-            for tile in range(2):
-                values = got_b[number * PAD : (number + 1) * PAD, tile * lanes : (tile + 1) * lanes]
+        back = lanes - 1 - small_lane
+        for number in groups:
+            for tile, values in enumerate(tiles_of(above, number)):
                 values = jnp.take_along_axis(values, back, axis=1)
                 if number < 3:
                     values = jnp.concatenate(
@@ -301,9 +370,14 @@
 
     @pl.when(jnp.logical_not(at_top))
     def _():
-        halo[0] = jnp.where(even, got_a[...], got_b[...])
-
-    halo[1] = jnp.where(at_bottom, 0.0, jnp.where(even, got_b[...], got_a[...]))
+        for number in groups:
+            for tile, values in enumerate(tiles_of(above, number)):
+                halo[0, number * PAD : (number + 1) * PAD, tile * lanes : (tile + 1) * lanes] = values
+
+    below = jnp.where(at_bottom, 0.0, jnp.where(even, two, one))
+    for number in groups:
+        for tile, values in enumerate(tiles_of(below, number)):
+            halo[1, number * PAD : (number + 1) * PAD, tile * lanes : (tile + 1) * lanes] = values
 
     def whole(number):
         place = slice(number * PAD, (number + 1) * PAD)
@@ -385,6 +459,29 @@
     same = iota((16, lanes), 0) == iota((16, lanes), 1)
     line = jnp.sum(jnp.where(same, sums, 0.0), axis=0, keepdims=True)
     gram[...] = jnp.broadcast_to(line, gram.shape)
+
+    face = planes[2]
+    level = level[:, :lanes]
+    top_face = face[rows - 1 :] + jnp.where(at_top, halo[0, PAIR_AT - 1 : PAIR_AT, :lanes], 0.0)
+    low_face = halo[1, PAIR_AT - 1 : PAIR_AT, :lanes]
+    for side, line, weight in ((0, core_end - 1, top_face), (1, PAD, low_face)):
+        other = line + 1 - 2 * side
+        bound = jnp.minimum(deep[line : line + 1], deep[other : other + 1])[:, :lanes]
+        outer = (
+            halo[side, PAIR_AT:, :lanes],
+            halo[side, RAW_AT:PAIR_AT, :lanes],
+            halo[side, PAIR_AT:, lanes:],
+        )
+        for number in range(3):
+            inner = rows_in[3 * side + number, :LEVEL_ROWS]
+            fixes[3 * side + number] = jnp.where(
+                level < bound, weight * (outer[number] - inner), 0.0
+            )
+    for number in range(tracer.shape[0]):
+        last = tracer_in[number, rows - 1 : rows] + fixes[2, number : number + 1]
+        first = tracer_in[number, 0:1] + fixes[5, number : number + 1]
+        tracer[number, rows - 1 : rows] = last
+        tracer[number, 0:1] = first
 
 
 def solve(line):
@@ -412,13 +509,12 @@
 
 
 def final_kernel(
-    thickness, totals, basis, depth_wide, planes_in, face_west, halo, rows_in,
-    east, north, tracer_in,
+    thickness, totals, basis, depth_wide, planes_in, face_west, halo, fixes, east, north, tracer,
     tracer_hbm, east_hbm, north_hbm, surface,
-    planes, fixes, tracer, east_out, north_out, sems, tracer_sem,
+    planes, east_out, north_out, sems, tracer_sem,
 ):
     levels, rows, lanes = east.shape
-    size = levels // PARTS
+    size = levels // OUT_PARTS
     core_end = PAD + rows
     outs = ((east_out, east_hbm), (north_out, north_hbm))
 
@@ -428,6 +524,7 @@
         return pltpu.make_async_copy(source.at[place], target.at[place], sems.at[number, part])
 
     tracer_copy = pltpu.make_async_copy(tracer, tracer_hbm, tracer_sem)
+    tracer_copy.start()
     at_top = lax.axis_index("lat") == lax.axis_size("lat") - 1
     row = iota((rows, lanes), 0)
     deep = depth_wide[...]
@@ -441,20 +538,6 @@
     planes[0] = deep[PAD:core_end, :lanes]
     for number in range(4):
         planes[1 + number] = bounds[number]
-    level = iota((LEVEL_ROWS, lanes), 0).astype(jnp.float32)
-    for side, line in ((0, rows - 1), (1, 0)):
-        bound = bounds[2 + side][line : line + 1]
-        weight = faces[2 + side][line : line + 1]
-        outer = (
-            halo[side, PAIR_AT:, :lanes],
-            halo[side, RAW_AT:PAIR_AT, :lanes],
-            halo[side, PAIR_AT:, lanes:],
-        )
-        for number in range(3):
-            inner = rows_in[3 * side + number, :LEVEL_ROWS]
-            fixes[3 * side + number] = jnp.where(
-                level < bound, weight * (outer[number] - inner), 0.0
-            )
     parts = solve(jnp.sum(totals[...], axis=0, keepdims=True))
     height = parts[0] * basis[0]
     for number in range(1, 4):
@@ -502,22 +585,9 @@
         part_copy(1, part).start()
         return carry
 
-    def tracer_step(level, carry):
-        for tile in range(rows // PAD):
-            place = slice(tile * PAD, (tile + 1) * PAD)
-            result = tracer_in[level, place]
-            if tile == 0:
-                result = result + jnp.where(first_line, fixes[5, pl.ds(level, 1), :], 0.0)
-            if tile == rows // PAD - 1:
-                result = result + jnp.where(last_line, fixes[2, pl.ds(level, 1), :], 0.0)
-            tracer[level, place] = result
-        return carry
-
-    lax.fori_loop(0, levels, tracer_step, 0, unroll=5)
-    tracer_copy.start()
-    lax.fori_loop(0, PARTS, part_step, 0)
+    lax.fori_loop(0, OUT_PARTS, part_step, 0)
     tracer_copy.wait()
-    for part in range(PARTS):
+    for part in range(OUT_PARTS):
         part_copy(0, part).wait()
         part_copy(1, part).wait()
 
@@ -528,8 +598,8 @@
         for lon in range(lons):
             other = lat + 1 if lat % 2 == odd else lat - 1
             if other < 0:
-                continue
-            if other == lats:
+                pairs.append((lon, (lon ^ 1) % lons))
+            elif other == lats:
                 pairs.append((lat * lons + lon, lat * lons + lons - 1 - lon))
             else:
                 pairs.append((lat * lons + lon, other * lons + lon))
@@ -554,9 +624,13 @@
     in_hbm = pl.BlockSpec(memory_space=pltpu.HBM)
     in_vmem = pl.BlockSpec(memory_space=pltpu.VMEM)
     params = pltpu.CompilerParams(vmem_limit_bytes=VMEM_BYTES)
+    cost = lambda work: pl.CostEstimate(
+        flops=work * levels * rows * lanes, bytes_accessed=8 * levels * rows * lanes,
+        transcendentals=0,
+    )
     plane, pair, field = (rows, lanes), (rows, 2 * lanes), (levels, rows, lanes)
     full = (rows + 2 * PAD, 2 * lanes)
-    message = (MESSAGE_ROWS, 2 * lanes)
+    message, strips = (MESSAGE_ROWS, lanes), (2, HALO_ROWS, 2 * lanes)
 
     message_0, message_1, planes, edge_rows, edges, east, north, tracer = pl.pallas_call(
         pack_kernel,
@@ -582,9 +656,22 @@
         ]
     )
 
-    got_1 = near(lax.ppermute(message_1, "lon", lon_swaps(lons, 1)))
-    got_0 = near(lax.ppermute(message_0, "lon", lon_swaps(lons, 0)))
-
+    got_1 = lax.ppermute(message_1, "lon", lon_swaps(lons, 1))
+    got_0 = lax.ppermute(message_0, "lon", lon_swaps(lons, 0))
+
+    east_part, north_part, tracer_part = pl.pallas_call(
+        inner_kernel,
+        in_specs=[in_vmem] * 4,
+        out_specs=[in_vmem] * 3,
+        out_shape=[scratch(*field)] * 3,
+        scratch_shapes=[scratch(4, *plane), scratch(2, *plane)],
+        compiler_params=params,
+        cost_estimate=cost(60),
+        name="inner",
+    )(near(planes), near(east), near(north), near(tracer))
+
+    edges, east_part = lax.optimization_barrier((edges, east_part))
+    got_0, got_1 = near(got_0), near(got_1)
     wide, face_west, message_a, message_b = pl.pallas_call(
         stitch_kernel,
         in_specs=[in_vmem] * 5,
@@ -598,33 +685,36 @@
     got_a = lax.ppermute(message_a, BOTH, swaps(lats, lons, 0))
 
     east_part, north_part, tracer_part = pl.pallas_call(
-        level_kernel,
+        rim_kernel,
         in_specs=[in_vmem] * 9,
         out_specs=[in_vmem] * 3,
         out_shape=[scratch(*field)] * 3,
-        scratch_shapes=[scratch(2, *plane), scratch(3, *plane)],
+        scratch_shapes=[scratch(3, *plane)],
+        input_output_aliases={6: 0, 7: 1, 8: 2},
         compiler_params=params,
-        cost_estimate=pl.CostEstimate(
-            flops=60 * levels * rows * lanes, bytes_accessed=24 * levels * rows * lanes,
-            transcendentals=0,
-        ),
-        name="level",
+        cost_estimate=cost(10),
+        name="rim",
     )(
-        got_0, got_1, near(wide), near(planes), near(face_west), near(edges), near(east),
-        near(north), near(tracer),
+        got_0, got_1, near(wide), near(planes), near(face_west), near(edges), near(east_part),
+        near(north_part), near(tracer_part),
     )
 
     wide, east_part = lax.optimization_barrier((wide, east_part))
-    gram, basis, depth_wide, halo = pl.pallas_call(
+    gram, basis, depth_wide, halo, fixes, tracer_part = pl.pallas_call(
         basis_kernel,
-        in_specs=[scalars] + [in_vmem] * 3,
-        out_specs=[in_vmem] * 4,
+        in_specs=[scalars] + [in_vmem] * 6,
+        out_specs=[in_vmem] * 6,
         out_shape=[
-            scratch(lats * lons, lanes), scratch(4, *full), scratch(*full), scratch(2, *message)
+            scratch(lats * lons, lanes), scratch(4, *full), scratch(*full), scratch(*strips),
+            scratch(6, LEVEL_ROWS, lanes), scratch(*field),
         ],
+        input_output_aliases={6: 5},
         compiler_params=params,
         name="basis",
-    )(thickness, near(got_a), near(got_b), near(wide))
+    )(
+        thickness, near(got_a), near(got_b), near(wide), near(planes), near(edge_rows),
+        near(tracer_part),
+    )
 
     totals = lax.all_to_all(gram, BOTH, 0, 0, tiled=True)
 
@@ -634,14 +724,14 @@
         out_specs=[in_hbm] * 3 + [in_vmem],
         out_shape=[floats(*field)] * 3 + [jax.ShapeDtypeStruct(plane, jnp.float32)],
         scratch_shapes=[
-            scratch(15, *plane), scratch(6, LEVEL_ROWS, lanes), scratch(*field), scratch(*field),
-            scratch(*field), pltpu.SemaphoreType.DMA((2, PARTS)), pltpu.SemaphoreType.DMA,
+            scratch(15, *plane), scratch(*field), scratch(*field),
+            pltpu.SemaphoreType.DMA((2, OUT_PARTS)), pltpu.SemaphoreType.DMA,
         ],
         compiler_params=params,
         name="final",
     )(
         thickness, near(totals), near(basis), near(depth_wide), near(planes), near(face_west),
-        near(halo), near(edge_rows), near(east_part), near(north_part), near(tracer_part),
+        near(halo), near(fixes), near(east_part), near(north_part), near(tracer_part),
     )
     return tracer_adj, east_adj, north_adj, surface_adj
 

time: 54.9 us -> 49.7 us (0.905)
  blocking collectives: 25.9 us -> 21.2 us
  starting transfers between devices: 4.9 us -> 7.86 us
  waiting for transfers between devices: 2.34 us -> 0.01 us
  Pallas kernels: 20.9 us -> 19.8 us
    all_to_all x1, blocking collectives: 25.9 us -> 21.2 us  [local(): totals = lax.all_to_all(gram, BOTH, 0, 0, tiled=True)]
    ppermute x1, starting transfers between devices: 0.66 us -> 3.7 us  [local(): got_b = lax.ppermute(message_b, BOTH, swaps(lats, lons, 1))]
    ppermute x2, waiting for transfers between devices: 2.33 us -> 0.01 us  [the longest x1 0.01 us: local(): got_0 = lax.ppermute(message_0, 'lon', lon_swaps(lons, 0))]
    pallas_call x2 -> x3, Pallas kernels: 9.67 us -> 8.93 us  [the longest x1 4.24 us: local(): pl.pallas_call(inner_kernel, in_specs=[in_vmem] * 4, out_specs=[in_vmem]...]
  transfers between devices with their start and end apart: 4 -> 4, of which waited for: 1 -> 0; matrix products, arithmetic and copies ran while one was open for 0% -> 0% of each run, Pallas kernels for 15% -> 15%
where the time goes in v3:
time: 49.7 us; the launch traced here: 49.5 us
  blocking collectives  21.2 us (43%)
  Pallas kernels  19.8 us (40%)
  starting transfers between devices  7.86 us (16%)
  between operations  0.7 us (1%)
    all_to_all x1, blocking collectives, local(): totals = lax.all_to_all(gram, BOTH, 0, 0, tiled=True)  21.2 us
    pallas_call x1, Pallas kernels, local(): pl.pallas_call(final_kernel, in_specs=[scalars] + [in_vmem] * 10, out_spe...  6.1 us
    pallas_call x1, Pallas kernels, local(): pl.pallas_call(pack_kernel, in_specs=[in_hbm] * 8, out_specs=[in_vmem] *...  4.35 us
    pallas_call x1, Pallas kernels, local(): pl.pallas_call(inner_kernel, in_specs=[in_vmem] * 4, out_specs=[in_vmem]...  4.24 us
    ppermute x1, starting transfers between devices, local(): got_b = lax.ppermute(message_b, BOTH, swaps(lats, lons, 1))  3.7 us
    pallas_call x1, Pallas kernels, local(): pl.pallas_call(rim_kernel, in_specs=[in_vmem] * 9, out_specs=[in_vmem] *...  3.19 us
    ppermute x1, starting transfers between devices, local(): got_0 = lax.ppermute(message_0, 'lon', lon_swaps(lons, 0))  1.5 us
    pallas_call x1, Pallas kernels, local(): pl.pallas_call(basis_kernel, in_specs=[scalars] + [in_vmem] * 6, out_spec...  1.5 us
  transfers between devices with their start and end apart: 4, of which 0 were waited for; matrix products, arithmetic and copies ran while one was open for 0% of the time, Pallas kernels for 15%

profile of v3, /device:TPU:1, one launch (start us, length us, event | category | flops | bytes accessed | tf_op | source)
XLA Modules:
  0.0 49.5 jit_solution(14603725169539442563)
XLA Ops:
  0.6 4.4 %pack.1 = (f32[64,256]{1,0:T(8,128)S(1)}, f32[64,256]{1,0:T(8,128)S(1)}, f32[5,64,128]{2,1,0:T(8,128)S(1)}, f32[6,64,128]{2,1,0:T(8,128)S(1)}, f32[3,64,128]{2,1...) custom-call(f32[50,64,128]{2,1,0:T(8,128)} %east_in.1, ...), custom_call_target="tpu_custom_call" | custom-call | tf_op jit(solution)/shard_map/pack/pallas_call | solution.py:635
  5.0 1.5 %collective-permute-start = (f32[64,256]{1,0:T(8,128)S(1)}, f32[64,256]{1,0:T(8,128)S(1)}, u32[]{:S(2)}, u32[]{:S(2)}) collective-permute-start(f32[64,256]{1,0:T(8,128)S(1)} %get-tuple-element.32), channel_id=1, source_target_pairs={{0,1},{1,0},{2,3},{3,2},{4,5},{5,4},{6,7},{7,6},{8,9},{9,8},{10,11... | collective-permute-start | bytes 196616 | tf_op jit(solution)/shard_map/ppermute | solution.py:660
  6.5 1.4 %collective-permute-start.1 = (f32[64,256]{1,0:T(8,128)S(1)}, f32[64,256]{1,0:T(8,128)S(1)}, u32[]{:S(2)}, u32[]{:S(2)}) collective-permute-start(f32[64,256]{1,0:T(8,128)S(1)} %get-tuple-element.33), channel_id=1, source_target_pairs={{0,15},{1,2},{2,1},{3,4},{4,3},{5,6},{6,5},{7,8},{8,7},{9,10},{10,... | collective-permute-start | bytes 196616 | tf_op jit(solution)/shard_map/ppermute | solution.py:659
  7.9 4.2 %inner.1 = (f32[50,64,128]{2,1,0:T(8,128)S(1)}, f32[50,64,128]{2,1,0:T(8,128)S(1)}, f32[50,64,128]{2,1,0:T(8,128)S(1)}) custom-call(f32[5,64,128]{2,1,0:T(8,128)S(1)} %get-tuple-element.34.planes.planes_in, f32[50,64,128]{2,1,0:T(8,128)S(1)} %get-tuple-element.37.east, f32[50,64,128]{2,1,0:T(8,128)S(1)} %get-tuple-element.38.north, ...), custom_call_target="tpu_custom_call" | custom-call | flops 24576000 | bytes 3276800 | tf_op jit(solution)/shard_map/inner/pallas_call | solution.py:662
  12.1 0.0 collective-permute-done.got_0
  12.1 0.0 collective-permute-done.1.got_1
  12.1 0.4 stitch.1
  12.5 1.3 %collective-permute-start.2 = (f32[200,128]{1,0:T(8,128)S(1)}, f32[200,128]{1,0:T(8,128)S(1)}, u32[]{:S(2)}, u32[]{:S(2)}) collective-permute-start(f32[200,128]{1,0:T(8,128)S(1)} %get-tuple-element.42), channel_id=1, source_target_pairs={{0,16},{1,17},{2,18},{3,19},{4,20},{5,21},{6,22},{7,23},{8,24},{9,... | collective-permute-start | bytes 307208 | tf_op jit(solution)/shard_map/ppermute | solution.py:685
  13.8 3.7 %collective-permute-start.3 = (f32[200,128]{1,0:T(8,128)S(1)}, f32[200,128]{1,0:T(8,128)S(1)}, u32[]{:S(2)}, u32[]{:S(2)}) collective-permute-start(f32[200,128]{1,0:T(8,128)S(1)} %get-tuple-element.43), channel_id=1, source_target_pairs={{0,1},{1,0},{2,3},{3,2},{4,5},{5,4},{6,7},{7,6},{8,9},{9,8},{10,11... | collective-permute-start | bytes 307208 | tf_op jit(solution)/shard_map/ppermute | solution.py:684
  17.5 0.0 copy-start
  17.5 3.2 %rim.1 = (f32[50,64,128]{2,1,0:T(8,128)S(1)}, f32[50,64,128]{2,1,0:T(8,128)S(1)}, f32[50,64,128]{2,1,0:T(8,128)S(1)}) custom-call(f32[64,256]{1,0:T(8,128)S(1)} %collective-permute-done.got_0, f32[64,256]{1,0:T(8,128)S(1)} %collective-permute-done.1.got_1, ...), custom_call_target="tpu_custom_call", output_to_operand_aliasing={{0}: (6, {}), {1}: (7, {}), {2}: (8, {})} | custom-call | flops 4096000 | bytes 3276800 | tf_op jit(solution)/shard_map/rim/pallas_call | solution.py:687
  20.7 0.0 collective-permute-done.2.got_a
  20.7 0.0 collective-permute-done.3.got_b
  20.7 0.0 copy-done
  20.7 1.5 %basis.1 = (f32[128,128]{1,0:T(8,128)S(1)}, f32[4,80,256]{2,1,0:T(8,128)S(1)}, f32[80,256]{1,0:T(8,128)S(1)}, f32[2,136,256]{2,1,0:T(8,128)S(1)}, f32[6,56,128]{2,1,0:T(8,128)S(1)}, /*index=5*/f32[50,64,128]{2,1,0:T(8,128)S(1)}) custom-call(f32[50]{0:T(128)S(1)} %copy-done, ...), custom_call_target="tpu_custom_call", output_to_operand_aliasing={{5}: (6, {})} | custom-call | tf_op jit(solution)/shard_map/basis/pallas_call | solution.py:703
  22.2 21.2 %all_to_all.11 = f32[128,1,128]{2,1,0:T(1,128)S(1)} all-to-all(f32[128,1,128]{2,1,0:T(1,128)S(1)} %bitcast.5), channel_id=1, replica_groups=mesh['lat'=8,'lon'=16] {'lat','lon'}, dimensions={0} | all-to-all | bytes 131072 | tf_op jit(solution)/shard_map/all_to_all | solution.py:719
  43.4 6.1 %final.1 = (f32[50,64,128]{2,1,0:T(8,128)}, f32[50,64,128]{2,1,0:T(8,128)}, f32[50,64,128]{2,1,0:T(8,128)}, f32[64,128]{1,0:T(8,128)}) custom-call(f32[50]{0:T(128)S(1)} %copy-done, f32[128,128]{1,0:T(8,128)S(1)} %bitcast.4, f32[4,80,256]{2,1,0:T(8,128)S(1)} %get-tuple-element.53.basis, f32[80,256]{1,0:T(8,128)S(1)} %get-tuple-element.54.depth_wide, ...), custom_call_target="tpu_custom_call" | custom-call | tf_op jit(solution)/shard_map/final/pallas_call | solution.py:721
Async XLA Ops:
  5.0 7.1 %collective-permute-start = (f32[64,256]{1,0:T(8,128)S(1)}, f32[64,256]{1,0:T(8,128)S(1)}, u32[]{:S(2)}, u32[]{:S(2)}) collective-permute-start(f32[64,256]{1,0:T(8,128)S(1)} %get-tuple-element.32), channel_id=1, source_target_pairs={{0,1},{1,0},{2,3},{3,2},{4,5},{5,4},{6,7},{7,6},{8,9},{9,8},{10,11... | collective-permute-start | bytes 196616 | tf_op jit(solution)/shard_map/ppermute | solution.py:660
  6.5 5.6 %collective-permute-start.1 = (f32[64,256]{1,0:T(8,128)S(1)}, f32[64,256]{1,0:T(8,128)S(1)}, u32[]{:S(2)}, u32[]{:S(2)}) collective-permute-start(f32[64,256]{1,0:T(8,128)S(1)} %get-tuple-element.33), channel_id=1, source_target_pairs={{0,15},{1,2},{2,1},{3,4},{4,3},{5,6},{6,5},{7,8},{8,7},{9,10},{10,... | collective-permute-start | bytes 196616 | tf_op jit(solution)/shard_map/ppermute | solution.py:659
  12.5 8.2 %collective-permute-start.2 = (f32[200,128]{1,0:T(8,128)S(1)}, f32[200,128]{1,0:T(8,128)S(1)}, u32[]{:S(2)}, u32[]{:S(2)}) collective-permute-start(f32[200,128]{1,0:T(8,128)S(1)} %get-tuple-element.42), channel_id=1, source_target_pairs={{0,16},{1,17},{2,18},{3,19},{4,20},{5,21},{6,22},{7,23},{8,24},{9,... | collective-permute-start | bytes 307208 | tf_op jit(solution)/shard_map/ppermute | solution.py:685
  13.8 6.9 %collective-permute-start.3 = (f32[200,128]{1,0:T(8,128)S(1)}, f32[200,128]{1,0:T(8,128)S(1)}, u32[]{:S(2)}, u32[]{:S(2)}) collective-permute-start(f32[200,128]{1,0:T(8,128)S(1)} %get-tuple-element.43), channel_id=1, source_target_pairs={{0,1},{1,0},{2,3},{3,2},{4,5},{5,4},{6,7},{7,6},{8,9},{9,8},{10,11... | collective-permute-start | bytes 307208 | tf_op jit(solution)/shard_map/ppermute | solution.py:684
  17.5 3.2 %copy-start = (f32[50]{0:T(128)S(1)}, f32[50]{0:T(128)}, u32[]{:S(2)}) copy-start(f32[50]{0:T(128)} %thickness.3) | copy-start | bytes 604

commit v4 on v3

--- a/solution.py
+++ b/solution.py
@@ -62,7 +62,7 @@
         move.start()
     for part in range(PARTS):
         for number in range(3):
-            part_copy(number, part).start()
+            part_copy(number, part).start(priority=min(part, 1))
     rows_out[:, levels - levels % PAD :] = jnp.zeros((6, rows - levels + levels % PAD, lanes), jnp.float32)
     px[...] = jnp.zeros((rows, lanes), jnp.float32)
     py[...] = jnp.zeros((rows, lanes), jnp.float32)
@@ -283,7 +283,7 @@
 
 def rim_kernel(
     got_0, got_1, wide, planes, face_west, edges, east, north, tracer,
-    east_out, north_out, tracer_out,
+    east_out, north_out, tracer_out, limits, faces,
     sides,
 ):
     levels, rows, lanes = east.shape
@@ -292,6 +292,15 @@
     deep, beside = wide[0, :, :lanes], wide[0, :, lanes:]
     level_of = lax.shift_right_logical(lane, 1).astype(jnp.float32)
     odd_lane = lax.rem(lane, 2) == 1
+    limits[0] = deep
+    limits[1] = jnp.minimum(deep, jnp.where(lane == lanes - 1, beside[:, 0:1], turn(deep, -1, 1)))
+    limits[2] = jnp.minimum(deep, jnp.where(lane == 0, beside[:, lanes - 1 :], turn(deep, 1, 1)))
+    limits[3] = jnp.minimum(deep, turn(deep, -1, 0))
+    limits[4] = jnp.minimum(deep, turn(deep, 1, 0))
+    faces[0] = planes[2]
+    faces[1] = face_west[...]
+    faces[2] = planes[2]
+    faces[3] = turn(planes[2], 1, 0)
     bound_east = jnp.minimum(deep[:, lanes - 1 :], beside[:, 0:1])
     bound_west = jnp.minimum(deep[:, 0:1], beside[:, lanes - 1 :])
     weight = jnp.where(odd_lane, face_west[:, 0:1], planes[2, :, lanes - 1 :])
@@ -329,8 +338,9 @@
 
 
 def basis_kernel(
-    thickness, got_a, got_b, wide, planes, rows_in, tracer_in,
-    gram, basis, depth_wide, halo, fixes, tracer,
+    thickness, got_a, got_b, wide, rows_in, tracer_in, limits_in, faces_in,
+    gram, basis, fixes, tracer, limits, faces,
+    halo,
 ):
     rows, lanes = wide.shape[1], wide.shape[2] // 2
     lat = lax.axis_index("lat")
@@ -384,7 +394,6 @@
         return jnp.concatenate([halo[1, place], wide[number], halo[0, place]], axis=0)
 
     deep, store, plane = whole(0), whole(1), whole(2)
-    depth_wide[...] = deep
     full = deep.shape
     row = iota(full, 0)
     core_end = PAD + rows
@@ -460,13 +469,14 @@
     line = jnp.sum(jnp.where(same, sums, 0.0), axis=0, keepdims=True)
     gram[...] = jnp.broadcast_to(line, gram.shape)
 
-    face = planes[2]
     level = level[:, :lanes]
-    top_face = face[rows - 1 :] + jnp.where(at_top, halo[0, PAIR_AT - 1 : PAIR_AT, :lanes], 0.0)
+    top_face = faces_in[2, rows - 1 :] + jnp.where(at_top, halo[0, PAIR_AT - 1 : PAIR_AT, :lanes], 0.0)
     low_face = halo[1, PAIR_AT - 1 : PAIR_AT, :lanes]
     for side, line, weight in ((0, core_end - 1, top_face), (1, PAD, low_face)):
         other = line + 1 - 2 * side
         bound = jnp.minimum(deep[line : line + 1], deep[other : other + 1])[:, :lanes]
+        limits[3 + side, line - PAD : line - PAD + 1] = bound
+        faces[2 + side, line - PAD : line - PAD + 1] = weight
         outer = (
             halo[side, PAIR_AT:, :lanes],
             halo[side, RAW_AT:PAIR_AT, :lanes],
@@ -485,7 +495,7 @@
 
 
 def solve(line):
-    entry = [line[:, i : i + 1] for i in range(14)]
+    entry = [jnp.broadcast_to(line[:, i : i + 1], line.shape) for i in range(14)]
     system = [[None] * 5 for _ in range(4)]
     for i in range(4):
         for j in range(i, 4):
@@ -509,9 +519,9 @@
 
 
 def final_kernel(
-    thickness, totals, basis, depth_wide, planes_in, face_west, halo, fixes, east, north, tracer,
+    thickness, totals, basis, planes_in, limits, faces, fixes, east, north, tracer,
     tracer_hbm, east_hbm, north_hbm, surface,
-    planes, east_out, north_out, sems, tracer_sem,
+    planes, work, east_out, north_out, sems, tracer_sem,
 ):
     levels, rows, lanes = east.shape
     size = levels // OUT_PARTS
@@ -526,35 +536,52 @@
     tracer_copy = pltpu.make_async_copy(tracer, tracer_hbm, tracer_sem)
     tracer_copy.start()
     at_top = lax.axis_index("lat") == lax.axis_size("lat") - 1
-    row = iota((rows, lanes), 0)
-    deep = depth_wide[...]
-    bounds = [jnp.minimum(deep, item)[PAD:core_end, :lanes] for item in shifted(deep)]
-    face = planes_in[2]
-    north_face = face + jnp.where(
-        at_top & (row == rows - 1), halo[0, PAIR_AT - 1 : PAIR_AT, :lanes], 0.0
-    )
-    south_face = jnp.where(row == 0, halo[1, PAIR_AT - 1 : PAIR_AT, :lanes], turn(face, 1, 0))
-    faces = (face, face_west[...], north_face, south_face)
-    planes[0] = deep[PAD:core_end, :lanes]
-    for number in range(4):
-        planes[1 + number] = bounds[number]
     parts = solve(jnp.sum(totals[...], axis=0, keepdims=True))
-    height = parts[0] * basis[0]
-    for number in range(1, 4):
-        height = height + parts[number] * basis[number]
-    surface[...] = planes_in[1] * height[PAD:core_end, :lanes]
-    full_row = iota(height.shape, 0)
-    folded = at_top & (full_row == core_end)
-    to_east, to_west, to_north, to_south = shifted(height)
-    slope_x = jnp.where(folded, to_west, to_east) - height
-    slope_y = jnp.where(folded, to_south, to_north) - height
-    inner_x, inner_y = slope_x[PAD:core_end, :lanes], slope_y[PAD:core_end, :lanes]
+    tall = (rows + 2 * PAD, lanes)
+    lane, row = iota(tall, 1), iota(tall, 0)
+
+    def combine(start):
+        total = parts[0] * basis[0, :, start : start + lanes]
+        for number in range(1, 4):
+            total = total + parts[number] * basis[number, :, start : start + lanes]
+        return total
+
+    inner, outer = combine(0), combine(lanes)
+    surface[...] = planes_in[1] * inner[PAD:core_end]
+
+    def to_east(first, second):
+        return jnp.where(lane[: first.shape[0]] == lanes - 1, turn(second, -1, 1), turn(first, -1, 1))
+
+    def to_west(first, second):
+        return jnp.where(lane[: first.shape[0]] == 0, turn(second, 1, 1), turn(first, 1, 1))
+
+    end = slice(core_end, core_end + PAD)
+    fold = at_top & (row[:PAD] == 0)
+
+    def slopes(first, second):
+        along = to_east(first, second)
+        across = turn(first, -1, 0)
+        along_end = jnp.where(fold, to_west(first[end], second[end]), along[end])
+        across_end = jnp.where(fold, turn(first, 1, 0)[end], across[end])
+        along = jnp.concatenate([along[:core_end], along_end], axis=0)
+        across = jnp.concatenate([across[:core_end], across_end], axis=0)
+        return along - first, across - first
+
+    inner_x, inner_y = slopes(inner, outer)
+    outer_x, outer_y = slopes(outer, inner)
+    core = slice(PAD, core_end)
     spin = planes_in[4]
-    planes[5] = inner_x - spin * inner_y
-    planes[6] = inner_y + spin * inner_x
-    for start, slope, inner in ((7, slope_x, inner_x), (11, slope_y, inner_y)):
-        for number, item in enumerate(shifted(slope)):
-            planes[start + number] = faces[number] * (inner - item[PAD:core_end, :lanes])
+    planes[0] = inner_x[core] - spin * inner_y[core]
+    planes[1] = inner_y[core] + spin * inner_x[core]
+    for start, first, second in ((2, inner_x, outer_x), (6, inner_y, outer_y)):
+        work[...] = first
+        own = first[core]
+        sides = (
+            to_east(own, second[core]), to_west(own, second[core]),
+            work[PAD + 1 : core_end + 1], work[PAD - 1 : core_end - 1],
+        )
+        for number, item in enumerate(sides):
+            planes[start + number] = faces[number] * (own - item)
 
     line = iota((PAD, lanes), 0)
     first_line, last_line = line == 0, line == PAD - 1
@@ -562,13 +589,14 @@
     def part_step(part, carry):
         for tile in range(rows // PAD):
             place = slice(tile * PAD, (tile + 1) * PAD)
-            own = [planes[number, place] for number in range(15)]
+            bounds = [limits[number, place] for number in range(5)]
+            own = [planes[number, place] for number in range(10)]
             for t in range(size):
                 level = part * size + t
                 height = level.astype(jnp.float32)
-                open_sides = [height < own[number] for number in range(5)]
+                open_sides = [height < bound for bound in bounds]
                 for out, values, base, start, number in (
-                    (east_out, east, 5, 7, 0), (north_out, north, 6, 11, 1)
+                    (east_out, east, 0, 2, 0), (north_out, north, 1, 6, 1)
                 ):
                     change = jnp.where(open_sides[0], own[base], 0.0)
                     for side in range(4):
@@ -684,11 +712,11 @@
     got_b = lax.ppermute(message_b, BOTH, swaps(lats, lons, 1))
     got_a = lax.ppermute(message_a, BOTH, swaps(lats, lons, 0))
 
-    east_part, north_part, tracer_part = pl.pallas_call(
+    east_part, north_part, tracer_part, limits, faces = pl.pallas_call(
         rim_kernel,
         in_specs=[in_vmem] * 9,
-        out_specs=[in_vmem] * 3,
-        out_shape=[scratch(*field)] * 3,
+        out_specs=[in_vmem] * 5,
+        out_shape=[scratch(*field)] * 3 + [scratch(5, *plane), scratch(4, *plane)],
         scratch_shapes=[scratch(3, *plane)],
         input_output_aliases={6: 0, 7: 1, 8: 2},
         compiler_params=params,
@@ -700,38 +728,39 @@
     )
 
     wide, east_part = lax.optimization_barrier((wide, east_part))
-    gram, basis, depth_wide, halo, fixes, tracer_part = pl.pallas_call(
+    gram, basis, fixes, tracer_part, limits, faces = pl.pallas_call(
         basis_kernel,
-        in_specs=[scalars] + [in_vmem] * 6,
+        in_specs=[scalars] + [in_vmem] * 7,
         out_specs=[in_vmem] * 6,
         out_shape=[
-            scratch(lats * lons, lanes), scratch(4, *full), scratch(*full), scratch(*strips),
-            scratch(6, LEVEL_ROWS, lanes), scratch(*field),
+            scratch(lats * lons, lanes), scratch(4, *full), scratch(6, LEVEL_ROWS, lanes),
+            scratch(*field), scratch(5, *plane), scratch(4, *plane),
         ],
-        input_output_aliases={6: 5},
+        scratch_shapes=[scratch(*strips)],
+        input_output_aliases={5: 3, 6: 4, 7: 5},
         compiler_params=params,
         name="basis",
     )(
-        thickness, near(got_a), near(got_b), near(wide), near(planes), near(edge_rows),
-        near(tracer_part),
+        thickness, near(got_a), near(got_b), near(wide), near(edge_rows), near(tracer_part),
+        near(limits), near(faces),
     )
 
     totals = lax.all_to_all(gram, BOTH, 0, 0, tiled=True)
 
     tracer_adj, east_adj, north_adj, surface_adj = pl.pallas_call(
         final_kernel,
-        in_specs=[scalars] + [in_vmem] * 10,
+        in_specs=[scalars] + [in_vmem] * 9,
         out_specs=[in_hbm] * 3 + [in_vmem],
         out_shape=[floats(*field)] * 3 + [jax.ShapeDtypeStruct(plane, jnp.float32)],
         scratch_shapes=[
-            scratch(15, *plane), scratch(*field), scratch(*field),
+            scratch(10, *plane), scratch(rows + 2 * PAD, lanes), scratch(*field), scratch(*field),
             pltpu.SemaphoreType.DMA((2, OUT_PARTS)), pltpu.SemaphoreType.DMA,
         ],
         compiler_params=params,
         name="final",
     )(
-        thickness, near(totals), near(basis), near(depth_wide), near(planes), near(face_west),
-        near(halo), near(fixes), near(east_part), near(north_part), near(tracer_part),
+        thickness, near(totals), near(basis), near(planes), near(limits), near(faces), near(fixes),
+        near(east_part), near(north_part), near(tracer_part),
     )
     return tracer_adj, east_adj, north_adj, surface_adj
 

time: 49.7 us -> 46.8 us (0.942)
  Pallas kernels: 19.8 us -> 16.9 us
    pallas_call x2, Pallas kernels: 7.59 us -> 5.78 us  [the longest x1 4.29 us: local(): pl.pallas_call(final_kernel, in_specs=[scalars] + [in_vmem] * 9, out_spec...]
    pallas_call x1, Pallas kernels: 4.35 us -> 3.27 us  [local(): pl.pallas_call(pack_kernel, in_specs=[in_hbm] * 8, out_specs=[in_vmem] *...]
  transfers between devices with their start and end apart: 4 -> 4, of which waited for: 0 -> 0; matrix products, arithmetic and copies ran while one was open for 0% -> 0% of each run, Pallas kernels for 15% -> 16%
where the time goes in v4:
time: 46.8 us; the launch traced here: 46.6 us
  blocking collectives  21.1 us (45%)
  Pallas kernels  16.9 us (36%)
  starting transfers between devices  7.86 us (17%)
  between operations  0.7 us (1%)
    all_to_all x1, blocking collectives, local(): totals = lax.all_to_all(gram, BOTH, 0, 0, tiled=True)  21.1 us
    pallas_call x1, Pallas kernels, local(): pl.pallas_call(final_kernel, in_specs=[scalars] + [in_vmem] * 9, out_spec...  4.29 us
    pallas_call x1, Pallas kernels, local(): pl.pallas_call(inner_kernel, in_specs=[in_vmem] * 4, out_specs=[in_vmem]...  4.24 us
    ppermute x1, starting transfers between devices, local(): got_b = lax.ppermute(message_b, BOTH, swaps(lats, lons, 1))  3.7 us
    pallas_call x1, Pallas kernels, local(): pl.pallas_call(pack_kernel, in_specs=[in_hbm] * 8, out_specs=[in_vmem] *...  3.27 us
    pallas_call x1, Pallas kernels, local(): pl.pallas_call(rim_kernel, in_specs=[in_vmem] * 9, out_specs=[in_vmem] *...  3.24 us
    ppermute x1, starting transfers between devices, local(): got_0 = lax.ppermute(message_0, 'lon', lon_swaps(lons, 0))  1.5 us
    pallas_call x1, Pallas kernels, local(): pl.pallas_call(basis_kernel, in_specs=[scalars] + [in_vmem] * 7, out_spec...  1.49 us
  transfers between devices with their start and end apart: 4, of which 0 were waited for; matrix products, arithmetic and copies ran while one was open for 0% of the time, Pallas kernels for 16%

profile of v4, /device:TPU:1, one launch (start us, length us, event | category | flops | bytes accessed | tf_op | source)
XLA Modules:
  0.0 46.6 jit_solution(592544079935242189)
XLA Ops:
  0.6 3.3 %pack.1 = (f32[64,256]{1,0:T(8,128)S(1)}, f32[64,256]{1,0:T(8,128)S(1)}, f32[5,64,128]{2,1,0:T(8,128)S(1)}, f32[6,64,128]{2,1,0:T(8,128)S(1)}, f32[3,64,128]{2,1...) custom-call(f32[50,64,128]{2,1,0:T(8,128)} %east_in.1, ...), custom_call_target="tpu_custom_call" | custom-call | tf_op jit(solution)/shard_map/pack/pallas_call | solution.py:663
  3.9 1.5 %collective-permute-start = (f32[64,256]{1,0:T(8,128)S(1)}, f32[64,256]{1,0:T(8,128)S(1)}, u32[]{:S(2)}, u32[]{:S(2)}) collective-permute-start(f32[64,256]{1,0:T(8,128)S(1)} %get-tuple-element.34), channel_id=1, source_target_pairs={{0,1},{1,0},{2,3},{3,2},{4,5},{5,4},{6,7},{7,6},{8,9},{9,8},{10,11... | collective-permute-start | bytes 196616 | tf_op jit(solution)/shard_map/ppermute | solution.py:688
  5.4 1.4 %collective-permute-start.1 = (f32[64,256]{1,0:T(8,128)S(1)}, f32[64,256]{1,0:T(8,128)S(1)}, u32[]{:S(2)}, u32[]{:S(2)}) collective-permute-start(f32[64,256]{1,0:T(8,128)S(1)} %get-tuple-element.35), channel_id=1, source_target_pairs={{0,15},{1,2},{2,1},{3,4},{4,3},{5,6},{6,5},{7,8},{8,7},{9,10},{10,... | collective-permute-start | bytes 196616 | tf_op jit(solution)/shard_map/ppermute | solution.py:687
  6.8 4.2 %inner.1 = (f32[50,64,128]{2,1,0:T(8,128)S(1)}, f32[50,64,128]{2,1,0:T(8,128)S(1)}, f32[50,64,128]{2,1,0:T(8,128)S(1)}) custom-call(f32[5,64,128]{2,1,0:T(8,128)S(1)} %get-tuple-element.36.planes.planes_in, f32[50,64,128]{2,1,0:T(8,128)S(1)} %get-tuple-element.39.east, f32[50,64,128]{2,1,0:T(8,128)S(1)} %get-tuple-element.40.north, ...), custom_call_target="tpu_custom_call" | custom-call | flops 24576000 | bytes 3276800 | tf_op jit(solution)/shard_map/inner/pallas_call | solution.py:690
  11.0 0.0 collective-permute-done.got_0
  11.0 0.0 collective-permute-done.1.got_1
  11.0 0.4 stitch.1
  11.4 1.3 %collective-permute-start.2 = (f32[200,128]{1,0:T(8,128)S(1)}, f32[200,128]{1,0:T(8,128)S(1)}, u32[]{:S(2)}, u32[]{:S(2)}) collective-permute-start(f32[200,128]{1,0:T(8,128)S(1)} %get-tuple-element.44), channel_id=1, source_target_pairs={{0,16},{1,17},{2,18},{3,19},{4,20},{5,21},{6,22},{7,23},{8,24},{9,... | collective-permute-start | bytes 307208 | tf_op jit(solution)/shard_map/ppermute | solution.py:713
  12.7 3.7 %collective-permute-start.3 = (f32[200,128]{1,0:T(8,128)S(1)}, f32[200,128]{1,0:T(8,128)S(1)}, u32[]{:S(2)}, u32[]{:S(2)}) collective-permute-start(f32[200,128]{1,0:T(8,128)S(1)} %get-tuple-element.45), channel_id=1, source_target_pairs={{0,1},{1,0},{2,3},{3,2},{4,5},{5,4},{6,7},{7,6},{8,9},{9,8},{10,11... | collective-permute-start | bytes 307208 | tf_op jit(solution)/shard_map/ppermute | solution.py:712
  16.4 0.0 copy-start
  16.4 3.2 %rim.1 = (f32[50,64,128]{2,1,0:T(8,128)S(1)}, f32[50,64,128]{2,1,0:T(8,128)S(1)}, f32[50,64,128]{2,1,0:T(8,128)S(1)}, f32[5,64,128]{2,1,0:T(8,128)S(1)}, f32[4,64,128]{2,1,0:T(8,128)S(1)}) custom-call(f32[64,256]{1,0:T(8,128)S(1)} %collective-permute-done.got_0, ...), custom_call_target="tpu_custom_call", output_to_operand_aliasing={{0}: (6, {}), {1}: (7, {}), {2}: (8, {})} | custom-call | flops 4096000 | bytes 3276800 | tf_op jit(solution)/shard_map/rim/pallas_call | solution.py:715
  19.7 0.0 collective-permute-done.2.got_a
  19.7 0.0 collective-permute-done.3.got_b
  19.7 0.0 copy-done
  19.7 1.5 %basis.1 = (f32[128,128]{1,0:T(8,128)S(1)}, f32[4,80,256]{2,1,0:T(8,128)S(1)}, f32[6,56,128]{2,1,0:T(8,128)S(1)}, f32[50,64,128]{2,1,0:T(8,128)S(1)}, f32[5,64,1...) custom-call(f32[50]{0:T(128)S(1)} %copy-done, ...), custom_call_target="tpu_custom_call", output_to_operand_aliasing={{3}: (5, {}), {4}: (6, {}), {5}: (7, {})} | custom-call | tf_op jit(solution)/shard_map/basis/pallas_call | solution.py:731
  21.2 21.1 %all_to_all.11 = f32[128,1,128]{2,1,0:T(1,128)S(1)} all-to-all(f32[128,1,128]{2,1,0:T(1,128)S(1)} %bitcast.5), channel_id=1, replica_groups=mesh['lat'=8,'lon'=16] {'lat','lon'}, dimensions={0} | all-to-all | bytes 131072 | tf_op jit(solution)/shard_map/all_to_all | solution.py:748
  42.3 4.3 %final.1 = (f32[50,64,128]{2,1,0:T(8,128)}, f32[50,64,128]{2,1,0:T(8,128)}, f32[50,64,128]{2,1,0:T(8,128)}, f32[64,128]{1,0:T(8,128)}) custom-call(f32[50]{0:T(128)S(1)} %copy-done, f32[128,128]{1,0:T(8,128)S(1)} %bitcast.4, f32[4,80,256]{2,1,0:T(8,128)S(1)} %get-tuple-element.57.basis, f32[5,64,128]{2,1,0:T(8,128)S(1)} %get-tuple-element.36.planes.planes_in, ...), custom_call_target="tpu_custom_call" | custom-call | tf_op jit(solution)/shard_map/final/pallas_call | solution.py:750
Async XLA Ops:
  3.9 7.1 %collective-permute-start = (f32[64,256]{1,0:T(8,128)S(1)}, f32[64,256]{1,0:T(8,128)S(1)}, u32[]{:S(2)}, u32[]{:S(2)}) collective-permute-start(f32[64,256]{1,0:T(8,128)S(1)} %get-tuple-element.34), channel_id=1, source_target_pairs={{0,1},{1,0},{2,3},{3,2},{4,5},{5,4},{6,7},{7,6},{8,9},{9,8},{10,11... | collective-permute-start | bytes 196616 | tf_op jit(solution)/shard_map/ppermute | solution.py:688
  5.4 5.6 %collective-permute-start.1 = (f32[64,256]{1,0:T(8,128)S(1)}, f32[64,256]{1,0:T(8,128)S(1)}, u32[]{:S(2)}, u32[]{:S(2)}) collective-permute-start(f32[64,256]{1,0:T(8,128)S(1)} %get-tuple-element.35), channel_id=1, source_target_pairs={{0,15},{1,2},{2,1},{3,4},{4,3},{5,6},{6,5},{7,8},{8,7},{9,10},{10,... | collective-permute-start | bytes 196616 | tf_op jit(solution)/shard_map/ppermute | solution.py:687
  11.4 8.3 %collective-permute-start.2 = (f32[200,128]{1,0:T(8,128)S(1)}, f32[200,128]{1,0:T(8,128)S(1)}, u32[]{:S(2)}, u32[]{:S(2)}) collective-permute-start(f32[200,128]{1,0:T(8,128)S(1)} %get-tuple-element.44), channel_id=1, source_target_pairs={{0,16},{1,17},{2,18},{3,19},{4,20},{5,21},{6,22},{7,23},{8,24},{9,... | collective-permute-start | bytes 307208 | tf_op jit(solution)/shard_map/ppermute | solution.py:713
  12.7 7.0 %collective-permute-start.3 = (f32[200,128]{1,0:T(8,128)S(1)}, f32[200,128]{1,0:T(8,128)S(1)}, u32[]{:S(2)}, u32[]{:S(2)}) collective-permute-start(f32[200,128]{1,0:T(8,128)S(1)} %get-tuple-element.45), channel_id=1, source_target_pairs={{0,1},{1,0},{2,3},{3,2},{4,5},{5,4},{6,7},{7,6},{8,9},{9,8},{10,11... | collective-permute-start | bytes 307208 | tf_op jit(solution)/shard_map/ppermute | solution.py:712
  16.4 3.3 %copy-start = (f32[50]{0:T(128)S(1)}, f32[50]{0:T(128)}, u32[]{:S(2)}) copy-start(f32[50]{0:T(128)} %thickness.3) | copy-start | bytes 604

commit v5 on v4

--- a/solution.py
+++ b/solution.py
@@ -9,10 +9,10 @@
 PAD = 8
 SHIFTS = (1.0, 0.3, 1.7)
 PARTS = 5
-OUT_PARTS = 10
+OUT_PARTS = 5
 LANES = 128
 GROUP = 5
-TILES = 4
+TILES = 8
 BOTH = ("lat", "lon")
 VMEM_BYTES = 32 * 1024 * 1024
 
@@ -111,36 +111,39 @@
         moved = turn(values, place - start, 1)
         return jnp.where((lane >= place) & (lane < place + count), moved, target)
 
+    half = rows // 2
+
     def fill(ref, eastward):
         if eastward:
-            ref[:, :lanes] = jnp.where(odd_lane, turn(edges[1], 1, 1), edges[0])
+            tile = jnp.where(odd_lane, turn(edges[1], 1, 1), edges[0])
+            ref[rows:] = jnp.where(odd_lane[half:], turn(edges[2, half:], 1, 1), edges[2, :half])
         else:
-            ref[:, :lanes] = jnp.where(odd_lane, edges[0], turn(edges[1], -1, 1))
+            tile = jnp.where(odd_lane, edges[0], turn(edges[1], -1, 1))
+            ref[rows:] = jnp.where(odd_lane[half:], edges[2, :half], turn(edges[2, half:], -1, 1))
         start = lanes - WIDE if eastward else 0
-        tile = edges[2]
         for values, place in (
             (deep, DEPTH_AT), (planes[1], STORE_AT), (plane, SOURCE_AT), (rows_out[1], STRIP_AT)
         ):
             tile = put(tile, values, start, place, WIDE)
-        ref[:, lanes:] = put(tile, planes[2], lanes - 1, DIFF_AT, 1)
-
-    even = lax.rem(lax.axis_index("lon"), 2) == 0
-
-    @pl.when(even)
+        ref[:rows] = put(tile, planes[2], lanes - 1, DIFF_AT, 1)
+
+    odd = lax.rem(lax.axis_index("lon"), 2) == 1
+
+    @pl.when(odd)
     def _():
         fill(message_0, True)
         fill(message_1, False)
 
-    @pl.when(jnp.logical_not(even))
+    @pl.when(jnp.logical_not(odd))
     def _():
         fill(message_0, False)
         fill(message_1, True)
 
 
 def received(got_0, got_1):
-    even = lax.rem(lax.axis_index("lon"), 2) == 0
+    odd = lax.rem(lax.axis_index("lon"), 2) == 1
     one, two = got_0[...], got_1[...]
-    return jnp.where(even, two, one), jnp.where(even, one, two)
+    return jnp.where(odd, two, one), jnp.where(odd, one, two)
 
 
 def stitch_kernel(
@@ -150,7 +153,7 @@
     rows, lanes = planes.shape[1:]
     from_west, from_east = received(got_0, got_1)
     lane = iota((rows, lanes), 1)
-    left_tile, right_tile = from_west[:, lanes:], from_east[:, lanes:]
+    left_tile, right_tile = from_west[:rows], from_east[:rows]
 
     def side(place):
         right = turn(right_tile, -place, 1)
@@ -169,7 +172,7 @@
         return jnp.sum(jnp.where(used, values, 0.0), axis=1, keepdims=True)
 
     flux_east = flux(edges[0], jnp.minimum(deep[:, lanes - 1 :], deep_side[:, 0:1]))
-    flux_west = flux(from_west[:, :lanes], jnp.minimum(deep_side[:, lanes - 1 :], deep[:, 0:1]))
+    flux_west = flux(left_tile, jnp.minimum(deep_side[:, lanes - 1 :], deep[:, 0:1]))
     first, last = lane == 0, lane == lanes - 1
     plane = plane + jnp.where(last, flux_east, 0.0) - jnp.where(first, flux_west, 0.0)
     plane_side = plane_side - jnp.where(first, flux_east, 0.0) + jnp.where(last, flux_west, 0.0)
@@ -305,10 +308,19 @@
     bound_west = jnp.minimum(deep[:, 0:1], beside[:, lanes - 1 :])
     weight = jnp.where(odd_lane, face_west[:, 0:1], planes[2, :, lanes - 1 :])
     weight = jnp.where(level_of < jnp.where(odd_lane, bound_west, bound_east), weight, 0.0)
+    left, right = from_west[:rows], from_east[:rows]
+    left_half, right_half = from_west[rows:], from_east[rows:]
+    half = odd_lane[: rows // 2]
     halos = (
-        jnp.where(odd_lane, turn(from_west[:, :lanes], 1, 1), turn(from_east[:, :lanes], -1, 1)),
-        jnp.where(odd_lane, from_west[:, :lanes], from_east[:, :lanes]),
-        jnp.where(odd_lane, turn(from_west[:, lanes:], 1, 1), turn(from_east[:, lanes:], -1, 1)),
+        jnp.where(odd_lane, turn(left, 1, 1), turn(right, -1, 1)),
+        jnp.where(odd_lane, left, right),
+        jnp.concatenate(
+            [
+                jnp.where(half, turn(left_half, 1, 1), turn(right_half, -1, 1)),
+                jnp.where(half, left_half, right_half),
+            ],
+            axis=0,
+        ),
     )
     for number in range(3):
         sides[number] = turn(weight * (halos[number] - edges[number]), -1, 1)
@@ -521,7 +533,7 @@
 def final_kernel(
     thickness, totals, basis, planes_in, limits, faces, fixes, east, north, tracer,
     tracer_hbm, east_hbm, north_hbm, surface,
-    planes, work, east_out, north_out, sems, tracer_sem,
+    planes, bounds_at, work, east_out, north_out, sems, tracer_sem,
 ):
     levels, rows, lanes = east.shape
     size = levels // OUT_PARTS
@@ -583,24 +595,51 @@
         for number, item in enumerate(sides):
             planes[start + number] = faces[number] * (own - item)
 
+    for tile in range(rows // PAD):
+        place = slice(tile * PAD, (tile + 1) * PAD)
+        keys = [limits[1 + number, place] for number in range(4)]
+        sides_of = [[planes[start + number, place] for number in range(4)] for start in (2, 6)]
+        for one, two in ((0, 1), (2, 3), (0, 2), (1, 3), (1, 2)):
+            swap = keys[one] > keys[two]
+            keys[one], keys[two] = (
+                jnp.minimum(keys[one], keys[two]), jnp.maximum(keys[one], keys[two])
+            )
+            for item in sides_of:
+                item[one], item[two] = (
+                    jnp.where(swap, item[two], item[one]),
+                    jnp.where(swap, item[one], item[two]),
+                )
+        for number in range(4):
+            bounds_at[number, place] = keys[number]
+            planes[2 + number, place] = sides_of[0][number]
+            planes[6 + number, place] = sides_of[1][number]
+
     line = iota((PAD, lanes), 0)
     first_line, last_line = line == 0, line == PAD - 1
 
     def part_step(part, carry):
         for tile in range(rows // PAD):
             place = slice(tile * PAD, (tile + 1) * PAD)
-            bounds = [limits[number, place] for number in range(5)]
-            own = [planes[number, place] for number in range(10)]
+            keys = [bounds_at[number, place] for number in range(4)] + [limits[0, place]]
+            keys = [jnp.maximum(key, 0.0) for key in keys]
+            sums = []
+            for start in (0, 1):
+                line_of = [planes[start, place]]
+                for number in range(3, -1, -1):
+                    line_of.append(line_of[-1] - planes[2 + 4 * start + number, place])
+                sums.append(line_of)
             for t in range(size):
                 level = part * size + t
                 height = level.astype(jnp.float32)
-                open_sides = [height < bound for bound in bounds]
-                for out, values, base, start, number in (
-                    (east_out, east, 0, 2, 0), (north_out, north, 1, 6, 1)
-                ):
-                    change = jnp.where(open_sides[0], own[base], 0.0)
-                    for side in range(4):
-                        change = change - jnp.where(open_sides[1 + side], own[start + side], 0.0)
+                changes = [0.0, 0.0]
+                for side in range(5):
+                    open_side = height < keys[4 - side]
+                    changes = [
+                        jnp.where(open_side, sums[number][side], changes[number])
+                        for number in range(2)
+                    ]
+                for out, values, number in ((east_out, east, 0), (north_out, north, 1)):
+                    change = changes[number]
                     result = values[level, place] + thickness[level] * change
                     if tile == 0:
                         fix = fixes[3 + number, pl.ds(level, 1), :]
@@ -657,6 +696,7 @@
         transcendentals=0,
     )
     plane, pair, field = (rows, lanes), (rows, 2 * lanes), (levels, rows, lanes)
+    columns = (rows + rows // 2, lanes)
     full = (rows + 2 * PAD, 2 * lanes)
     message, strips = (MESSAGE_ROWS, lanes), (2, HALO_ROWS, 2 * lanes)
 
@@ -665,7 +705,7 @@
         in_specs=[in_hbm] * 8,
         out_specs=[in_vmem] * 8,
         out_shape=[
-            scratch(*pair), scratch(*pair), scratch(5, *plane), scratch(6, *plane),
+            scratch(*columns), scratch(*columns), scratch(5, *plane), scratch(6, *plane),
             scratch(3, *plane), scratch(*field), scratch(*field), scratch(*field),
         ],
         scratch_shapes=[
@@ -684,8 +724,8 @@
         ]
     )
 
-    got_1 = lax.ppermute(message_1, "lon", lon_swaps(lons, 1))
-    got_0 = lax.ppermute(message_0, "lon", lon_swaps(lons, 0))
+    got_1 = lax.ppermute(message_1, "lon", lon_swaps(lons, 0))
+    got_0 = lax.ppermute(message_0, "lon", lon_swaps(lons, 1))
 
     east_part, north_part, tracer_part = pl.pallas_call(
         inner_kernel,
@@ -753,7 +793,7 @@
         out_specs=[in_hbm] * 3 + [in_vmem],
         out_shape=[floats(*field)] * 3 + [jax.ShapeDtypeStruct(plane, jnp.float32)],
         scratch_shapes=[
-            scratch(10, *plane), scratch(rows + 2 * PAD, lanes), scratch(*field), scratch(*field),
+            scratch(10, *plane), scratch(4, *plane), scratch(rows + 2 * PAD, lanes), scratch(*field), scratch(*field),
             pltpu.SemaphoreType.DMA((2, OUT_PARTS)), pltpu.SemaphoreType.DMA,
         ],
         compiler_params=params,

time: 46.8 us -> 45.8 us (0.979)
  Pallas kernels: 16.9 us -> 15.3 us
  waiting for transfers between devices: 0.01 us -> 1.32 us
  starting transfers between devices: 7.86 us -> 7.19 us
    ppermute x2, starting transfers between devices: 2.86 us -> 6.5 us  [the longest x1 3.73 us: local(): got_1 = lax.ppermute(message_1, 'lon', lon_swaps(lons, 0))]
    ppermute x1, starting transfers between devices: 3.7 us -> 0.28 us  [local(): got_b = lax.ppermute(message_b, BOTH, swaps(lats, lons, 1))]
    ppermute x1, waiting for transfers between devices: 0.01 us -> 1.31 us  [local(): got_a = lax.ppermute(message_a, BOTH, swaps(lats, lons, 0))]
    ppermute x1, starting transfers between devices: 1.31 us -> 0.41 us  [local(): got_a = lax.ppermute(message_a, BOTH, swaps(lats, lons, 0))]
    pallas_call x1, Pallas kernels: 3.24 us -> 2.57 us  [local(): pl.pallas_call(rim_kernel, in_specs=[in_vmem] * 9, out_specs=[in_vmem] *...]
    pallas_call x1, Pallas kernels: 4.24 us -> 3.7 us  [local(): pl.pallas_call(inner_kernel, in_specs=[in_vmem] * 4, out_specs=[in_vmem]...]
  transfers between devices with their start and end apart: 4 -> 4, of which waited for: 0 -> 1; matrix products, arithmetic and copies ran while one was open for 0% -> 0% of each run, Pallas kernels for 16% -> 14%
where the time goes in v5:
time: 45.8 us; the launch traced here: 45.7 us
  blocking collectives  21.2 us (46%)
  Pallas kernels  15.3 us (33%)
  starting transfers between devices  7.19 us (16%)
  waiting for transfers between devices  1.32 us (3%)
  between operations  0.68 us (1%)
    all_to_all x1, blocking collectives, local(): totals = lax.all_to_all(gram, BOTH, 0, 0, tiled=True)  21.2 us
    pallas_call x1, Pallas kernels, local(): pl.pallas_call(final_kernel, in_specs=[scalars] + [in_vmem] * 9, out_spec...  3.87 us
    ppermute x1, starting transfers between devices, local(): got_1 = lax.ppermute(message_1, 'lon', lon_swaps(lons, 0))  3.73 us
    pallas_call x1, Pallas kernels, local(): pl.pallas_call(inner_kernel, in_specs=[in_vmem] * 4, out_specs=[in_vmem]...  3.7 us
    pallas_call x1, Pallas kernels, local(): pl.pallas_call(pack_kernel, in_specs=[in_hbm] * 8, out_specs=[in_vmem] *...  3.28 us
    ppermute x1, starting transfers between devices, local(): got_0 = lax.ppermute(message_0, 'lon', lon_swaps(lons, 1))  2.77 us
    pallas_call x1, Pallas kernels, local(): pl.pallas_call(rim_kernel, in_specs=[in_vmem] * 9, out_specs=[in_vmem] *...  2.57 us
    pallas_call x1, Pallas kernels, local(): pl.pallas_call(basis_kernel, in_specs=[scalars] + [in_vmem] * 7, out_spec...  1.49 us
  transfers between devices with their start and end apart: 4, of which 1 were waited for; matrix products, arithmetic and copies ran while one was open for 0% of the time, Pallas kernels for 14%

profile of v5, /device:TPU:1, one launch (start us, length us, event | category | flops | bytes accessed | tf_op | source)
XLA Modules:
  0.0 45.7 jit_solution(2463284065203748664)
XLA Ops:
  0.6 3.3 %pack.1 = (f32[96,128]{1,0:T(8,128)S(1)}, f32[96,128]{1,0:T(8,128)S(1)}, f32[5,64,128]{2,1,0:T(8,128)S(1)}, f32[6,64,128]{2,1,0:T(8,128)S(1)}, f32[3,64,128]{2,1...) custom-call(f32[50,64,128]{2,1,0:T(8,128)} %east_in.1, ...), custom_call_target="tpu_custom_call" | custom-call | tf_op jit(solution)/shard_map/pack/pallas_call | solution.py:703
  3.9 2.8 %collective-permute-start = (f32[96,128]{1,0:T(8,128)S(1)}, f32[96,128]{1,0:T(8,128)S(1)}, u32[]{:S(2)}, u32[]{:S(2)}) collective-permute-start(f32[96,128]{1,0:T(8,128)S(1)} %get-tuple-element.34), channel_id=1, source_target_pairs={{0,15},{1,2},{2,1},{3,4},{4,3},{5,6},{6,5},{7,8},{8,7},{9,10},{10,... | collective-permute-start | bytes 147464 | tf_op jit(solution)/shard_map/ppermute | solution.py:728
  6.7 3.7 %collective-permute-start.1 = (f32[96,128]{1,0:T(8,128)S(1)}, f32[96,128]{1,0:T(8,128)S(1)}, u32[]{:S(2)}, u32[]{:S(2)}) collective-permute-start(f32[96,128]{1,0:T(8,128)S(1)} %get-tuple-element.35), channel_id=1, source_target_pairs={{0,1},{1,0},{2,3},{3,2},{4,5},{5,4},{6,7},{7,6},{8,9},{9,8},{10,11... | collective-permute-start | bytes 147464 | tf_op jit(solution)/shard_map/ppermute | solution.py:727
  10.4 3.7 %inner.1 = (f32[50,64,128]{2,1,0:T(8,128)S(1)}, f32[50,64,128]{2,1,0:T(8,128)S(1)}, f32[50,64,128]{2,1,0:T(8,128)S(1)}) custom-call(f32[5,64,128]{2,1,0:T(8,128)S(1)} %get-tuple-element.36.planes.planes_in, f32[50,64,128]{2,1,0:T(8,128)S(1)} %get-tuple-element.39.east, f32[50,64,128]{2,1,0:T(8,128)S(1)} %get-tuple-element.40.north, ...), custom_call_target="tpu_custom_call" | custom-call | flops 24576000 | bytes 3276800 | tf_op jit(solution)/shard_map/inner/pallas_call | solution.py:730
  14.1 0.0 collective-permute-done.got_0
  14.1 0.0 collective-permute-done.1.got_1
  14.2 0.4 stitch.1
  14.5 0.4 collective-permute-start.2
  15.0 0.3 collective-permute-start.3
  15.2 0.0 copy-start
  15.2 2.6 %rim.1 = (f32[50,64,128]{2,1,0:T(8,128)S(1)}, f32[50,64,128]{2,1,0:T(8,128)S(1)}, f32[50,64,128]{2,1,0:T(8,128)S(1)}, f32[5,64,128]{2,1,0:T(8,128)S(1)}, f32[4,64,128]{2,1,0:T(8,128)S(1)}) custom-call(f32[96,128]{1,0:T(8,128)S(1)} %collective-permute-done.got_0, ...), custom_call_target="tpu_custom_call", output_to_operand_aliasing={{0}: (6, {}), {1}: (7, {}), {2}: (8, {})} | custom-call | flops 4096000 | bytes 3276800 | tf_op jit(solution)/shard_map/rim/pallas_call | solution.py:755
  17.8 1.3 %collective-permute-done.2.got_a = f32[200,128]{1,0:T(8,128)S(1)} collective-permute-done((f32[200,128]{1,0:T(8,128)S(1)}, f32[200,128]{1,0:T(8,128)S(1)}, u32[]{:S(2)}, u32[]{:S(2)}) %collective-permute-start.2) | collective-permute-done | bytes 102432 | tf_op jit(solution)/shard_map/ppermute | solution.py:753
  19.1 0.0 collective-permute-done.3.got_b
  19.1 0.0 copy-done
  19.1 1.5 %basis.1 = (f32[128,128]{1,0:T(8,128)S(1)}, f32[4,80,256]{2,1,0:T(8,128)S(1)}, f32[6,56,128]{2,1,0:T(8,128)S(1)}, f32[50,64,128]{2,1,0:T(8,128)S(1)}, f32[5,64,1...) custom-call(f32[50]{0:T(128)S(1)} %copy-done, ...), custom_call_target="tpu_custom_call", output_to_operand_aliasing={{3}: (5, {}), {4}: (6, {}), {5}: (7, {})} | custom-call | tf_op jit(solution)/shard_map/basis/pallas_call | solution.py:771
  20.6 21.2 %all_to_all.11 = f32[128,1,128]{2,1,0:T(1,128)S(1)} all-to-all(f32[128,1,128]{2,1,0:T(1,128)S(1)} %bitcast.5), channel_id=1, replica_groups=mesh['lat'=8,'lon'=16] {'lat','lon'}, dimensions={0} | all-to-all | bytes 131072 | tf_op jit(solution)/shard_map/all_to_all | solution.py:788
  41.8 3.9 %final.1 = (f32[50,64,128]{2,1,0:T(8,128)}, f32[50,64,128]{2,1,0:T(8,128)}, f32[50,64,128]{2,1,0:T(8,128)}, f32[64,128]{1,0:T(8,128)}) custom-call(f32[50]{0:T(128)S(1)} %copy-done, f32[128,128]{1,0:T(8,128)S(1)} %bitcast.4, f32[4,80,256]{2,1,0:T(8,128)S(1)} %get-tuple-element.57.basis, f32[5,64,128]{2,1,0:T(8,128)S(1)} %get-tuple-element.36.planes.planes_in, ...), custom_call_target="tpu_custom_call" | custom-call | tf_op jit(solution)/shard_map/final/pallas_call | solution.py:790
Async XLA Ops:
  3.9 10.2 %collective-permute-start = (f32[96,128]{1,0:T(8,128)S(1)}, f32[96,128]{1,0:T(8,128)S(1)}, u32[]{:S(2)}, u32[]{:S(2)}) collective-permute-start(f32[96,128]{1,0:T(8,128)S(1)} %get-tuple-element.34), channel_id=1, source_target_pairs={{0,15},{1,2},{2,1},{3,4},{4,3},{5,6},{6,5},{7,8},{8,7},{9,10},{10,... | collective-permute-start | bytes 147464 | tf_op jit(solution)/shard_map/ppermute | solution.py:728
  6.7 7.5 %collective-permute-start.1 = (f32[96,128]{1,0:T(8,128)S(1)}, f32[96,128]{1,0:T(8,128)S(1)}, u32[]{:S(2)}, u32[]{:S(2)}) collective-permute-start(f32[96,128]{1,0:T(8,128)S(1)} %get-tuple-element.35), channel_id=1, source_target_pairs={{0,1},{1,0},{2,3},{3,2},{4,5},{5,4},{6,7},{7,6},{8,9},{9,8},{10,11... | collective-permute-start | bytes 147464 | tf_op jit(solution)/shard_map/ppermute | solution.py:727
  14.5 4.6 %collective-permute-start.2 = (f32[200,128]{1,0:T(8,128)S(1)}, f32[200,128]{1,0:T(8,128)S(1)}, u32[]{:S(2)}, u32[]{:S(2)}) collective-permute-start(f32[200,128]{1,0:T(8,128)S(1)} %get-tuple-element.44), channel_id=1, source_target_pairs={{0,16},{1,17},{2,18},{3,19},{4,20},{5,21},{6,22},{7,23},{8,24},{9,... | collective-permute-start | bytes 307208 | tf_op jit(solution)/shard_map/ppermute | solution.py:753
  15.0 4.2 %collective-permute-start.3 = (f32[200,128]{1,0:T(8,128)S(1)}, f32[200,128]{1,0:T(8,128)S(1)}, u32[]{:S(2)}, u32[]{:S(2)}) collective-permute-start(f32[200,128]{1,0:T(8,128)S(1)} %get-tuple-element.45), channel_id=1, source_target_pairs={{0,1},{1,0},{2,3},{3,2},{4,5},{5,4},{6,7},{7,6},{8,9},{9,8},{10,11... | collective-permute-start | bytes 307208 | tf_op jit(solution)/shard_map/ppermute | solution.py:752
  15.2 3.9 %copy-start = (f32[50]{0:T(128)S(1)}, f32[50]{0:T(128)}, u32[]{:S(2)}) copy-start(f32[50]{0:T(128)} %thickness.3) | copy-start | bytes 604

commit v6 on v5

--- a/solution.py
+++ b/solution.py
@@ -285,8 +285,8 @@
 
 
 def rim_kernel(
-    got_0, got_1, wide, planes, face_west, edges, east, north, tracer,
-    east_out, north_out, tracer_out, limits, faces,
+    thickness, got_0, got_1, wide, planes, face_west, edges, east, north, tracer,
+    east_out, north_out, tracer_out, limits, faces, depths,
     sides,
 ):
     levels, rows, lanes = east.shape
@@ -295,6 +295,11 @@
     deep, beside = wide[0, :, :lanes], wide[0, :, lanes:]
     level_of = lax.shift_right_logical(lane, 1).astype(jnp.float32)
     odd_lane = lax.rem(lane, 2) == 1
+    place = iota((PAD, lanes), 1)
+    table = jnp.zeros((PAD, lanes), jnp.float32)
+    for number in range(levels):
+        table = table + jnp.where(place > number, thickness[number], 0.0)
+    depths[...] = table
     limits[0] = deep
     limits[1] = jnp.minimum(deep, jnp.where(lane == lanes - 1, beside[:, 0:1], turn(deep, -1, 1)))
     limits[2] = jnp.minimum(deep, jnp.where(lane == 0, beside[:, lanes - 1 :], turn(deep, 1, 1)))
@@ -350,9 +355,9 @@
 
 
 def basis_kernel(
-    thickness, got_a, got_b, wide, rows_in, tracer_in, limits_in, faces_in,
+    depths, got_a, got_b, wide, rows_in, tracer_in, limits_in, faces_in,
     gram, basis, fixes, tracer, limits, faces,
-    halo,
+    halo, work,
 ):
     rows, lanes = wide.shape[1], wide.shape[2] // 2
     lat = lax.axis_index("lat")
@@ -418,10 +423,7 @@
     flux = jnp.sum(jnp.where(level < bound, halo[1, RAW_AT:PAIR_AT], 0.0), axis=0, keepdims=True)
     plane = plane + jnp.where(row == PAD - 1, flux, 0.0) - jnp.where(row == PAD, flux, 0.0)
 
-    place = iota((PAD, lanes), 1)
-    table = jnp.zeros((PAD, lanes), jnp.float32)
-    for number in range(thickness.shape[0]):
-        table = table + jnp.where(place > number, thickness[number], 0.0)
+    table = depths[...]
 
     def column(bound):
         index = bound.astype(jnp.int32)
@@ -451,12 +453,20 @@
     inverse = jnp.where(there, 1.0 / jnp.where(there, diag, 1.0), 0.0)
 
     def operate(values):
-        east_side, west_side, north_side, south_side = shifted(values)
+        for tile in range(2):
+            work[tile, PAD : PAD + full[0]] = values[:, tile * lanes : (tile + 1) * lanes]
+        north_side, south_side = [
+            jnp.concatenate([work[tile, start : start + full[0]] for tile in range(2)], axis=1)
+            for start in (PAD + 1, PAD - 1)
+        ]
+        east_side, west_side = turn(values, -1, 1), turn(values, 1, 1)
         total = (
             store * values + to_east * (values - east_side) + to_west * (values - west_side)
         )
         return total + to_north * (values - north_side) + to_south * (values - south_side)
 
+    for start in (0, PAD + full[0]):
+        work[:, start : start + PAD] = jnp.zeros((2, PAD, lanes), jnp.float32)
     vectors, images = [plane * inverse], []
     for number in range(4):
         images.append(operate(vectors[-1]))
@@ -752,36 +762,37 @@
     got_b = lax.ppermute(message_b, BOTH, swaps(lats, lons, 1))
     got_a = lax.ppermute(message_a, BOTH, swaps(lats, lons, 0))
 
-    east_part, north_part, tracer_part, limits, faces = pl.pallas_call(
+    east_part, north_part, tracer_part, limits, faces, depths = pl.pallas_call(
         rim_kernel,
-        in_specs=[in_vmem] * 9,
-        out_specs=[in_vmem] * 5,
-        out_shape=[scratch(*field)] * 3 + [scratch(5, *plane), scratch(4, *plane)],
+        in_specs=[scalars] + [in_vmem] * 9,
+        out_specs=[in_vmem] * 6,
+        out_shape=[scratch(*field)] * 3
+        + [scratch(5, *plane), scratch(4, *plane), scratch(PAD, lanes)],
         scratch_shapes=[scratch(3, *plane)],
-        input_output_aliases={6: 0, 7: 1, 8: 2},
+        input_output_aliases={7: 0, 8: 1, 9: 2},
         compiler_params=params,
         cost_estimate=cost(10),
         name="rim",
     )(
-        got_0, got_1, near(wide), near(planes), near(face_west), near(edges), near(east_part),
+        thickness, got_0, got_1, near(wide), near(planes), near(face_west), near(edges), near(east_part),
         near(north_part), near(tracer_part),
     )
 
     wide, east_part = lax.optimization_barrier((wide, east_part))
     gram, basis, fixes, tracer_part, limits, faces = pl.pallas_call(
         basis_kernel,
-        in_specs=[scalars] + [in_vmem] * 7,
+        in_specs=[in_vmem] * 8,
         out_specs=[in_vmem] * 6,
         out_shape=[
             scratch(lats * lons, lanes), scratch(4, *full), scratch(6, LEVEL_ROWS, lanes),
             scratch(*field), scratch(5, *plane), scratch(4, *plane),
         ],
-        scratch_shapes=[scratch(*strips)],
+        scratch_shapes=[scratch(*strips), scratch(2, rows + 4 * PAD, lanes)],
         input_output_aliases={5: 3, 6: 4, 7: 5},
         compiler_params=params,
         name="basis",
     )(
-        thickness, near(got_a), near(got_b), near(wide), near(edge_rows), near(tracer_part),
+        near(depths), near(got_a), near(got_b), near(wide), near(edge_rows), near(tracer_part),
         near(limits), near(faces),
     )
 

time: 45.8 us -> 45.2 us (0.987)
  waiting for transfers between devices: 1.32 us -> 0.78 us
    ppermute x1, waiting for transfers between devices: 1.31 us -> 0.77 us  [local(): got_a = lax.ppermute(message_a, BOTH, swaps(lats, lons, 0))]
  transfers between devices with their start and end apart: 4 -> 4, of which waited for: 1 -> 1; matrix products, arithmetic and copies ran while one was open for 0% -> 0% of each run, Pallas kernels for 14% -> 15%
where the time goes in v6:
time: 45.2 us; the launch traced here: 45.1 us
  blocking collectives  21.2 us (47%)
  Pallas kernels  15.3 us (34%)
  starting transfers between devices  7.19 us (16%)
  waiting for transfers between devices  0.78 us (2%)
  between operations  0.68 us (2%)
    all_to_all x1, blocking collectives, local(): totals = lax.all_to_all(gram, BOTH, 0, 0, tiled=True)  21.2 us
    pallas_call x1, Pallas kernels, local(): pl.pallas_call(final_kernel, in_specs=[scalars] + [in_vmem] * 9, out_spec...  3.87 us
    ppermute x1, starting transfers between devices, local(): got_1 = lax.ppermute(message_1, 'lon', lon_swaps(lons, 0))  3.73 us
    pallas_call x1, Pallas kernels, local(): pl.pallas_call(inner_kernel, in_specs=[in_vmem] * 4, out_specs=[in_vmem]...  3.7 us
    pallas_call x1, Pallas kernels, local(): pl.pallas_call(pack_kernel, in_specs=[in_hbm] * 8, out_specs=[in_vmem] *...  3.28 us
    pallas_call x1, Pallas kernels, local(): pl.pallas_call(rim_kernel, in_specs=[scalars] + [in_vmem] * 9, out_specs=...  3.12 us
    ppermute x1, starting transfers between devices, local(): got_0 = lax.ppermute(message_0, 'lon', lon_swaps(lons, 1))  2.77 us
  transfers between devices with their start and end apart: 4, of which 1 were waited for; matrix products, arithmetic and copies ran while one was open for 0% of the time, Pallas kernels for 15%

profile of v6, /device:TPU:1, one launch (start us, length us, event | category | flops | bytes accessed | tf_op | source)
XLA Modules:
  0.0 45.1 jit_solution(17805851909571159674)
XLA Ops:
  0.6 3.3 %pack.1 = (f32[96,128]{1,0:T(8,128)S(1)}, f32[96,128]{1,0:T(8,128)S(1)}, f32[5,64,128]{2,1,0:T(8,128)S(1)}, f32[6,64,128]{2,1,0:T(8,128)S(1)}, f32[3,64,128]{2,1...) custom-call(f32[50,64,128]{2,1,0:T(8,128)} %east_in.1, ...), custom_call_target="tpu_custom_call" | custom-call | tf_op jit(solution)/shard_map/pack/pallas_call | solution.py:713
  3.9 2.8 %collective-permute-start = (f32[96,128]{1,0:T(8,128)S(1)}, f32[96,128]{1,0:T(8,128)S(1)}, u32[]{:S(2)}, u32[]{:S(2)}) collective-permute-start(f32[96,128]{1,0:T(8,128)S(1)} %get-tuple-element.35), channel_id=1, source_target_pairs={{0,15},{1,2},{2,1},{3,4},{4,3},{5,6},{6,5},{7,8},{8,7},{9,10},{10,... | collective-permute-start | bytes 147464 | tf_op jit(solution)/shard_map/ppermute | solution.py:738
  6.7 3.7 %collective-permute-start.1 = (f32[96,128]{1,0:T(8,128)S(1)}, f32[96,128]{1,0:T(8,128)S(1)}, u32[]{:S(2)}, u32[]{:S(2)}) collective-permute-start(f32[96,128]{1,0:T(8,128)S(1)} %get-tuple-element.36), channel_id=1, source_target_pairs={{0,1},{1,0},{2,3},{3,2},{4,5},{5,4},{6,7},{7,6},{8,9},{9,8},{10,11... | collective-permute-start | bytes 147464 | tf_op jit(solution)/shard_map/ppermute | solution.py:737
  10.4 0.0 copy-start
  10.4 3.7 %inner.1 = (f32[50,64,128]{2,1,0:T(8,128)S(1)}, f32[50,64,128]{2,1,0:T(8,128)S(1)}, f32[50,64,128]{2,1,0:T(8,128)S(1)}) custom-call(f32[5,64,128]{2,1,0:T(8,128)S(1)} %get-tuple-element.37.planes.planes_in, f32[50,64,128]{2,1,0:T(8,128)S(1)} %get-tuple-element.40.east, f32[50,64,128]{2,1,0:T(8,128)S(1)} %get-tuple-element.41.north, ...), custom_call_target="tpu_custom_call" | custom-call | flops 24576000 | bytes 3276800 | tf_op jit(solution)/shard_map/inner/pallas_call | solution.py:740
  14.1 0.0 collective-permute-done.got_0
  14.1 0.0 collective-permute-done.1.got_1
  14.2 0.4 stitch.1
  14.5 0.4 collective-permute-start.2
  15.0 0.3 collective-permute-start.3
  15.2 0.0 copy-done
  15.2 3.1 %rim.1 = (f32[50,64,128]{2,1,0:T(8,128)S(1)}, f32[50,64,128]{2,1,0:T(8,128)S(1)}, f32[50,64,128]{2,1,0:T(8,128)S(1)}, f32[5,64,128]{2,1,0:T(8,128)S(1)}, f32[4,6...) custom-call(f32[50]{0:T(128)S(1)} %copy-done, ...), custom_call_target="tpu_custom_call", output_to_operand_aliasing={{0}: (7, {}), {1}: (8, {}), {2}: (9, {})} | custom-call | flops 4096000 | bytes 3276800 | tf_op jit(solution)/shard_map/rim/pallas_call | solution.py:765
  18.4 0.8 %collective-permute-done.2.got_a = f32[200,128]{1,0:T(8,128)S(1)} collective-permute-done((f32[200,128]{1,0:T(8,128)S(1)}, f32[200,128]{1,0:T(8,128)S(1)}, u32[]{:S(2)}, u32[]{:S(2)}) %collective-permute-start.2) | collective-permute-done | bytes 102432 | tf_op jit(solution)/shard_map/ppermute | solution.py:763
  19.1 0.0 collective-permute-done.3.got_b
  19.1 0.9 %basis.1 = (f32[128,128]{1,0:T(8,128)S(1)}, f32[4,80,256]{2,1,0:T(8,128)S(1)}, f32[6,56,128]{2,1,0:T(8,128)S(1)}, f32[50,64,128]{2,1,0:T(8,128)S(1)}, f32[5,64,1...) custom-call(f32[8,128]{1,0:T(8,128)S(1)} %get-tuple-element.50.depths, ...), custom_call_target="tpu_custom_call", output_to_operand_aliasing={{3}: (5, {}), {4}: (6, {}), {5}: (7, {})} | custom-call | tf_op jit(solution)/shard_map/basis/pallas_call | solution.py:782
  20.0 21.2 %all_to_all.11 = f32[128,1,128]{2,1,0:T(1,128)S(1)} all-to-all(f32[128,1,128]{2,1,0:T(1,128)S(1)} %bitcast.5), channel_id=1, replica_groups=mesh['lat'=8,'lon'=16] {'lat','lon'}, dimensions={0} | all-to-all | bytes 131072 | tf_op jit(solution)/shard_map/all_to_all | solution.py:799
  41.2 3.9 %final.1 = (f32[50,64,128]{2,1,0:T(8,128)}, f32[50,64,128]{2,1,0:T(8,128)}, f32[50,64,128]{2,1,0:T(8,128)}, f32[64,128]{1,0:T(8,128)}) custom-call(f32[50]{0:T(128)S(1)} %copy-done, f32[128,128]{1,0:T(8,128)S(1)} %bitcast.4, f32[4,80,256]{2,1,0:T(8,128)S(1)} %get-tuple-element.59.basis, f32[5,64,128]{2,1,0:T(8,128)S(1)} %get-tuple-element.37.planes.planes_in, ...), custom_call_target="tpu_custom_call" | custom-call | tf_op jit(solution)/shard_map/final/pallas_call | solution.py:801
Async XLA Ops:
  3.9 10.2 %collective-permute-start = (f32[96,128]{1,0:T(8,128)S(1)}, f32[96,128]{1,0:T(8,128)S(1)}, u32[]{:S(2)}, u32[]{:S(2)}) collective-permute-start(f32[96,128]{1,0:T(8,128)S(1)} %get-tuple-element.35), channel_id=1, source_target_pairs={{0,15},{1,2},{2,1},{3,4},{4,3},{5,6},{6,5},{7,8},{8,7},{9,10},{10,... | collective-permute-start | bytes 147464 | tf_op jit(solution)/shard_map/ppermute | solution.py:738
  6.7 7.5 %collective-permute-start.1 = (f32[96,128]{1,0:T(8,128)S(1)}, f32[96,128]{1,0:T(8,128)S(1)}, u32[]{:S(2)}, u32[]{:S(2)}) collective-permute-start(f32[96,128]{1,0:T(8,128)S(1)} %get-tuple-element.36), channel_id=1, source_target_pairs={{0,1},{1,0},{2,3},{3,2},{4,5},{5,4},{6,7},{7,6},{8,9},{9,8},{10,11... | collective-permute-start | bytes 147464 | tf_op jit(solution)/shard_map/ppermute | solution.py:737
  10.4 4.8 %copy-start = (f32[50]{0:T(128)S(1)}, f32[50]{0:T(128)}, u32[]{:S(2)}) copy-start(f32[50]{0:T(128)} %thickness.3) | copy-start | bytes 604
  14.5 4.6 %collective-permute-start.2 = (f32[200,128]{1,0:T(8,128)S(1)}, f32[200,128]{1,0:T(8,128)S(1)}, u32[]{:S(2)}, u32[]{:S(2)}) collective-permute-start(f32[200,128]{1,0:T(8,128)S(1)} %get-tuple-element.51), channel_id=1, source_target_pairs={{0,16},{1,17},{2,18},{3,19},{4,20},{5,21},{6,22},{7,23},{8,24},{9,... | collective-permute-start | bytes 307208 | tf_op jit(solution)/shard_map/ppermute | solution.py:763
  15.0 4.2 %collective-permute-start.3 = (f32[200,128]{1,0:T(8,128)S(1)}, f32[200,128]{1,0:T(8,128)S(1)}, u32[]{:S(2)}, u32[]{:S(2)}) collective-permute-start(f32[200,128]{1,0:T(8,128)S(1)} %get-tuple-element.52), channel_id=1, source_target_pairs={{0,1},{1,0},{2,3},{3,2},{4,5},{5,4},{6,7},{7,6},{8,9},{9,8},{10,11... | collective-permute-start | bytes 307208 | tf_op jit(solution)/shard_map/ppermute | solution.py:762

commit v7 on v6

--- a/solution.py
+++ b/solution.py
@@ -582,13 +582,15 @@
 
     def slopes(first, second):
         along = to_east(first, second)
-        across = turn(first, -1, 0)
+        work[: rows + 2 * PAD] = first
+        across = work[1 : rows + 2 * PAD + 1]
         along_end = jnp.where(fold, to_west(first[end], second[end]), along[end])
-        across_end = jnp.where(fold, turn(first, 1, 0)[end], across[end])
+        across_end = jnp.where(fold, work[core_end - 1 : core_end + PAD - 1], across[end])
         along = jnp.concatenate([along[:core_end], along_end], axis=0)
         across = jnp.concatenate([across[:core_end], across_end], axis=0)
         return along - first, across - first
 
+    work[rows + 2 * PAD :] = jnp.zeros((PAD, lanes), jnp.float32)
     inner_x, inner_y = slopes(inner, outer)
     outer_x, outer_y = slopes(outer, inner)
     core = slice(PAD, core_end)
@@ -596,7 +598,7 @@
     planes[0] = inner_x[core] - spin * inner_y[core]
     planes[1] = inner_y[core] + spin * inner_x[core]
     for start, first, second in ((2, inner_x, outer_x), (6, inner_y, outer_y)):
-        work[...] = first
+        work[: rows + 2 * PAD] = first
         own = first[core]
         sides = (
             to_east(own, second[core]), to_west(own, second[core]),
@@ -804,7 +806,7 @@
         out_specs=[in_hbm] * 3 + [in_vmem],
         out_shape=[floats(*field)] * 3 + [jax.ShapeDtypeStruct(plane, jnp.float32)],
         scratch_shapes=[
-            scratch(10, *plane), scratch(4, *plane), scratch(rows + 2 * PAD, lanes), scratch(*field), scratch(*field),
+            scratch(10, *plane), scratch(4, *plane), scratch(rows + 3 * PAD, lanes), scratch(*field), scratch(*field),
             pltpu.SemaphoreType.DMA((2, OUT_PARTS)), pltpu.SemaphoreType.DMA,
         ],
         compiler_params=params,

time: 45.2 us -> 45.2 us (level)
  no operation moved by 1% of the time
where the time goes in v7:
time: 45.2 us; the launch traced here: 45.1 us
  blocking collectives  21.2 us (47%)
  Pallas kernels  15.3 us (34%)
  starting transfers between devices  7.19 us (16%)
  waiting for transfers between devices  0.78 us (2%)
  between operations  0.68 us (2%)
    all_to_all x1, blocking collectives, local(): totals = lax.all_to_all(gram, BOTH, 0, 0, tiled=True)  21.2 us
    pallas_call x1, Pallas kernels, local(): pl.pallas_call(final_kernel, in_specs=[scalars] + [in_vmem] * 9, out_spec...  3.88 us
    ppermute x1, starting transfers between devices, local(): got_1 = lax.ppermute(message_1, 'lon', lon_swaps(lons, 0))  3.73 us
    pallas_call x1, Pallas kernels, local(): pl.pallas_call(inner_kernel, in_specs=[in_vmem] * 4, out_specs=[in_vmem]...  3.7 us
    pallas_call x1, Pallas kernels, local(): pl.pallas_call(pack_kernel, in_specs=[in_hbm] * 8, out_specs=[in_vmem] *...  3.28 us
    pallas_call x1, Pallas kernels, local(): pl.pallas_call(rim_kernel, in_specs=[scalars] + [in_vmem] * 9, out_specs=...  3.12 us
    ppermute x1, starting transfers between devices, local(): got_0 = lax.ppermute(message_0, 'lon', lon_swaps(lons, 1))  2.77 us
  transfers between devices with their start and end apart: 4, of which 1 were waited for; matrix products, arithmetic and copies ran while one was open for 0% of the time, Pallas kernels for 15%

profile of v7, /device:TPU:1, one launch (start us, length us, event | category | flops | bytes accessed | tf_op | source)
XLA Modules:
  0.0 45.1 jit_solution(16651786920273326965)
XLA Ops:
  0.6 3.3 %pack.1 = (f32[96,128]{1,0:T(8,128)S(1)}, f32[96,128]{1,0:T(8,128)S(1)}, f32[5,64,128]{2,1,0:T(8,128)S(1)}, f32[6,64,128]{2,1,0:T(8,128)S(1)}, f32[3,64,128]{2,1...) custom-call(f32[50,64,128]{2,1,0:T(8,128)} %east_in.1, ...), custom_call_target="tpu_custom_call" | custom-call | tf_op jit(solution)/shard_map/pack/pallas_call | solution.py:715
  3.9 2.8 %collective-permute-start = (f32[96,128]{1,0:T(8,128)S(1)}, f32[96,128]{1,0:T(8,128)S(1)}, u32[]{:S(2)}, u32[]{:S(2)}) collective-permute-start(f32[96,128]{1,0:T(8,128)S(1)} %get-tuple-element.35), channel_id=1, source_target_pairs={{0,15},{1,2},{2,1},{3,4},{4,3},{5,6},{6,5},{7,8},{8,7},{9,10},{10,... | collective-permute-start | bytes 147464 | tf_op jit(solution)/shard_map/ppermute | solution.py:740
  6.7 3.7 %collective-permute-start.1 = (f32[96,128]{1,0:T(8,128)S(1)}, f32[96,128]{1,0:T(8,128)S(1)}, u32[]{:S(2)}, u32[]{:S(2)}) collective-permute-start(f32[96,128]{1,0:T(8,128)S(1)} %get-tuple-element.36), channel_id=1, source_target_pairs={{0,1},{1,0},{2,3},{3,2},{4,5},{5,4},{6,7},{7,6},{8,9},{9,8},{10,11... | collective-permute-start | bytes 147464 | tf_op jit(solution)/shard_map/ppermute | solution.py:739
  10.4 0.0 copy-start
  10.4 3.7 %inner.1 = (f32[50,64,128]{2,1,0:T(8,128)S(1)}, f32[50,64,128]{2,1,0:T(8,128)S(1)}, f32[50,64,128]{2,1,0:T(8,128)S(1)}) custom-call(f32[5,64,128]{2,1,0:T(8,128)S(1)} %get-tuple-element.37.planes.planes_in, f32[50,64,128]{2,1,0:T(8,128)S(1)} %get-tuple-element.40.east, f32[50,64,128]{2,1,0:T(8,128)S(1)} %get-tuple-element.41.north, ...), custom_call_target="tpu_custom_call" | custom-call | flops 24576000 | bytes 3276800 | tf_op jit(solution)/shard_map/inner/pallas_call | solution.py:742
  14.1 0.0 collective-permute-done.got_0
  14.1 0.0 collective-permute-done.1.got_1
  14.2 0.4 stitch.1
  14.5 0.4 collective-permute-start.2
  15.0 0.3 collective-permute-start.3
  15.2 0.0 copy-done
  15.2 3.1 %rim.1 = (f32[50,64,128]{2,1,0:T(8,128)S(1)}, f32[50,64,128]{2,1,0:T(8,128)S(1)}, f32[50,64,128]{2,1,0:T(8,128)S(1)}, f32[5,64,128]{2,1,0:T(8,128)S(1)}, f32[4,6...) custom-call(f32[50]{0:T(128)S(1)} %copy-done, ...), custom_call_target="tpu_custom_call", output_to_operand_aliasing={{0}: (7, {}), {1}: (8, {}), {2}: (9, {})} | custom-call | flops 4096000 | bytes 3276800 | tf_op jit(solution)/shard_map/rim/pallas_call | solution.py:767
  18.4 0.8 %collective-permute-done.2.got_a = f32[200,128]{1,0:T(8,128)S(1)} collective-permute-done((f32[200,128]{1,0:T(8,128)S(1)}, f32[200,128]{1,0:T(8,128)S(1)}, u32[]{:S(2)}, u32[]{:S(2)}) %collective-permute-start.2) | collective-permute-done | bytes 102432 | tf_op jit(solution)/shard_map/ppermute | solution.py:765
  19.1 0.0 collective-permute-done.3.got_b
  19.1 0.9 %basis.1 = (f32[128,128]{1,0:T(8,128)S(1)}, f32[4,80,256]{2,1,0:T(8,128)S(1)}, f32[6,56,128]{2,1,0:T(8,128)S(1)}, f32[50,64,128]{2,1,0:T(8,128)S(1)}, f32[5,64,1...) custom-call(f32[8,128]{1,0:T(8,128)S(1)} %get-tuple-element.50.depths, ...), custom_call_target="tpu_custom_call", output_to_operand_aliasing={{3}: (5, {}), {4}: (6, {}), {5}: (7, {})} | custom-call | tf_op jit(solution)/shard_map/basis/pallas_call | solution.py:784
  20.0 21.2 %all_to_all.11 = f32[128,1,128]{2,1,0:T(1,128)S(1)} all-to-all(f32[128,1,128]{2,1,0:T(1,128)S(1)} %bitcast.5), channel_id=1, replica_groups=mesh['lat'=8,'lon'=16] {'lat','lon'}, dimensions={0} | all-to-all | bytes 131072 | tf_op jit(solution)/shard_map/all_to_all | solution.py:801
  41.2 3.9 %final.1 = (f32[50,64,128]{2,1,0:T(8,128)}, f32[50,64,128]{2,1,0:T(8,128)}, f32[50,64,128]{2,1,0:T(8,128)}, f32[64,128]{1,0:T(8,128)}) custom-call(f32[50]{0:T(128)S(1)} %copy-done, f32[128,128]{1,0:T(8,128)S(1)} %bitcast.4, f32[4,80,256]{2,1,0:T(8,128)S(1)} %get-tuple-element.59.basis, f32[5,64,128]{2,1,0:T(8,128)S(1)} %get-tuple-element.37.planes.planes_in, ...), custom_call_target="tpu_custom_call" | custom-call | tf_op jit(solution)/shard_map/final/pallas_call | solution.py:803
Async XLA Ops:
  3.9 10.2 %collective-permute-start = (f32[96,128]{1,0:T(8,128)S(1)}, f32[96,128]{1,0:T(8,128)S(1)}, u32[]{:S(2)}, u32[]{:S(2)}) collective-permute-start(f32[96,128]{1,0:T(8,128)S(1)} %get-tuple-element.35), channel_id=1, source_target_pairs={{0,15},{1,2},{2,1},{3,4},{4,3},{5,6},{6,5},{7,8},{8,7},{9,10},{10,... | collective-permute-start | bytes 147464 | tf_op jit(solution)/shard_map/ppermute | solution.py:740
  6.7 7.5 %collective-permute-start.1 = (f32[96,128]{1,0:T(8,128)S(1)}, f32[96,128]{1,0:T(8,128)S(1)}, u32[]{:S(2)}, u32[]{:S(2)}) collective-permute-start(f32[96,128]{1,0:T(8,128)S(1)} %get-tuple-element.36), channel_id=1, source_target_pairs={{0,1},{1,0},{2,3},{3,2},{4,5},{5,4},{6,7},{7,6},{8,9},{9,8},{10,11... | collective-permute-start | bytes 147464 | tf_op jit(solution)/shard_map/ppermute | solution.py:739
  10.4 4.8 %copy-start = (f32[50]{0:T(128)S(1)}, f32[50]{0:T(128)}, u32[]{:S(2)}) copy-start(f32[50]{0:T(128)} %thickness.3) | copy-start | bytes 604
  14.5 4.6 %collective-permute-start.2 = (f32[200,128]{1,0:T(8,128)S(1)}, f32[200,128]{1,0:T(8,128)S(1)}, u32[]{:S(2)}, u32[]{:S(2)}) collective-permute-start(f32[200,128]{1,0:T(8,128)S(1)} %get-tuple-element.51), channel_id=1, source_target_pairs={{0,16},{1,17},{2,18},{3,19},{4,20},{5,21},{6,22},{7,23},{8,24},{9,... | collective-permute-start | bytes 307208 | tf_op jit(solution)/shard_map/ppermute | solution.py:765
  15.0 4.2 %collective-permute-start.3 = (f32[200,128]{1,0:T(8,128)S(1)}, f32[200,128]{1,0:T(8,128)S(1)}, u32[]{:S(2)}, u32[]{:S(2)}) collective-permute-start(f32[200,128]{1,0:T(8,128)S(1)} %get-tuple-element.52), channel_id=1, source_target_pairs={{0,1},{1,0},{2,3},{3,2},{4,5},{5,4},{6,7},{7,6},{8,9},{9,8},{10,11... | collective-permute-start | bytes 307208 | tf_op jit(solution)/shard_map/ppermute | solution.py:764
